TPU v7x, 32 devices: a whole 2x2x4 slice. The times are simulated.
32 devices in a mesh: grp: 4 (over x, core), row: 8 (over z, y).
Axes of the slice: x: 2, y: 2, z: 4, core: 2. Of those that a mesh axis runs over, the one named last changes fastest.
Arguments:
- surface: float32 [16384, 256], P(('grp', 'row')), may hold values from -6 to 6
- panel_lower: bfloat16 [16384, 1024], P(('grp', 'row')), may hold values from -0.1875 to 0.1875
- top_rows: bfloat16 [1024, 256], P('row'), may hold values from -6 to 6
- panel_inverse: bfloat16 [1024, 1024], P('row'), may hold values from -0.1875 to 0.1875
- panel_order: int32 [1024], replicated, may hold values from 0 to 1023, each once
- front_inverse: bfloat16 [4, 6144, 6144], P('grp', 'row'), may hold values from -0.078125 to 0.078125
- front_upper: bfloat16 [4, 6144, 256], P('grp', 'row'), may hold values from -6 to 6
- front_lower: bfloat16 [4, 1024, 6144], P('grp', None, 'row'), may hold values from -0.078125 to 0.078125
- front_sizes: int32 [4], replicated, may hold values from 1536 to 6144, as said below
- border_blocks: int32 [4, 8], replicated, may hold values from 0 to 127
Outputs:
- updated: float32 [16384, 256], P(('grp', 'row'))
Inputs may be any that keep to these rules, and one draw needn't show every extreme that they name: `front_sizes`: every front has at least 1536 live pivots, and in every draw some front has exactly 6144.
All inputs are finite; a program needn't handle non-finite values.
Results may differ from a plain program's by a relative error of at most 0.0022.
Values may be sent and summed in bfloat16 or wider, within the bound.
No kernel may reach another device: no remote copies, remote signals or barrier semaphores. Data moves between devices by JAX's collectives and lax.ppermute only.
A program may use at most 64 MiB of HBM per device.

v0:
```python
import jax
import jax.numpy as jnp
from jax import lax
from jax.sharding import PartitionSpec as P

BLOCK = 128


def per_device(
    surface,
    panel_lower,
    top_rows,
    panel_inverse,
    panel_order,
    front_inverse,
    front_upper,
    front_lower,
    front_sizes,
    border_blocks,
):
    row_count = lax.axis_size("row")
    grp_index = lax.axis_index("grp")
    row_index = lax.axis_index("row")
    inverse_rows = front_inverse[0]
    upper_local = front_upper[0]
    lower_local = front_lower[0]
    local_piv = upper_local.shape[0]
    col_count = upper_local.shape[1]
    live_count = front_sizes[grp_index]
    pivot_ids = row_index * local_piv + jnp.arange(local_piv, dtype=jnp.int32)
    live_mask = pivot_ids < live_count
    upper_kept = jnp.where(live_mask[:, None], upper_local, jnp.zeros_like(upper_local))
    lower_kept = jnp.where(live_mask[None, :], lower_local, jnp.zeros_like(lower_local))
    solved = jnp.dot(
        inverse_rows,
        lax.all_gather(upper_kept, "row", axis=0, tiled=True),
        preferred_element_type=jnp.float32,
    ).astype(jnp.bfloat16)
    local_blocks = surface.shape[0] // BLOCK
    block_ids = jnp.arange(local_blocks, dtype=jnp.int32)
    own_share = lax.psum_scatter(
        jnp.dot(lower_kept, solved, preferred_element_type=jnp.float32),
        "row",
        scatter_dimension=0,
        tiled=True,
    )
    contributions = lax.all_gather(own_share, ("grp", "row"), axis=0, tiled=True)
    device_id = grp_index * row_count + row_index
    own_ids = device_id * local_blocks + block_ids
    targets = border_blocks.reshape(-1)
    selector = (own_ids[:, None] == targets[None, :]).astype(jnp.float32)
    slabs = contributions.reshape(targets.shape[0], BLOCK * col_count)
    collected = jnp.dot(
        selector, slabs, precision=lax.Precision.HIGHEST, preferred_element_type=jnp.float32
    ).reshape(surface.shape)
    local_panel = panel_inverse.shape[0]
    panel_width = panel_inverse.shape[1]
    panel_ids = jnp.arange(panel_width, dtype=jnp.int32)
    top_all = lax.all_gather(top_rows, "row", axis=0, tiled=True)
    ordered = jnp.take(top_all, panel_order, axis=0)
    own_rows = row_index * local_panel + jnp.arange(local_panel, dtype=jnp.int32)
    strict = jnp.where(
        panel_ids[None, :] < own_rows[:, None], panel_inverse, jnp.zeros_like(panel_inverse)
    )
    own_top = lax.dynamic_slice_in_dim(ordered, row_index * local_panel, local_panel, 0)
    own_solved = (
        jnp.dot(strict, ordered, preferred_element_type=jnp.float32) + own_top.astype(jnp.float32)
    ).astype(jnp.bfloat16)
    factor = lax.all_gather(own_solved, "row", axis=0, tiled=True)
    return surface - collected - jnp.dot(panel_lower, factor, preferred_element_type=jnp.float32)


def solution(mesh):
    in_specs = (
        P(("grp", "row"), None),
        P(("grp", "row"), None),
        P("row", None),
        P("row", None),
        P(),
        P("grp", "row", None),
        P("grp", "row", None),
        P("grp", None, "row"),
        P(),
        P(),
    )
    out_specs = P(("grp", "row"), None)
    return jax.shard_map(
        per_device, mesh=mesh, in_specs=in_specs, out_specs=out_specs, check_vma=False
    )
```

profile of v0, /device:TPU:0, one launch (start us, length us, event | category | flops | bytes accessed | tf_op | source)
XLA Modules:
  0.0 231.0 jit_solution(6115857849547590854)
XLA Ops:
  6.5 1.3 dynamic_slice.6
  7.9 0.7 add_compare_fusion
  8.5 1.9 bitcast_select_fusion.2
  10.4 0.0 all-gather.3.cloned.1.call-update
  10.5 0.0 reduce-scatter.2.cloned.1.call-start
  10.6 63.2 %all-gather.3.cloned.1.call-done = bf16[6144,256]{1,0:T(8,128)(2,1)} async-done(((bf16[768,256]{1,0:T(8,128)(2,1)}), bf16[6144,256]{1,0:T(8,128)(2,1)}) %all-gather.3.cloned.1.call-update) | async-done | bytes 3145744 | tf_op jit(solution)/shard_map/all_gather | solution.py:36
  73.8 9.5 %fusion.2 = f32[1024,256]{1,0:T(8,128)} fusion(bf16[1,1024,768]{2,1,0:T(8,128)(2,1)} %param.17, pred[768]{0:T(1024)(128)(4,1)S(1)} %add_compare_fusion, bf16[6144,256]{1,0:T(8,128)(2,1)} %all-gather.3.cloned.1.call-done, bf16[1,768,6144]{2,1,0:T(8,128)(2,1)} %param.15), kind=kOutput, calls=%fused_computation.4 | convolution fusion | flops 2819555328 | bytes 15205120 | tf_op jit(solution)/shard_map/dot_general | solution.py:42
  83.3 0.0 reduce-scatter.2.cloned.1.call-update
  83.3 0.0 all-gather.5.cloned.1.call-start
  83.4 62.2 %reduce-scatter.2.cloned.1.call-done = f32[128,256]{1,0:T(8,128)} async-done(((f32[1024,256]{1,0:T(8,128)}), f32[128,256]{1,0:T(8,128)}) %reduce-scatter.2.cloned.1.call-update) | async-done | bytes 131088 | tf_op jit(solution)/shard_map/reduce_scatter | solution.py:41
  145.5 0.0 all-gather.5.cloned.1.call-update
  145.6 0.1 eq.16
  145.7 0.2 copy.11
  145.9 31.8 %all_gather.14 = bf16[1024,256]{1,0:T(8,128)(2,1)S(1)} all-gather(bf16[128,256]{1,0:T(8,128)(2,1)S(1)} %copy-done.2), channel_id=1, replica_groups=mesh['grp'=4,'row'=8] {'row'}, dimensions={0}, use_global_device_ids=true | all-gather | bytes 589824 | tf_op jit(solution)/shard_map/all_gather | solution.py:59
  177.7 3.9 %gather_fusion = bf16[1024,256]{1,0:T(8,128)(2,1)S(1)} fusion(bf16[1024,256]{1,0:T(8,128)(2,1)S(1)} %all_gather.14, s32[1024]{0:T(1024)S(1)} %fusion.14), kind=kCustom, calls=%fused_computation | custom fusion | bytes 1052672 | tf_op jit(solution)/shard_map/jit(_take)/gather | solution.py:60
  181.7 0.2 broadcast_select_fusion
  181.9 0.3 fusion.8
  182.2 31.5 %all_gather.15 = bf16[1024,256]{1,0:T(8,128)(2,1)S(1)} all-gather(bf16[128,256]{1,0:T(8,128)(2,1)S(1)} %fusion.8), channel_id=1, replica_groups=mesh['grp'=4,'row'=8] {'row'}, dimensions={0}, use_global_device_ids=true | all-gather | bytes 589824 | tf_op jit(solution)/shard_map/all_gather | solution.py:69
  213.8 5.0 %reshape.30 = f32[32,32768]{1,0:T(8,128)} reshape(f32[4096,256]{1,0:T(8,128)} %all-gather.5.cloned.1.call-done) | data formatting | bytes 8388608 | tf_op jit(solution)/shard_map/reshape | solution.py:52
  218.7 3.6 %fusion.15 = f32[4,32768]{1,0:T(4,128)S(1)} fusion(f32[32,32768]{1,0:T(8,128)} %reshape.30, s32[32]{0:T(128)S(1)} %eq.16, s32[4]{0:T(128)S(1)} %iota_add_fusion.1), kind=kOutput, calls=%fused_computation.22 | convolution fusion | flops 50331776 | bytes 4718736 | tf_op jit(solution)/shard_map/dot_general | solution.py:53
  222.4 0.4 reshape.31
  222.7 0.2 copy.12
  222.9 0.5 fusion.7
  223.4 1.0 copy.13
  (18 shorter events, 0.1 us)
Async XLA Ops:
  6.5 216.4 %copy-start = (bf16[512,1024]{1,0:T(8,128)(2,1)S(1)}, bf16[512,1024]{1,0:T(8,128)(2,1)}, u32[]{:S(2)}) copy-start(bf16[512,1024]{1,0:T(8,128)(2,1)} %param.11) | copy-start | bytes 3145732
  6.5 67.2 %all-gather.3.cloned.1.call-start = ((), (), s32[]{:S(2)}) async-start(), calls=%async_computation.1 | async-start | bytes 3538944 | tf_op jit(solution)/shard_map/all_gather | solution.py:36
  10.5 135.1 %copy-start.4 = (s32[4,8]{1,0:T(4,128)S(1)}, s32[4,8]{1,0:T(4,128)}, u32[]{:S(2)}) copy-start(s32[4,8]{1,0:T(4,128)} %param.19) | copy-start | bytes 388
  10.5 135.2 %copy-start.1 = (f32[512,256]{1,0:T(8,128)S(1)}, f32[512,256]{1,0:T(8,128)}, u32[]{:S(2)}) copy-start(f32[512,256]{1,0:T(8,128)} %param.10) | copy-start | bytes 1572868
  10.5 135.4 %copy-start.3 = (s32[1024]{0:T(1024)S(1)}, s32[1024]{0:T(1024)}, u32[]{:S(2)}) copy-start(s32[1024]{0:T(1024)} %param.14) | copy-start | bytes 12292
  10.5 135.4 %copy-start.2 = (bf16[128,256]{1,0:T(8,128)(2,1)S(1)}, bf16[128,256]{1,0:T(8,128)(2,1)}, u32[]{:S(2)}) copy-start(bf16[128,256]{1,0:T(8,128)(2,1)} %param.12) | copy-start | bytes 196612
  10.5 135.0 %reduce-scatter.2.cloned.1.call-start = ((), (), s32[]{:S(2)}) async-start(), calls=%async_computation.2 | async-start | bytes 1179648 | tf_op jit(solution)/shard_map/reduce_scatter | solution.py:41
  83.3 130.4 %all-gather.5.cloned.1.call-start = ((), (), s32[]{:S(2)}) async-start(), calls=%async_computation.3 | async-start | bytes 4325376 | tf_op jit(solution)/shard_map/all_gather | solution.py:47
  145.9 36.0 %copy-start.5 = (bf16[128,1024]{1,0:T(8,128)(2,1)S(1)}, bf16[128,1024]{1,0:T(8,128)(2,1)}, u32[]{:S(2)}) copy-start(bf16[128,1024]{1,0:T(8,128)(2,1)} %param.13) | copy-start | bytes 786436
Sparse Core Ops, SparseCore 0:
  10.6 63.1 all-gather.2
  83.4 62.0 reduce-scatter.1
  149.1 63.9 all-gather.4
where the time goes:
time: 231 us
  waiting for transfers between devices  125 us (54%)
  blocking collectives  63.4 us (27%)
  matrix products  13.9 us (6%)
  between operations  13.3 us (6%)
  local copies, waits for them, and re-layouts  12.1 us (5%)
  other arithmetic  2.79 us (1%)
    all_gather x1, waiting for transfers between devices, per_device(): lax.all_gather(upper_kept, 'row', axis=0, tiled=True)  63.2 us
    reduce_scatter x1, waiting for transfers between devices, per_device(): lax.psum_scatter(jnp.dot(lower_kept, solved, preferred_element_type=jnp.f...  62.2 us
    all_gather x1, blocking collectives, per_device(): top_all = lax.all_gather(top_rows, 'row', axis=0, tiled=True)  31.8 us
    all_gather x1, blocking collectives, per_device(): factor = lax.all_gather(own_solved, 'row', axis=0, tiled=True)  31.5 us
    dot_general x1, matrix products, per_device(): jnp.dot(lower_kept, solved, preferred_element_type=jnp.float32)  9.53 us
    reshape x1, local copies, waits for them, and re-layouts, per_device(): slabs = contributions.reshape(targets.shape[0], BLOCK * col_count)  4.97 us
  transfers between devices with their start and end apart: 3, of which 2 were waited for; matrix products, arithmetic and copies ran while one was open for 2% of the time, Pallas kernels for 0%

commit v1 on v0

v1 whole, which is shorter than its diff:
```python
import functools

import jax
import jax.numpy as jnp
from jax import lax
from jax.experimental import pallas as pl
from jax.experimental.pallas import tpu as pltpu
from jax.sharding import PartitionSpec as P

BLOCK = 128
HALVES = 2
NEXT = (1, 3, 0, 2)
PREV = (2, 0, 3, 1)
LIMIT = 40 << 20
F32 = jnp.float32
BF16 = jnp.bfloat16
together = lax.optimization_barrier


def params():
    return pltpu.CompilerParams(vmem_limit_bytes=LIMIT)


def whole(shape):
    return pl.BlockSpec(shape, lambda *_: (0,) * len(shape))


def row_permute(value, target):
    pairs = [(z * 2 + y, target(z, y)) for z in range(4) for y in range(2)]
    return lax.ppermute(value, "row", [(s, t[0] * 2 + t[1]) for s, t in pairs])


def cycle(value):
    return row_permute(value, lambda z, y: (NEXT[z], y))


def across(value):
    return row_permute(value, lambda z, y: (z, 1 - y))


def along(value, step):
    return row_permute(value, lambda z, y: (z ^ step, y))


def group_swap(value, step):
    return lax.ppermute(value, "grp", [(g, g ^ step) for g in range(4)])


def multiply_body(count, has_total, blocks_ref, inverse_ref, *refs):
    pieces = refs[:count]
    total_ref = refs[-1]
    step = pl.program_id(0)
    for k in range(count):

        @pl.when(step == k)
        def _():
            part = jnp.dot(inverse_ref[...], pieces[k][...], preferred_element_type=F32)
            if k > 0:
                total_ref[...] += part
            elif has_total:
                total_ref[...] = refs[count][...] + part
            else:
                total_ref[...] = part


def multiply(inverse, blocks, pieces, total=None):
    rows = inverse.shape[0]
    depth, cols = pieces[0].shape
    count = len(pieces)
    extra = [] if total is None else [total]
    return pl.pallas_call(
        functools.partial(multiply_body, count, bool(extra)),
        out_shape=jax.ShapeDtypeStruct((rows, cols), F32),
        grid_spec=pltpu.PrefetchScalarGridSpec(
            num_scalar_prefetch=1,
            grid=(count,),
            in_specs=[pl.BlockSpec((rows, depth), lambda i, b: (0, b[i]))]
            + [whole((depth, cols))] * count
            + [whole((rows, cols))] * len(extra),
            out_specs=whole((rows, cols)),
        ),
        compiler_params=params(),
        cost_estimate=pl.CostEstimate(
            flops=2 * rows * depth * cols * count,
            bytes_accessed=2 * rows * depth * count,
            transcendentals=0,
        ),
    )(blocks, inverse, *pieces, *extra)


def contribute_body(count, scalars_ref, inverse_ref, *refs):
    pieces = refs[:count]
    before_ref, lower_ref, keep_ref, send_ref, total_ref, product_ref = refs[count:]
    step = pl.program_id(0)
    for k in range(count):

        @pl.when(step == k)
        def _():
            part = jnp.dot(inverse_ref[...], pieces[k][...], preferred_element_type=F32)
            total_ref[...] = (before_ref if k == 0 else total_ref)[...] + part

    @pl.when(step == count - 1)
    def _():
        live, own_y = scalars_ref[count], scalars_ref[count + 1]
        pivots = lax.broadcasted_iota(jnp.int32, total_ref.shape, 0)
        solved = jnp.where(pivots < live, total_ref[...], 0.0).astype(BF16)
        product_ref[...] = jnp.dot(lower_ref[...], solved, preferred_element_type=F32)
        slots, slabs, height, _ = keep_ref.shape
        for z in range(slots):
            for j in range(slabs):
                base = j * BLOCK + z * 2 * height
                mine = pl.multiple_of(base + own_y * height, height)
                other = pl.multiple_of(base + (1 - own_y) * height, height)
                keep_ref[z, j] = product_ref[pl.ds(mine, height)]
                send_ref[z, j] = product_ref[pl.ds(other, height)].astype(BF16)


def contribute(inverse, scalars, pieces, before, lower):
    rows = inverse.shape[0]
    depth, cols = pieces[0].shape
    border = lower.shape[0]
    count = len(pieces)
    slots = (4, border // BLOCK, BLOCK // 8, cols)
    return pl.pallas_call(
        functools.partial(contribute_body, count),
        out_shape=[jax.ShapeDtypeStruct(slots, F32), jax.ShapeDtypeStruct(slots, BF16)],
        grid_spec=pltpu.PrefetchScalarGridSpec(
            num_scalar_prefetch=1,
            grid=(count,),
            in_specs=[pl.BlockSpec((rows, depth), lambda i, b: (0, b[i]))]
            + [whole((depth, cols))] * count
            + [whole((rows, cols)), whole((border, rows))],
            out_specs=[whole(slots), whole(slots)],
            scratch_shapes=[pltpu.VMEM((rows, cols), F32), pltpu.VMEM((border, cols), F32)],
        ),
        compiler_params=params(),
        cost_estimate=pl.CostEstimate(
            flops=2 * rows * cols * (depth * count + border),
            bytes_accessed=2 * rows * (depth * count + border),
            transcendentals=0,
        ),
    )(scalars, inverse, *pieces, before, lower)


def split_body(z_ref, keep_ref, come_ref, own_ref, *send_refs):
    z = z_ref[0]
    own_ref[...] = keep_ref[z] + come_ref[z].astype(F32)
    for k, ref in enumerate(send_refs, 1):
        ref[...] = (keep_ref[z ^ k] + come_ref[z ^ k].astype(F32)).astype(BF16)


def split(z, keep, come):
    shape = keep.shape[1:]
    return pl.pallas_call(
        split_body,
        out_shape=[jax.ShapeDtypeStruct(shape, F32)] + [jax.ShapeDtypeStruct(shape, BF16)] * 3,
        in_specs=[pl.BlockSpec(memory_space=pltpu.SMEM)]
        + [pl.BlockSpec(memory_space=pltpu.VMEM)] * 2,
        out_specs=[pl.BlockSpec(memory_space=pltpu.VMEM)] * 4,
        compiler_params=params(),
    )(z[None], keep, come)


def place_body(targets_ref, first_ref, *refs):
    pieces, slots_ref, total_ref = refs[:4], refs[4], refs[5]
    total_ref[...] = jnp.zeros_like(total_ref)
    blocks = total_ref.shape[0]
    slabs = pieces[0].shape[0]
    first, group = first_ref[0], first_ref[1]
    for k, piece in enumerate(pieces):
        for j in range(slabs):
            place = targets_ref[group ^ k, j] - first

            @pl.when((place >= 0) & (place < blocks))
            def _():
                total_ref[place] += piece[j].astype(F32)

    slots_ref[...] = total_ref[...].astype(BF16)


def place(targets, first, pieces, blocks):
    shape = (blocks,) + pieces[0].shape[1:]
    return pl.pallas_call(
        place_body,
        out_shape=jax.ShapeDtypeStruct(shape, BF16),
        in_specs=[pl.BlockSpec(memory_space=pltpu.SMEM)] * 2
        + [pl.BlockSpec(memory_space=pltpu.VMEM)] * 4,
        out_specs=pl.BlockSpec(memory_space=pltpu.VMEM),
        scratch_shapes=[pltpu.VMEM(shape, F32)],
        compiler_params=params(),
    )(targets, first, *pieces)


def factor_body(place_ref, order_ref, inverse_ref, mine_ref, other_ref, out_ref):
    row, core = place_ref[0], place_ref[1]
    local, width = inverse_ref.shape
    half = local // 2
    rows = row * local + lax.broadcasted_iota(jnp.int32, (local, width), 0)
    cols = lax.broadcasted_iota(jnp.int32, (local, width), 1)
    lower = jnp.where(cols < rows, inverse_ref[...].astype(F32), jnp.where(cols == rows, 1.0, 0.0))
    lower = lower.astype(BF16)
    total = jnp.zeros((local, out_ref.shape[1]), F32)
    for ref, side in ((mine_ref, core), (other_ref, 1 - core)):
        for k in range(width // local):
            first = (row ^ k) * local + side * half
            ids = first + lax.broadcasted_iota(jnp.int32, (half, width), 0)
            pick = (ids == order_ref[...]).astype(F32).astype(BF16)
            moved = lax.dot_general(
                lower, pick, (((1,), (1,)), ((), ())), preferred_element_type=F32
            ).astype(BF16)
            total += jnp.dot(moved, ref[k], preferred_element_type=F32)
    out_ref[...] = total.astype(BF16)


def panel_factor(place_scalars, order, inverse, mine, other):
    local = inverse.shape[0]
    return pl.pallas_call(
        factor_body,
        out_shape=jax.ShapeDtypeStruct((local, mine.shape[-1]), BF16),
        in_specs=[pl.BlockSpec(memory_space=pltpu.SMEM)]
        + [pl.BlockSpec(memory_space=pltpu.VMEM)] * 4,
        out_specs=pl.BlockSpec(memory_space=pltpu.VMEM),
        compiler_params=params(),
    )(place_scalars, order[None], inverse, mine, other)


def base_body(place_ref, surface_ref, lower_ref, mine_ref, other_ref, out_ref, factor_ref):
    row, core = place_ref[0], place_ref[1]
    half = mine_ref.shape[1]
    for ref, side in ((mine_ref, core), (other_ref, 1 - core)):
        for k in range(mine_ref.shape[0]):
            first = pl.multiple_of(((row ^ k) * 2 + side) * half, half)
            factor_ref[pl.ds(first, half)] = ref[k]
    product = jnp.dot(lower_ref[...], factor_ref[...], preferred_element_type=F32)
    out_ref[...] = surface_ref[...] - product


def panel_update(place_scalars, surface, lower, mine, other):
    return pl.pallas_call(
        base_body,
        out_shape=jax.ShapeDtypeStruct(surface.shape, F32),
        in_specs=[pl.BlockSpec(memory_space=pltpu.SMEM)]
        + [pl.BlockSpec(memory_space=pltpu.VMEM)] * 4,
        out_specs=pl.BlockSpec(memory_space=pltpu.VMEM),
        scratch_shapes=[pltpu.VMEM((lower.shape[1], surface.shape[1]), BF16)],
        compiler_params=params(),
    )(place_scalars, surface, lower, mine, other)


def doubled(value):
    pair = jnp.stack([value, across(value)])
    four = jnp.concatenate([pair, along(pair, 1)])
    return jnp.concatenate([four, along(four, 2)])


def staged(
    surface,
    panel_lower,
    top_rows,
    panel_inverse,
    panel_order,
    front_inverse,
    front_upper,
    front_lower,
    front_sizes,
    border_blocks,
):
    row_count = lax.axis_size("row")
    group = lax.axis_index("grp")
    row = lax.axis_index("row")
    z, y, core = row // 2, row % 2, group % 2
    inverse, upper, lower = front_inverse[0], front_upper[0], front_lower[0]
    local_piv = upper.shape[0]
    live = front_sizes[group] - row * local_piv
    kept = jnp.where(jnp.arange(local_piv, dtype=jnp.int32)[:, None] < live, upper, 0)
    depth = local_piv // HALVES
    a, b = kept[:depth], kept[depth:]
    spot = jnp.stack([row, core])

    half = top_rows.shape[0] // 2
    top_half = lax.dynamic_slice_in_dim(top_rows, core * half, half, 0)
    top_mine = doubled(top_half)
    top_other = group_swap(top_mine, 1)
    own_factor = panel_factor(spot, panel_order, panel_inverse, top_mine, top_other)
    factor_half = lax.dynamic_slice_in_dim(own_factor, core * half, half, 0)
    factor_mine = doubled(factor_half)
    factor_other = group_swap(factor_mine, 1)
    base = panel_update(spot, surface, panel_lower, factor_mine, factor_other)

    a1, ay0, b1, by0 = cycle(a), across(a), cycle(b), across(b)
    a1, ay0 = together((a1, ay0))
    a2, ay1 = cycle(a1), across(a1)
    b1, by0 = together((b1, by0))
    b2, by1 = cycle(b1), across(b1)
    a2, ay1 = together((a2, ay1))
    a3, ay2 = cycle(a2), across(a2)
    b2, by1 = together((b2, by1))
    b3, by2 = cycle(b2), across(b2)
    a3, ay2 = together((a3, ay2))
    ay3 = across(a3)
    b3, by2 = together((b3, by2))
    by3 = across(b3)

    prev = jnp.asarray(PREV, jnp.int32)
    sources = [z]
    for _ in range(3):
        sources.append(prev[sources[-1]])

    def block(k, other, h):
        return (sources[k] * 2 + (1 - y if other else y)) * HALVES + h

    early = [(0, 0, 0, a), (0, 0, 1, b), (1, 0, 0, a1), (0, 1, 0, ay0), (1, 0, 1, b1)]
    early += [(0, 1, 1, by0), (2, 0, 0, a2), (1, 1, 0, ay1), (2, 0, 1, b2), (1, 1, 1, by1)]
    late = [(3, 0, 0, a3), (2, 1, 0, ay2), (3, 0, 1, b3), (2, 1, 1, by2)]
    late += [(3, 1, 0, ay3), (3, 1, 1, by3)]
    early_blocks = jnp.stack([block(*e[:3]) for e in early])
    late_scalars = jnp.stack([block(*e[:3]) for e in late] + [live, y])
    total = multiply(inverse, early_blocks, [e[3] for e in early])
    keep, send = contribute(inverse, late_scalars, [e[3] for e in late], total, lower)

    own, s1, s2, s3 = split(z, keep, across(send))
    r3, r2, r1 = along(s3, 3), along(s2, 2), along(s1, 1)
    mine = (own + r1.astype(F32) + r2.astype(F32) + r3.astype(F32)).astype(BF16)
    pieces = [mine] + [group_swap(mine, k) for k in (1, 2, 3)]
    local_blocks = surface.shape[0] // BLOCK
    blocks = local_blocks * row_count
    slots = place(border_blocks, jnp.stack([group * blocks, group]), pieces, blocks)
    slots = slots.reshape((row_count, local_blocks) + slots.shape[1:])
    got = lax.all_to_all(slots, "row", 0, 0, tiled=True)
    collected = got.transpose(1, 0, 2, 3).reshape(surface.shape).astype(F32)
    return base - collected


def gathered(
    surface,
    panel_lower,
    top_rows,
    panel_inverse,
    panel_order,
    front_inverse,
    front_upper,
    front_lower,
    front_sizes,
    border_blocks,
):
    row_count = lax.axis_size("row")
    grp_index = lax.axis_index("grp")
    row_index = lax.axis_index("row")
    inverse_rows, upper_local, lower_local = front_inverse[0], front_upper[0], front_lower[0]
    local_piv, col_count = upper_local.shape
    pivot_ids = row_index * local_piv + jnp.arange(local_piv, dtype=jnp.int32)
    live_mask = pivot_ids < front_sizes[grp_index]
    upper_kept = jnp.where(live_mask[:, None], upper_local, jnp.zeros_like(upper_local))
    lower_kept = jnp.where(live_mask[None, :], lower_local, jnp.zeros_like(lower_local))
    upper_all = lax.all_gather(upper_kept, "row", axis=0, tiled=True)
    solved = jnp.dot(inverse_rows, upper_all, preferred_element_type=F32).astype(BF16)
    partial_sum = jnp.dot(lower_kept, solved, preferred_element_type=F32)
    own_share = lax.psum_scatter(partial_sum, "row", scatter_dimension=0, tiled=True)
    contributions = lax.all_gather(own_share, ("grp", "row"), axis=0, tiled=True)
    local_blocks = surface.shape[0] // BLOCK
    device_id = grp_index * row_count + row_index
    own_ids = device_id * local_blocks + jnp.arange(local_blocks, dtype=jnp.int32)
    targets = border_blocks.reshape(-1)
    selector = (own_ids[:, None] == targets[None, :]).astype(F32)
    slabs = contributions.reshape(targets.shape[0], BLOCK * col_count)
    collected = jnp.dot(
        selector, slabs, precision=lax.Precision.HIGHEST, preferred_element_type=F32
    ).reshape(surface.shape)
    local_panel, panel_width = panel_inverse.shape
    panel_ids = jnp.arange(panel_width, dtype=jnp.int32)
    top_all = lax.all_gather(top_rows, "row", axis=0, tiled=True)
    ordered = jnp.take(top_all, panel_order, axis=0)
    own_rows = row_index * local_panel + jnp.arange(local_panel, dtype=jnp.int32)
    strict = jnp.where(
        panel_ids[None, :] < own_rows[:, None], panel_inverse, jnp.zeros_like(panel_inverse)
    )
    own_top = lax.dynamic_slice_in_dim(ordered, row_index * local_panel, local_panel, 0)
    product = jnp.dot(strict, ordered, preferred_element_type=F32)
    own_solved = (product + own_top.astype(F32)).astype(BF16)
    factor = lax.all_gather(own_solved, "row", axis=0, tiled=True)
    return surface - collected - jnp.dot(panel_lower, factor, preferred_element_type=F32)


def solution(mesh):
    in_specs = (
        P(("grp", "row"), None),
        P(("grp", "row"), None),
        P("row", None),
        P("row", None),
        P(),
        P("grp", "row", None),
        P("grp", "row", None),
        P("grp", None, "row"),
        P(),
        P(),
    )
    out_specs = P(("grp", "row"), None)
    small = mesh.shape["row"] == 8 and mesh.shape["grp"] == 4
    return jax.shard_map(
        staged if small else gathered,
        mesh=mesh,
        in_specs=in_specs,
        out_specs=out_specs,
        check_vma=False,
    )
```

time: 231 us -> 123 us (0.53)
  waiting for transfers between devices: 125 us -> 34.8 us
  blocking collectives: 63.4 us -> 0 us
  starting transfers between devices: 0.09 us -> 36.7 us
  Pallas kernels: 0 us -> 16.7 us
  matrix products: 13.9 us -> 0 us
  local copies, waits for them, and re-layouts: 12.1 us -> 23.1 us
  between operations: 13.3 us -> 6.75 us
    all_gather x2 -> x0, blocking collectives: 63.4 us -> none  [the longest x1 31.8 us: per_device(): top_all = lax.all_gather(top_rows, 'row', axis=0, tiled=True)]
    all_gather x2 -> x0, waiting for transfers between devices: 63.2 us -> none  [the longest x1 63.2 us: per_device(): lax.all_gather(upper_kept, 'row', axis=0, tiled=True)]
    reduce_scatter x1 -> x0, waiting for transfers between devices: 62.2 us -> none  [per_device(): lax.psum_scatter(jnp.dot(lower_kept, solved, preferred_element_type=jnp.f...]
    ppermute x0 -> x29, starting transfers between devices: none -> 32.4 us  [the longest x24 30.3 us: row_permute(): return lax.ppermute(value, 'row', [(s, t[0] * 2 + t[1]) for s, t in pairs])]
    ppermute x0 -> x29, waiting for transfers between devices: none -> 30 us  [the longest x24 24.9 us: row_permute(): return lax.ppermute(value, 'row', [(s, t[0] * 2 + t[1]) for s, t in pairs])]
    unnamed x13 -> x52, local copies, waits for them, and re-layouts: 0.23 us -> 17.7 us
    pallas_call x0 -> x6, Pallas kernels: none -> 16.7 us  [the longest x1 5.53 us: multiply(): pl.pallas_call(functools.partial(multiply_body, count, bool(extra)), out_...]
    dot_general x4 -> x0, matrix products: 13.9 us -> none  [the longest x1 9.53 us: per_device(): jnp.dot(lower_kept, solved, preferred_element_type=jnp.float32)]
  transfers between devices with their start and end apart: 3 -> 30, of which waited for: 2 -> 11; matrix products, arithmetic and copies ran while one was open for 2% -> 5% of each run, Pallas kernels for 0% -> 14%
where the time goes in v1:
time: 123 us; the launch traced here: 122 us
  starting transfers between devices  36.7 us (30%)
  waiting for transfers between devices  34.8 us (28%)
  local copies, waits for them, and re-layouts  23.1 us (19%)
  Pallas kernels  16.7 us (14%)
  between operations  6.75 us (5%)
  other arithmetic  3.89 us (3%)
    ppermute x24, starting transfers between devices, row_permute(): return lax.ppermute(value, 'row', [(s, t[0] * 2 + t[1]) for s, t in pairs])  30.3 us
    ppermute x24, waiting for transfers between devices, row_permute(): return lax.ppermute(value, 'row', [(s, t[0] * 2 + t[1]) for s, t in pairs])  24.9 us
    unnamed x52, local copies, waits for them, and re-layouts  17.7 us
    pallas_call x1, Pallas kernels, multiply(): pl.pallas_call(functools.partial(multiply_body, count, bool(extra)), out_...  5.53 us
    pallas_call x1, Pallas kernels, contribute(): pl.pallas_call(functools.partial(contribute_body, count), out_shape=[jax....  5.37 us
    ppermute x5, waiting for transfers between devices, group_swap(): return lax.ppermute(value, 'grp', [(g, g ^ step) for g in range(4)])  5.17 us
    all_to_all x1, waiting for transfers between devices, staged(): got = lax.all_to_all(slots, 'row', 0, 0, tiled=True)  4.78 us
    all_to_all x1, starting transfers between devices, staged(): got = lax.all_to_all(slots, 'row', 0, 0, tiled=True)  4.37 us
  transfers between devices with their start and end apart: 30, of which 11 were waited for; matrix products, arithmetic and copies ran while one was open for 5% of the time, Pallas kernels for 14%

profile of v1, /device:TPU:0, one launch (start us, length us, event | category | flops | bytes accessed | tf_op | source)
XLA Modules:
  0.0 122.0 jit_solution(1421769746216784034)
XLA Ops:
  3.2 3.1 %collective-permute-start.14 = (bf16[384,256]{1,0:T(8,128)(2,1)S(1)}, bf16[384,256]{1,0:T(8,128)(2,1)S(1)}, u32[]{:S(2)}, u32[]{:S(2)}) collective-permute-start(bf16[384,256]{1,0:T(8,128)(2,1)S(1)} %get-tuple-element.41.refs_1_), channel_id=1, source_target_pairs={{0,2},{1,3},{2,6},{3,7},{4,0},{5,1},{6,4},{7,5},{8,10},{9,11},{10,... | collective-permute-start | bytes 589832 | tf_op jit(solution)/shard_map/ppermute | solution.py:30
  7.8 2.6 %collective-permute-start.8 = (bf16[384,256]{1,0:T(8,128)(2,1)S(1)}, bf16[384,256]{1,0:T(8,128)(2,1)S(1)}, u32[]{:S(2)}, u32[]{:S(2)}) collective-permute-start(bf16[384,256]{1,0:T(8,128)(2,1)S(1)} %get-tuple-element.42.refs_0_), channel_id=1, source_target_pairs={{0,2},{1,3},{2,6},{3,7},{4,0},{5,1},{6,4},{7,5},{8,10},{9,11},{10,... | collective-permute-start | bytes 589832 | tf_op jit(solution)/shard_map/ppermute | solution.py:30
  12.5 5.1 %collective-permute-done = bf16[64,256]{1,0:T(8,128)(2,1)S(1)} collective-permute-done((bf16[64,256]{1,0:T(8,128)(2,1)S(1)}, bf16[64,256]{1,0:T(8,128)(2,1)S(1)}, u32[]{:S(2)}, u32[]{:S(2)}) %collective-permute-start) | collective-permute-done | bytes 32800 | tf_op jit(solution)/shard_map/ppermute | solution.py:30
  17.6 2.7 %collective-permute-start.1 = (bf16[2,64,256]{2,1,0:T(8,128)(2,1)S(1)}, bf16[2,64,256]{2,1,0:T(8,128)(2,1)S(1)}, u32[]{:S(2)}, u32[]{:S(2)}) collective-permute-start(bf16[2,64,256]{2,1,0:T(8,128)(2,1)S(1)} %pad_maximum_fusion.4), channel_id=1, source_target_pairs={{0,2},{1,3},{2,0},{3,1},{4,6},{5,7},{6,4},{7,5},{8,10},{9,11},{10,... | collective-permute-start | bytes 196616 | tf_op jit(solution)/shard_map/ppermute | solution.py:30
  20.4 1.6 %collective-permute-start.17 = (bf16[384,256]{1,0:T(8,128)(2,1)S(1)}, bf16[384,256]{1,0:T(8,128)(2,1)S(1)}, u32[]{:S(2)}, u32[]{:S(2)}) collective-permute-start(bf16[384,256]{1,0:T(8,128)(2,1)S(1)} %collective-permute-done.14.refs_4_), channel_id=1, source_target_pairs={{0,1},{1,0},{2,3},{3,2},{4,5},{5,4},{6,7},{7,6},{8,9},{9,8},{10,11... | collective-permute-start | bytes 589832 | tf_op jit(solution)/shard_map/ppermute | solution.py:30
  24.5 4.1 %collective-permute-done.1 = bf16[2,64,256]{2,1,0:T(8,128)(2,1)S(1)} collective-permute-done((bf16[2,64,256]{2,1,0:T(8,128)(2,1)S(1)}, bf16[2,64,256]{2,1,0:T(8,128)(2,1)S(1)}, u32[]{:S(2)}, u32[]{:S(2)}) %collective-permute-start.1) | collective-permute-done | bytes 65568 | tf_op jit(solution)/shard_map/ppermute | solution.py:30
  30.3 2.2 %collective-permute-start.18 = (bf16[384,256]{1,0:T(8,128)(2,1)S(1)}, bf16[384,256]{1,0:T(8,128)(2,1)}, u32[]{:S(2)}, u32[]{:S(2)}) collective-permute-start(bf16[384,256]{1,0:T(8,128)(2,1)S(1)} %collective-permute-done.16.refs_8_), channel_id=1, source_target_pairs={{0,2},{1,3},{2,6},{3,7},{4,0},{5,1},{6,4},{7,5},{8,10},{9,11},{10,... | collective-permute-start | bytes 589832 | tf_op jit(solution)/shard_map/ppermute | solution.py:30
  32.5 1.5 %collective-permute-start.19 = (bf16[384,256]{1,0:T(8,128)(2,1)S(1)}, bf16[384,256]{1,0:T(8,128)(2,1)}, u32[]{:S(2)}, u32[]{:S(2)}) collective-permute-start(bf16[384,256]{1,0:T(8,128)(2,1)S(1)} %collective-permute-done.16.refs_8_), channel_id=1, source_target_pairs={{0,1},{1,0},{2,3},{3,2},{4,5},{5,4},{6,7},{7,6},{8,9},{9,8},{10,11... | collective-permute-start | bytes 589832 | tf_op jit(solution)/shard_map/ppermute | solution.py:30
  34.1 1.9 %collective-permute-done.10.refs_6_ = bf16[384,256]{1,0:T(8,128)(2,1)S(1)} collective-permute-done((bf16[384,256]{1,0:T(8,128)(2,1)S(1)}, bf16[384,256]{1,0:T(8,128)(2,1)S(1)}, u32[]{:S(2)}, u32[]{:S(2)}) %collective-permute-start.10) | collective-permute-done | bytes 196640 | tf_op jit(solution)/shard_map/ppermute | solution.py:30
  48.9 1.5 %collective-permute-start.21 = (bf16[384,256]{1,0:T(8,128)(2,1)}, bf16[384,256]{1,0:T(8,128)(2,1)S(1)}, u32[]{:S(2)}, u32[]{:S(2)}) collective-permute-start(bf16[384,256]{1,0:T(8,128)(2,1)} %collective-permute-done.18.refs_2_), channel_id=1, source_target_pairs={{0,1},{1,0},{2,3},{3,2},{4,5},{5,4},{6,7},{7,6},{8,9},{9,8},{10,11... | collective-permute-start | bytes 589832 | tf_op jit(solution)/shard_map/ppermute | solution.py:30
  51.7 3.7 %copy-done.1 = bf16[1,768,6144]{2,1,0:T(8,128)(2,1)S(1)} copy-done((bf16[1,768,6144]{2,1,0:T(8,128)(2,1)S(1)}, bf16[1,768,6144]{2,1,0:T(8,128)(2,1)}, u32[]{:S(2)}) %copy-start.1) | copy-done | bytes 9437208
  61.8 5.5 %shard_map.111.refs_6_ = f32[768,256]{1,0:T(8,128)S(1)} custom-call(s32[10]{0:T(128)S(1)} %stack.127.blocks_ref, bf16[768,6144]{1,0:T(8,128)(2,1)S(1)} %bitcast.43, bf16[384,256]{1,0:T(8,128)(2,1)S(1)} %get-tuple-element.42.refs_0_, bf16[384,256]{1,0:T(8,128)(2,1)S(1)} %get-tuple-element.41.refs_1_, bf16[384,256]{1,0:T(8,128)(2,1)S(1)} %copy-done.10, ...), custom_call_target="tpu_custom_call" | custom-call | flops 1509949440 | bytes 5898240 | tf_op jit(solution)/shard_map/pallas_call | solution.py:71
  67.4 3.1 %shard_map.109 = bf16[128,256]{1,0:T(8,128)(2,1)S(1)} custom-call(s32[2]{0:T(128)S(1)} %pad_add_fusion.place_ref, s32[1,1024]{1,0:T(1,128)S(1)} %bitcast.46, bf16[128,1024]{1,0:T(8,128)(2,1)S(1)} %copy-done.6, bf16[8,64,256]{2,1,0:T(8,128)(2,1)S(1)} %pad_maximum_fusion.mine_ref, bf16[8,64,256]{2,1,0:T(8,128)(2,1)} %collective-permute-done.3.other_ref), custom_call_target="tpu_custom_call" | custom-call | tf_op jit(solution)/shard_map/pallas_call | solution.py:217
  70.5 1.6 %collective-permute-start.4 = (bf16[64,256]{1,0:T(8,128)(2,1)S(1)}, bf16[64,256]{1,0:T(8,128)(2,1)S(1)}, u32[]{:S(2)}, u32[]{:S(2)}) collective-permute-start(bf16[64,256]{1,0:T(8,128)(2,1)S(1)} %constant_dynamic-slice_fusion), channel_id=1, source_target_pairs={{0,1},{1,0},{2,3},{3,2},{4,5},{5,4},{6,7},{7,6},{8,9},{9,8},{10,11... | collective-permute-start | bytes 98312 | tf_op jit(solution)/shard_map/ppermute | solution.py:30
  72.1 3.7 %copy-done.2 = bf16[1,768,6144]{2,1,0:T(8,128)(2,1)S(1)} copy-done((bf16[1,768,6144]{2,1,0:T(8,128)(2,1)S(1)}, bf16[1,768,6144]{2,1,0:T(8,128)(2,1)}, u32[]{:S(2)}) %copy-start.2) | copy-done | bytes 9437208
  75.8 5.4 %shard_map.112 = (f32[4,8,16,256]{3,2,1,0:T(8,128)S(1)}, bf16[4,8,16,256]{3,2,1,0:T(8,128)(2,1)S(1)}) custom-call(s32[8]{0:T(128)S(1)} %stack.116.scalars_ref, bf16[768,6144]{1,0:T(8,128)(2,1)S(1)} %bitcast.44, bf16[384,256]{1,0:T(8,128)(2,1)} %collective-permute-done.12.refs_0_, bf16[384,256]{1,0:T(8,128)(2,1)S(1)} %copy-done.22, ...), custom_call_target="tpu_custom_call" | custom-call | flops 1308622848 | bytes 5111808 | tf_op jit(solution)/shard_map/pallas_call | solution.py:124
  81.9 7.2 %collective-permute-done.22.come_ref = bf16[4,8,16,256]{3,2,1,0:T(8,128)(2,1)S(1)} collective-permute-done((bf16[4,8,16,256]{3,2,1,0:T(8,128)(2,1)S(1)}, bf16[4,8,16,256]{3,2,1,0:T(8,128)(2,1)S(1)}, u32[]{:S(2)}, u32[]{:S(2)}) %collective-permute-start.22) | collective-permute-done | bytes 262176 | tf_op jit(solution)/shard_map/ppermute | solution.py:30
  89.2 1.9 %collective-permute-start.24 = (bf16[8,16,256]{2,1,0:T(8,128)(2,1)S(1)}, bf16[8,16,256]{2,1,0:T(8,128)(2,1)S(1)}, u32[]{:S(2)}, u32[]{:S(2)}) collective-permute-start(bf16[8,16,256]{2,1,0:T(8,128)(2,1)S(1)} %get-tuple-element.39), channel_id=1, source_target_pairs={{0,4},{1,5},{2,6},{3,7},{4,0},{5,1},{6,2},{7,3},{8,12},{9,13},{10,... | collective-permute-start | bytes 196616 | tf_op jit(solution)/shard_map/ppermute | solution.py:30
  91.1 2.5 %collective-permute-start.25 = (bf16[8,16,256]{2,1,0:T(8,128)(2,1)S(1)}, bf16[8,16,256]{2,1,0:T(8,128)(2,1)S(1)}, u32[]{:S(2)}, u32[]{:S(2)}) collective-permute-start(bf16[8,16,256]{2,1,0:T(8,128)(2,1)S(1)} %get-tuple-element.40), channel_id=1, source_target_pairs={{0,6},{1,7},{2,4},{3,5},{4,2},{5,3},{6,0},{7,1},{8,14},{9,15},{10,... | collective-permute-start | bytes 196616 | tf_op jit(solution)/shard_map/ppermute | solution.py:30
  94.7 5.3 %collective-permute-done.24 = bf16[8,16,256]{2,1,0:T(8,128)(2,1)S(1)} collective-permute-done((bf16[8,16,256]{2,1,0:T(8,128)(2,1)S(1)}, bf16[8,16,256]{2,1,0:T(8,128)(2,1)S(1)}, u32[]{:S(2)}, u32[]{:S(2)}) %collective-permute-start.24) | collective-permute-done | bytes 65568 | tf_op jit(solution)/shard_map/ppermute | solution.py:30
  102.1 2.6 %collective-permute-done.27.refs_2_ = bf16[8,16,256]{2,1,0:T(8,128)(2,1)S(1)} collective-permute-done((bf16[8,16,256]{2,1,0:T(8,128)(2,1)S(1)}, bf16[8,16,256]{2,1,0:T(8,128)(2,1)S(1)}, u32[]{:S(2)}, u32[]{:S(2)}) %collective-permute-start.27) | collective-permute-done | bytes 65568 | tf_op jit(solution)/shard_map/ppermute | solution.py:46
  105.7 1.6 %shard_map.114 = bf16[32,16,256]{2,1,0:T(8,128)(2,1)} custom-call(s32[4,8]{1,0:T(4,128)S(1)} %copy-done.24, s32[2]{0:T(128)S(1)} %pad_add_fusion.1.first_ref, bf16[8,16,256]{2,1,0:T(8,128)(2,1)S(1)} %add_convert_fusion.refs_0_, bf16[8,16,256]{2,1,0:T(8,128)(2,1)S(1)} %collective-permute-done.26.refs_1_, ...), custom_call_target="tpu_custom_call" | custom-call | tf_op jit(solution)/shard_map/pallas_call | solution.py:183
  107.4 4.4 %all-to-all-start = ((bf16[8,4,16,256]{3,2,1,0:T(8,128)(2,1)}), bf16[8,4,16,256]{3,2,1,0:T(8,128)(2,1)S(1)}, u32[]{:S(2)}, u32[]{:S(2)}) async-start(bf16[8,4,16,256]{3,2,1,0:T(8,128)(2,1)} %bitcast.35), calls=%async_computation | async-start | bytes 524288 | tf_op jit(solution)/shard_map/all_to_all | solution.py:329
  116.2 4.8 %all-to-all-done = bf16[8,4,16,256]{3,2,1,0:T(8,128)(2,1)S(1)} async-done(((bf16[8,4,16,256]{3,2,1,0:T(8,128)(2,1)}), bf16[8,4,16,256]{3,2,1,0:T(8,128)(2,1)S(1)}, u32[]{:S(2)}, u32[]{:S(2)}) %all-to-all-start) | async-done | bytes 262176 | tf_op jit(solution)/shard_map/all_to_all | solution.py:329
  (119 shorter events, 35.9 us)
Async XLA Ops:
  3.2 17.0 %collective-permute-start.14 = (bf16[384,256]{1,0:T(8,128)(2,1)S(1)}, bf16[384,256]{1,0:T(8,128)(2,1)S(1)}, u32[]{:S(2)}, u32[]{:S(2)}) collective-permute-start(bf16[384,256]{1,0:T(8,128)(2,1)S(1)} %get-tuple-element.41.refs_1_), channel_id=1, source_target_pairs={{0,2},{1,3},{2,6},{3,7},{4,0},{5,1},{6,4},{7,5},{8,10},{9,11},{10,... | collective-permute-start | bytes 589832 | tf_op jit(solution)/shard_map/ppermute | solution.py:30
  6.3 13.9 %collective-permute-start.15 = (bf16[384,256]{1,0:T(8,128)(2,1)S(1)}, bf16[384,256]{1,0:T(8,128)(2,1)S(1)}, u32[]{:S(2)}, u32[]{:S(2)}) collective-permute-start(bf16[384,256]{1,0:T(8,128)(2,1)S(1)} %get-tuple-element.41.refs_1_), channel_id=1, source_target_pairs={{0,1},{1,0},{2,3},{3,2},{4,5},{5,4},{6,7},{7,6},{8,9},{9,8},{10,11... | collective-permute-start | bytes 589832 | tf_op jit(solution)/shard_map/ppermute | solution.py:30
  7.8 14.1 %collective-permute-start.8 = (bf16[384,256]{1,0:T(8,128)(2,1)S(1)}, bf16[384,256]{1,0:T(8,128)(2,1)S(1)}, u32[]{:S(2)}, u32[]{:S(2)}) collective-permute-start(bf16[384,256]{1,0:T(8,128)(2,1)S(1)} %get-tuple-element.42.refs_0_), channel_id=1, source_target_pairs={{0,2},{1,3},{2,6},{3,7},{4,0},{5,1},{6,4},{7,5},{8,10},{9,11},{10,... | collective-permute-start | bytes 589832 | tf_op jit(solution)/shard_map/ppermute | solution.py:30
  10.4 11.5 %collective-permute-start.9 = (bf16[384,256]{1,0:T(8,128)(2,1)S(1)}, bf16[384,256]{1,0:T(8,128)(2,1)S(1)}, u32[]{:S(2)}, u32[]{:S(2)}) collective-permute-start(bf16[384,256]{1,0:T(8,128)(2,1)S(1)} %get-tuple-element.42.refs_0_), channel_id=1, source_target_pairs={{0,1},{1,0},{2,3},{3,2},{4,5},{5,4},{6,7},{7,6},{8,9},{9,8},{10,11... | collective-permute-start | bytes 589832 | tf_op jit(solution)/shard_map/ppermute | solution.py:30
  17.6 11.0 %collective-permute-start.1 = (bf16[2,64,256]{2,1,0:T(8,128)(2,1)S(1)}, bf16[2,64,256]{2,1,0:T(8,128)(2,1)S(1)}, u32[]{:S(2)}, u32[]{:S(2)}) collective-permute-start(bf16[2,64,256]{2,1,0:T(8,128)(2,1)S(1)} %pad_maximum_fusion.4), channel_id=1, source_target_pairs={{0,2},{1,3},{2,0},{3,1},{4,6},{5,7},{6,4},{7,5},{8,10},{9,11},{10,... | collective-permute-start | bytes 196616 | tf_op jit(solution)/shard_map/ppermute | solution.py:30
  20.3 10.0 %collective-permute-start.16 = (bf16[384,256]{1,0:T(8,128)(2,1)S(1)}, bf16[384,256]{1,0:T(8,128)(2,1)S(1)}, u32[]{:S(2)}, u32[]{:S(2)}) collective-permute-start(bf16[384,256]{1,0:T(8,128)(2,1)S(1)} %collective-permute-done.14.refs_4_), channel_id=1, source_target_pairs={{0,2},{1,3},{2,6},{3,7},{4,0},{5,1},{6,4},{7,5},{8,10},{9,11},{10,... | collective-permute-start | bytes 589832 | tf_op jit(solution)/shard_map/ppermute | solution.py:30
  20.4 9.9 %collective-permute-start.17 = (bf16[384,256]{1,0:T(8,128)(2,1)S(1)}, bf16[384,256]{1,0:T(8,128)(2,1)S(1)}, u32[]{:S(2)}, u32[]{:S(2)}) collective-permute-start(bf16[384,256]{1,0:T(8,128)(2,1)S(1)} %collective-permute-done.14.refs_4_), channel_id=1, source_target_pairs={{0,1},{1,0},{2,3},{3,2},{4,5},{5,4},{6,7},{7,6},{8,9},{9,8},{10,11... | collective-permute-start | bytes 589832 | tf_op jit(solution)/shard_map/ppermute | solution.py:30
  22.6 13.3 %collective-permute-start.10 = (bf16[384,256]{1,0:T(8,128)(2,1)S(1)}, bf16[384,256]{1,0:T(8,128)(2,1)S(1)}, u32[]{:S(2)}, u32[]{:S(2)}) collective-permute-start(bf16[384,256]{1,0:T(8,128)(2,1)S(1)} %collective-permute-done.8.refs_2_), channel_id=1, source_target_pairs={{0,2},{1,3},{2,6},{3,7},{4,0},{5,1},{6,4},{7,5},{8,10},{9,11},{10,... | collective-permute-start | bytes 589832 | tf_op jit(solution)/shard_map/ppermute | solution.py:30
  23.4 12.6 %collective-permute-start.11 = (bf16[384,256]{1,0:T(8,128)(2,1)S(1)}, bf16[384,256]{1,0:T(8,128)(2,1)S(1)}, u32[]{:S(2)}, u32[]{:S(2)}) collective-permute-start(bf16[384,256]{1,0:T(8,128)(2,1)S(1)} %collective-permute-done.8.refs_2_), channel_id=1, source_target_pairs={{0,1},{1,0},{2,3},{3,2},{4,5},{5,4},{6,7},{7,6},{8,9},{9,8},{10,11... | collective-permute-start | bytes 589832 | tf_op jit(solution)/shard_map/ppermute | solution.py:30
  28.6 10.3 %collective-permute-start.2 = (bf16[4,64,256]{2,1,0:T(8,128)(2,1)S(1)}, bf16[4,64,256]{2,1,0:T(8,128)(2,1)S(1)}, u32[]{:S(2)}, u32[]{:S(2)}) collective-permute-start(bf16[4,64,256]{2,1,0:T(8,128)(2,1)S(1)} %pad_maximum_fusion.2), channel_id=1, source_target_pairs={{0,4},{1,5},{2,6},{3,7},{4,0},{5,1},{6,2},{7,3},{8,12},{9,13},{10,... | collective-permute-start | bytes 393224 | tf_op jit(solution)/shard_map/ppermute | solution.py:30
  30.3 18.6 %collective-permute-start.18 = (bf16[384,256]{1,0:T(8,128)(2,1)S(1)}, bf16[384,256]{1,0:T(8,128)(2,1)}, u32[]{:S(2)}, u32[]{:S(2)}) collective-permute-start(bf16[384,256]{1,0:T(8,128)(2,1)S(1)} %collective-permute-done.16.refs_8_), channel_id=1, source_target_pairs={{0,2},{1,3},{2,6},{3,7},{4,0},{5,1},{6,4},{7,5},{8,10},{9,11},{10,... | collective-permute-start | bytes 589832 | tf_op jit(solution)/shard_map/ppermute | solution.py:30
  32.5 16.4 %collective-permute-start.19 = (bf16[384,256]{1,0:T(8,128)(2,1)S(1)}, bf16[384,256]{1,0:T(8,128)(2,1)}, u32[]{:S(2)}, u32[]{:S(2)}) collective-permute-start(bf16[384,256]{1,0:T(8,128)(2,1)S(1)} %collective-permute-done.16.refs_8_), channel_id=1, source_target_pairs={{0,1},{1,0},{2,3},{3,2},{4,5},{5,4},{6,7},{7,6},{8,9},{9,8},{10,11... | collective-permute-start | bytes 589832 | tf_op jit(solution)/shard_map/ppermute | solution.py:30
  36.7 13.8 %collective-permute-start.12 = (bf16[384,256]{1,0:T(8,128)(2,1)S(1)}, bf16[384,256]{1,0:T(8,128)(2,1)}, u32[]{:S(2)}, u32[]{:S(2)}) collective-permute-start(bf16[384,256]{1,0:T(8,128)(2,1)S(1)} %collective-permute-done.10.refs_6_), channel_id=1, source_target_pairs={{0,2},{1,3},{2,6},{3,7},{4,0},{5,1},{6,4},{7,5},{8,10},{9,11},{10,... | collective-permute-start | bytes 589832 | tf_op jit(solution)/shard_map/ppermute | solution.py:30
  36.7 13.8 %collective-permute-start.13 = (bf16[384,256]{1,0:T(8,128)(2,1)S(1)}, bf16[384,256]{1,0:T(8,128)(2,1)S(1)}, u32[]{:S(2)}, u32[]{:S(2)}) collective-permute-start(bf16[384,256]{1,0:T(8,128)(2,1)S(1)} %collective-permute-done.10.refs_6_), channel_id=1, source_target_pairs={{0,1},{1,0},{2,3},{3,2},{4,5},{5,4},{6,7},{7,6},{8,9},{9,8},{10,11... | collective-permute-start | bytes 589832 | tf_op jit(solution)/shard_map/ppermute | solution.py:30
  39.0 28.4 %collective-permute-start.3 = (bf16[8,64,256]{2,1,0:T(8,128)(2,1)S(1)}, bf16[8,64,256]{2,1,0:T(8,128)(2,1)}, u32[]{:S(2)}, u32[]{:S(2)}) collective-permute-start(bf16[8,64,256]{2,1,0:T(8,128)(2,1)S(1)} %pad_maximum_fusion.mine_ref), channel_id=1, source_target_pairs={{0,8},{8,0},{16,24},{24,16},{1,9},{9,1},{17,25},{25,17},{2,10},{10... | collective-permute-start | bytes 786440 | tf_op jit(solution)/shard_map/ppermute | solution.py:46
  48.9 23.2 %collective-permute-start.21 = (bf16[384,256]{1,0:T(8,128)(2,1)}, bf16[384,256]{1,0:T(8,128)(2,1)S(1)}, u32[]{:S(2)}, u32[]{:S(2)}) collective-permute-start(bf16[384,256]{1,0:T(8,128)(2,1)} %collective-permute-done.18.refs_2_), channel_id=1, source_target_pairs={{0,1},{1,0},{2,3},{3,2},{4,5},{5,4},{6,7},{7,6},{8,9},{9,8},{10,11... | collective-permute-start | bytes 589832 | tf_op jit(solution)/shard_map/ppermute | solution.py:30
  51.1 21.0 %collective-permute-start.20 = (bf16[384,256]{1,0:T(8,128)(2,1)}, bf16[384,256]{1,0:T(8,128)(2,1)S(1)}, u32[]{:S(2)}, u32[]{:S(2)}) collective-permute-start(bf16[384,256]{1,0:T(8,128)(2,1)} %collective-permute-done.12.refs_0_), channel_id=1, source_target_pairs={{0,1},{1,0},{2,3},{3,2},{4,5},{5,4},{6,7},{7,6},{8,9},{9,8},{10,11... | collective-permute-start | bytes 589832 | tf_op jit(solution)/shard_map/ppermute | solution.py:30
  70.5 11.3 %collective-permute-start.4 = (bf16[64,256]{1,0:T(8,128)(2,1)S(1)}, bf16[64,256]{1,0:T(8,128)(2,1)S(1)}, u32[]{:S(2)}, u32[]{:S(2)}) collective-permute-start(bf16[64,256]{1,0:T(8,128)(2,1)S(1)} %constant_dynamic-slice_fusion), channel_id=1, source_target_pairs={{0,1},{1,0},{2,3},{3,2},{4,5},{5,4},{6,7},{7,6},{8,9},{9,8},{10,11... | collective-permute-start | bytes 98312 | tf_op jit(solution)/shard_map/ppermute | solution.py:30
  81.2 7.9 %collective-permute-start.22 = (bf16[4,8,16,256]{3,2,1,0:T(8,128)(2,1)S(1)}, bf16[4,8,16,256]{3,2,1,0:T(8,128)(2,1)S(1)}, u32[]{:S(2)}, u32[]{:S(2)}) collective-permute-start(bf16[4,8,16,256]{3,2,1,0:T(8,128)(2,1)S(1)} %get-tuple-element.36), channel_id=1, source_target_pairs={{0,1},{1,0},{2,3},{3,2},{4,5},{5,4},{6,7},{7,6},{8,9},{9,8},{10,11... | collective-permute-start | bytes 786440 | tf_op jit(solution)/shard_map/ppermute | solution.py:30
  81.8 11.8 %collective-permute-start.5 = (bf16[2,64,256]{2,1,0:T(8,128)(2,1)S(1)}, bf16[2,64,256]{2,1,0:T(8,128)(2,1)S(1)}, u32[]{:S(2)}, u32[]{:S(2)}) collective-permute-start(bf16[2,64,256]{2,1,0:T(8,128)(2,1)S(1)} %pad_maximum_fusion.5), channel_id=1, source_target_pairs={{0,2},{1,3},{2,0},{3,1},{4,6},{5,7},{6,4},{7,5},{8,10},{9,11},{10,... | collective-permute-start | bytes 196616 | tf_op jit(solution)/shard_map/ppermute | solution.py:30
  89.2 10.8 %collective-permute-start.24 = (bf16[8,16,256]{2,1,0:T(8,128)(2,1)S(1)}, bf16[8,16,256]{2,1,0:T(8,128)(2,1)S(1)}, u32[]{:S(2)}, u32[]{:S(2)}) collective-permute-start(bf16[8,16,256]{2,1,0:T(8,128)(2,1)S(1)} %get-tuple-element.39), channel_id=1, source_target_pairs={{0,4},{1,5},{2,6},{3,7},{4,0},{5,1},{6,2},{7,3},{8,12},{9,13},{10,... | collective-permute-start | bytes 196616 | tf_op jit(solution)/shard_map/ppermute | solution.py:30
  91.1 8.9 %collective-permute-start.25 = (bf16[8,16,256]{2,1,0:T(8,128)(2,1)S(1)}, bf16[8,16,256]{2,1,0:T(8,128)(2,1)S(1)}, u32[]{:S(2)}, u32[]{:S(2)}) collective-permute-start(bf16[8,16,256]{2,1,0:T(8,128)(2,1)S(1)} %get-tuple-element.40), channel_id=1, source_target_pairs={{0,6},{1,7},{2,4},{3,5},{4,2},{5,3},{6,0},{7,1},{8,14},{9,15},{10,... | collective-permute-start | bytes 196616 | tf_op jit(solution)/shard_map/ppermute | solution.py:30
  94.4 17.4 %collective-permute-start.6 = (bf16[4,64,256]{2,1,0:T(8,128)(2,1)S(1)}, bf16[4,64,256]{2,1,0:T(8,128)(2,1)S(1)}, u32[]{:S(2)}, u32[]{:S(2)}) collective-permute-start(bf16[4,64,256]{2,1,0:T(8,128)(2,1)S(1)} %pad_maximum_fusion.3), channel_id=1, source_target_pairs={{0,4},{1,5},{2,6},{3,7},{4,0},{5,1},{6,2},{7,3},{8,12},{9,13},{10,... | collective-permute-start | bytes 393224 | tf_op jit(solution)/shard_map/ppermute | solution.py:30
  107.4 13.6 %all-to-all-start = ((bf16[8,4,16,256]{3,2,1,0:T(8,128)(2,1)}), bf16[8,4,16,256]{3,2,1,0:T(8,128)(2,1)S(1)}, u32[]{:S(2)}, u32[]{:S(2)}) async-start(bf16[8,4,16,256]{3,2,1,0:T(8,128)(2,1)} %bitcast.35), calls=%async_computation | async-start | bytes 524288 | tf_op jit(solution)/shard_map/all_to_all | solution.py:329
  (32 other events, 382.6 us)

commit v2 on v0

v2 whole, which is shorter than its diff:
```python
import functools

import jax
import jax.numpy as jnp
from jax import lax
from jax.experimental import pallas as pl
from jax.experimental.pallas import tpu as pltpu
from jax.sharding import PartitionSpec as P

BLOCK = 128
PARTS = 2
NEXT = (1, 3, 0, 2)
LIMIT = 20 << 20
F32 = jnp.float32
BF16 = jnp.bfloat16
together = lax.optimization_barrier


def params():
    return pltpu.CompilerParams(vmem_limit_bytes=LIMIT)


def row_permute(value, target):
    pairs = [(z * 2 + y, target(z, y)) for z in range(4) for y in range(2)]
    return lax.ppermute(value, "row", [(s, t[0] * 2 + t[1]) for s, t in pairs])


def cycle(value):
    return row_permute(value, lambda z, y: (NEXT[z], y))


def across(value):
    return row_permute(value, lambda z, y: (z, 1 - y))


def along(value, step):
    return row_permute(value, lambda z, y: (z ^ step, y))


def group_swap(value, step):
    return lax.ppermute(value, "grp", [(g, g ^ step) for g in range(4)])


def before(place):
    return (place >> 1) | ((1 - (place & 1)) << 1)


SMEM = pl.BlockSpec(memory_space=pltpu.SMEM)
VMEM = pl.BlockSpec(memory_space=pltpu.VMEM)
HBM = pl.BlockSpec(memory_space=pltpu.HBM)


def source_rows(spot_ref, steps, crossed):
    row = spot_ref[0]
    spot = row // 2
    for _ in range(steps):
        spot = before(spot)
    return spot * 2 + ((row & 1) ^ crossed)


def live_rows(piece, first, live):
    ids = lax.broadcasted_iota(jnp.int32, piece.shape, 0)
    return jnp.where(ids < live - first, piece.astype(F32), 0.0).astype(BF16)


def multiply_body(names, spot_ref, sizes_ref, inverse_ref, *refs):
    pieces = refs[: len(names)]
    total_ref, later_ref, left, right, sem = refs[len(names) :]
    chunks, height, _ = left.shape
    copies = [
        pltpu.make_async_copy(inverse_ref.at[pl.ds(c * height, height)], left.at[c], sem.at[c])
        for c in range(chunks)
    ]
    for copy in copies:
        copy.start()
    live = sizes_ref[spot_ref[1]]
    width, cols = right.shape
    share = later_ref.shape[1]
    depth = share // PARTS
    for (steps, crossed, part), piece in zip(names, pieces):
        source = source_rows(spot_ref, steps, crossed)
        first = pl.multiple_of((source * PARTS + part) * depth, depth)
        right[pl.ds(first, depth)] = live_rows(piece[:depth], first, live)
    late = pl.multiple_of(source_rows(spot_ref, 3, 1) * share, share)
    right[pl.ds(late, share)] = jnp.zeros((share, cols), BF16)
    for c in range(chunks):
        copies[c].wait()
        rows = pl.ds(c * height, height)
        total_ref[rows] = jnp.dot(left[c], right[...], preferred_element_type=F32)
        later_ref[rows] = left[c, :, pl.ds(late, share)]


def multiply(spot, sizes, inverse, depth, named):
    names = tuple(n[:3] for n in named)
    pieces = [n[3] for n in named]
    rows, width = inverse.shape
    cols = pieces[0].shape[1]
    chunks = 3
    return pl.pallas_call(
        functools.partial(multiply_body, names),
        out_shape=[
            jax.ShapeDtypeStruct((rows, cols), F32),
            jax.ShapeDtypeStruct((rows, depth * PARTS), BF16),
        ],
        in_specs=[SMEM, SMEM, HBM] + [VMEM] * len(pieces),
        out_specs=[VMEM, VMEM],
        scratch_shapes=[
            pltpu.VMEM((chunks, rows // chunks, width), BF16),
            pltpu.VMEM((width, cols), BF16),
            pltpu.SemaphoreType.DMA((chunks,)),
        ],
        compiler_params=params(),
        cost_estimate=pl.CostEstimate(
            flops=2 * rows * width * cols, bytes_accessed=2 * rows * width, transcendentals=0
        ),
    )(spot, sizes, inverse, *pieces)


def contribute_body(spot_ref, sizes_ref, total_ref, later_ref, lower_ref, *refs):
    pieces, carriers, outs = refs[:PARTS], refs[PARTS:-11], refs[-11:-3]
    top_ref, right, product_ref = refs[-3:]
    live, row = sizes_ref[spot_ref[1]], spot_ref[0]
    depth = later_ref.shape[1] // PARTS
    for k, carrier in enumerate((*carriers, pieces[0])):
        top_ref[k] = carrier[depth:]
    first = source_rows(spot_ref, 3, 1) * PARTS * depth
    for part, piece in enumerate(pieces):
        place = part * depth
        right[place : place + depth] = live_rows(piece[:depth], first + place, live)
    total = total_ref[...] + jnp.dot(later_ref[...], right[...], preferred_element_type=F32)
    solved = live_rows(total, row * total.shape[0], live)
    product_ref[...] = jnp.dot(lower_ref[...], solved, preferred_element_type=F32)
    z, y = row // 2, row & 1
    slabs, height, _ = outs[0].shape
    for k in range(4):
        for j in range(slabs):
            base = j * BLOCK + (z ^ k) * 2 * height
            mine = pl.multiple_of(base + y * height, height)
            other = pl.multiple_of(base + (1 - y) * height, height)
            outs[k][j] = product_ref[pl.ds(mine, height)]
            outs[4 + k][j] = product_ref[pl.ds(other, height)].astype(BF16)


def contribute(spot, sizes, total, later, lower, pieces, carriers):
    border, rows = lower.shape
    cols = total.shape[1]
    slot = (border // BLOCK, BLOCK // 8, cols)
    count = len(carriers) + 1
    tops = (count, pieces[0].shape[0] - later.shape[1] // PARTS, cols)
    out = pl.pallas_call(
        contribute_body,
        out_shape=[jax.ShapeDtypeStruct(slot, F32)] * 4
        + [jax.ShapeDtypeStruct(slot, BF16)] * 4
        + [jax.ShapeDtypeStruct(tops, BF16)],
        in_specs=[SMEM, SMEM] + [VMEM] * (3 + len(pieces) + len(carriers)),
        out_specs=[VMEM] * 9,
        scratch_shapes=[
            pltpu.VMEM((later.shape[1], cols), BF16),
            pltpu.VMEM((border, cols), F32),
        ],
        compiler_params=params(),
        cost_estimate=pl.CostEstimate(
            flops=2 * rows * cols * (later.shape[1] + border),
            bytes_accessed=2 * rows * (later.shape[1] + border),
            transcendentals=0,
        ),
    )(spot, sizes, total, later, lower, *pieces, *carriers)
    return out[:4], out[4:8], out[8]


def place_body(targets_ref, spot_ref, *refs):
    pieces, slots_ref, total_ref = refs[:4], refs[4], refs[5]
    total_ref[...] = jnp.zeros_like(total_ref)
    blocks = total_ref.shape[0]
    slabs = pieces[0].shape[0]
    group = spot_ref[1]
    first = group * blocks
    for k, piece in enumerate(pieces):
        for j in range(slabs):
            place = targets_ref[group ^ k, j] - first

            @pl.when((place >= 0) & (place < blocks))
            def _():
                total_ref[place] += piece[j].astype(F32)

    slots_ref[...] = total_ref[...].astype(BF16)


def place(targets, spot, pieces, blocks):
    shape = (blocks,) + pieces[0].shape[1:]
    return pl.pallas_call(
        place_body,
        out_shape=jax.ShapeDtypeStruct(shape, BF16),
        in_specs=[pl.BlockSpec(memory_space=pltpu.SMEM)] * 2
        + [pl.BlockSpec(memory_space=pltpu.VMEM)] * 4,
        out_specs=pl.BlockSpec(memory_space=pltpu.VMEM),
        scratch_shapes=[pltpu.VMEM(shape, F32)],
        compiler_params=params(),
    )(targets, spot, *pieces)


ORDER = ((0, 0), (0, 1), (1, 0), (1, 1), (2, 0), (2, 1), (3, 0), (3, 1))


def reorder_body(spot_ref, order_ref, inverse_ref, *out_refs):
    row, core = spot_ref[0], spot_ref[1] & 1
    half, width = inverse_ref.shape[0] // 2, inverse_ref.shape[1]
    rows = (row * 2 + core) * half + lax.broadcasted_iota(jnp.int32, (half, width), 0)
    cols = lax.broadcasted_iota(jnp.int32, (half, width), 1)
    mine = inverse_ref[pl.ds(pl.multiple_of(core * half, half), half)].astype(F32)
    lower = jnp.where(cols < rows, mine, jnp.where(cols == rows, 1.0, 0.0)).astype(BF16)
    for side, out_ref in ((core, out_refs[0]), (1 - core, out_refs[1])):
        picks = []
        for steps, crossed in ORDER:
            first = (source_rows(spot_ref, steps, crossed) * 2 + side) * half
            ids = first + lax.broadcasted_iota(jnp.int32, (half, width), 0)
            picks.append((ids == order_ref[...]).astype(F32).astype(BF16))
        pick = jnp.concatenate(picks)
        moved = lax.dot_general(
            lower, pick, (((1,), (1,)), ((), ())), preferred_element_type=F32
        )
        out_ref[...] = moved.astype(BF16)


def reorder(spot, order, inverse):
    half, width = inverse.shape[0] // 2, inverse.shape[1]
    return pl.pallas_call(
        reorder_body,
        out_shape=[jax.ShapeDtypeStruct((half, width // 2), BF16)] * 2,
        in_specs=[SMEM, VMEM, VMEM],
        out_specs=[VMEM, VMEM],
        compiler_params=params(),
    )(spot, order[None], inverse)


def factor_body(mine_ref, other_ref, top_ref, came_ref, out_ref):
    count, half, cols = top_ref.shape
    total = jnp.dot(
        mine_ref[...], top_ref[...].reshape(count * half, cols), preferred_element_type=F32
    ) + jnp.dot(
        other_ref[...], came_ref[...].reshape(count * half, cols), preferred_element_type=F32
    )
    out_ref[...] = total.astype(BF16)


def panel_factor(mine, other, top, came):
    return pl.pallas_call(
        factor_body,
        out_shape=jax.ShapeDtypeStruct((mine.shape[0], top.shape[-1]), BF16),
        in_specs=[VMEM] * 4,
        out_specs=VMEM,
        compiler_params=params(),
    )(mine, other, top, came)


def base_body(place_ref, surface_ref, lower_ref, mine_ref, other_ref, out_ref, factor_ref):
    row, core = place_ref[0], place_ref[1] & 1
    half = mine_ref.shape[1]
    for ref, side in ((mine_ref, core), (other_ref, 1 - core)):
        for k in range(mine_ref.shape[0]):
            first = pl.multiple_of(((row ^ k) * 2 + side) * half, half)
            factor_ref[pl.ds(first, half)] = ref[k]
    product = jnp.dot(lower_ref[...], factor_ref[...], preferred_element_type=F32)
    out_ref[...] = surface_ref[...] - product


def panel_update(place_scalars, surface, lower, mine, other):
    return pl.pallas_call(
        base_body,
        out_shape=jax.ShapeDtypeStruct(surface.shape, F32),
        in_specs=[pl.BlockSpec(memory_space=pltpu.SMEM)]
        + [pl.BlockSpec(memory_space=pltpu.VMEM)] * 4,
        out_specs=pl.BlockSpec(memory_space=pltpu.VMEM),
        scratch_shapes=[pltpu.VMEM((lower.shape[1], surface.shape[1]), BF16)],
        compiler_params=params(),
    )(place_scalars, surface, lower, mine, other)


def staged(
    surface,
    panel_lower,
    top_rows,
    panel_inverse,
    panel_order,
    front_inverse,
    front_upper,
    front_lower,
    front_sizes,
    border_blocks,
):
    row_count = lax.axis_size("row")
    group = lax.axis_index("grp")
    row = lax.axis_index("row")
    core = group % 2
    inverse, upper, lower = front_inverse[0], front_upper[0], front_lower[0]
    spot = jnp.stack([row, group])
    inverse = pltpu.with_memory_space_constraint(inverse, pltpu.HBM)
    depth = upper.shape[0] // PARTS

    half = top_rows.shape[0] // 2
    top = lax.dynamic_slice_in_dim(top_rows, core * half, half, 0)
    a, b = jnp.concatenate([upper[:depth], top]), upper[depth:]

    ay, az, by, bz = across(a), cycle(a), across(b), cycle(b)
    lower_mine, lower_other = reorder(spot, panel_order, panel_inverse)
    ay, az, lower_mine = together((ay, az, lower_mine))
    ay1, az1 = across(az), cycle(az)
    by, bz = together((by, bz))
    by1, bz1 = across(bz), cycle(bz)
    ay1, az1 = together((ay1, az1))
    ay2, az2 = across(az1), cycle(az1)
    by1, bz1 = together((by1, bz1))
    by2, bz2 = across(bz1), cycle(bz1)
    ay2, az2 = together((ay2, az2))
    ay3 = across(az2)
    by2, bz2, ay = together((by2, bz2, ay))
    by3 = across(bz2)
    named = [(0, 0, 0, a), (0, 0, 1, b), (0, 1, 0, ay), (0, 1, 1, by)]
    named += [(1, 0, 0, az), (1, 0, 1, bz), (1, 1, 0, ay1), (1, 1, 1, by1)]
    named += [(2, 0, 0, az1), (2, 0, 1, bz1), (2, 1, 0, ay2), (2, 1, 1, by2)]
    named += [(3, 0, 0, az2), (3, 0, 1, bz2)]
    total, later = multiply(spot, front_sizes, inverse, depth, named)
    carriers = (a, ay, az, ay1, az1, ay2, az2)
    keep, send, top_mine = contribute(
        spot, front_sizes, total, later, lower, (ay3, by3), carriers
    )

    top_other = group_swap(top_mine, 1)
    come = {k: across(send[k]) for k in (3, 2, 1, 0)}
    sums = [keep[k] + come[k].astype(F32) for k in range(4)]
    for k in (3, 2, 1):
        sums[k] = along(sums[k].astype(BF16), k).astype(F32)
    factor = panel_factor(lower_mine, lower_other, top_mine, top_other)
    factor_y = across(factor)
    mine = (sums[0] + sums[1] + sums[2] + sums[3]).astype(BF16)
    mine, factor_y = together((mine, factor_y))
    factor2 = jnp.stack([factor, factor_y])
    factor2_in = along(factor2, 1)
    pieces = [mine] + [group_swap(mine, k) for k in (1, 2, 3)]
    local_blocks = surface.shape[0] // BLOCK
    blocks = local_blocks * row_count
    slots = place(border_blocks, spot, pieces, blocks)
    slots, factor2_in = together((slots, factor2_in))
    factor4 = jnp.concatenate([factor2, factor2_in])
    factor_mine = jnp.concatenate([factor4, along(factor4, 2)])
    factor_other = group_swap(factor_mine, 1)
    base = panel_update(spot, surface, panel_lower, factor_mine, factor_other)
    slots = slots.reshape((row_count, local_blocks) + slots.shape[1:])
    got = lax.all_to_all(slots, "row", 0, 0, tiled=True)
    collected = got.transpose(1, 0, 2, 3).reshape(surface.shape).astype(F32)
    return base - collected


def gathered(
    surface,
    panel_lower,
    top_rows,
    panel_inverse,
    panel_order,
    front_inverse,
    front_upper,
    front_lower,
    front_sizes,
    border_blocks,
):
    row_count = lax.axis_size("row")
    grp_index = lax.axis_index("grp")
    row_index = lax.axis_index("row")
    inverse_rows, upper_local, lower_local = front_inverse[0], front_upper[0], front_lower[0]
    local_piv, col_count = upper_local.shape
    pivot_ids = row_index * local_piv + jnp.arange(local_piv, dtype=jnp.int32)
    live_mask = pivot_ids < front_sizes[grp_index]
    upper_kept = jnp.where(live_mask[:, None], upper_local, jnp.zeros_like(upper_local))
    lower_kept = jnp.where(live_mask[None, :], lower_local, jnp.zeros_like(lower_local))
    upper_all = lax.all_gather(upper_kept, "row", axis=0, tiled=True)
    solved = jnp.dot(inverse_rows, upper_all, preferred_element_type=F32).astype(BF16)
    partial_sum = jnp.dot(lower_kept, solved, preferred_element_type=F32)
    own_share = lax.psum_scatter(partial_sum, "row", scatter_dimension=0, tiled=True)
    contributions = lax.all_gather(own_share, ("grp", "row"), axis=0, tiled=True)
    local_blocks = surface.shape[0] // BLOCK
    device_id = grp_index * row_count + row_index
    own_ids = device_id * local_blocks + jnp.arange(local_blocks, dtype=jnp.int32)
    targets = border_blocks.reshape(-1)
    selector = (own_ids[:, None] == targets[None, :]).astype(F32)
    slabs = contributions.reshape(targets.shape[0], BLOCK * col_count)
    collected = jnp.dot(
        selector, slabs, precision=lax.Precision.HIGHEST, preferred_element_type=F32
    ).reshape(surface.shape)
    local_panel, panel_width = panel_inverse.shape
    panel_ids = jnp.arange(panel_width, dtype=jnp.int32)
    top_all = lax.all_gather(top_rows, "row", axis=0, tiled=True)
    ordered = jnp.take(top_all, panel_order, axis=0)
    own_rows = row_index * local_panel + jnp.arange(local_panel, dtype=jnp.int32)
    strict = jnp.where(
        panel_ids[None, :] < own_rows[:, None], panel_inverse, jnp.zeros_like(panel_inverse)
    )
    own_top = lax.dynamic_slice_in_dim(ordered, row_index * local_panel, local_panel, 0)
    product = jnp.dot(strict, ordered, preferred_element_type=F32)
    own_solved = (product + own_top.astype(F32)).astype(BF16)
    factor = lax.all_gather(own_solved, "row", axis=0, tiled=True)
    return surface - collected - jnp.dot(panel_lower, factor, preferred_element_type=F32)


def solution(mesh):
    in_specs = (
        P(("grp", "row"), None),
        P(("grp", "row"), None),
        P("row", None),
        P("row", None),
        P(),
        P("grp", "row", None),
        P("grp", "row", None),
        P("grp", None, "row"),
        P(),
        P(),
    )
    out_specs = P(("grp", "row"), None)
    small = mesh.shape["row"] == 8 and mesh.shape["grp"] == 4
    return jax.shard_map(
        staged if small else gathered,
        mesh=mesh,
        in_specs=in_specs,
        out_specs=out_specs,
        check_vma=False,
    )
```

time: 231 us -> 85.4 us (0.37)
  waiting for transfers between devices: 125 us -> 28.9 us
  blocking collectives: 63.4 us -> 0 us
  starting transfers between devices: 0.09 us -> 38.7 us
  matrix products: 13.9 us -> 0 us
  Pallas kernels: 0 us -> 13.4 us
  between operations: 13.3 us -> 0.22 us
  local copies, waits for them, and re-layouts: 12.1 us -> 2.79 us
    all_gather x2 -> x0, blocking collectives: 63.4 us -> none  [the longest x1 31.8 us: per_device(): top_all = lax.all_gather(top_rows, 'row', axis=0, tiled=True)]
    all_gather x2 -> x0, waiting for transfers between devices: 63.2 us -> none  [the longest x1 63.2 us: per_device(): lax.all_gather(upper_kept, 'row', axis=0, tiled=True)]
    reduce_scatter x1 -> x0, waiting for transfers between devices: 62.2 us -> none  [per_device(): lax.psum_scatter(jnp.dot(lower_kept, solved, preferred_element_type=jnp.f...]
    ppermute x0 -> x29, starting transfers between devices: none -> 35.2 us  [the longest x24 33.3 us: row_permute(): return lax.ppermute(value, 'row', [(s, t[0] * 2 + t[1]) for s, t in pairs])]
    ppermute x0 -> x29, waiting for transfers between devices: none -> 26.1 us  [the longest x24 21.5 us: row_permute(): return lax.ppermute(value, 'row', [(s, t[0] * 2 + t[1]) for s, t in pairs])]
    dot_general x4 -> x0, matrix products: 13.9 us -> none  [the longest x1 9.53 us: per_device(): jnp.dot(lower_kept, solved, preferred_element_type=jnp.float32)]
    pallas_call x0 -> x6, Pallas kernels: none -> 13.4 us  [the longest x1 7.11 us: multiply(): pl.pallas_call(functools.partial(multiply_body, names), out_shape=[jax.Sh...]
    reshape x3 -> x0, local copies, waits for them, and re-layouts: 5.52 us -> none  [the longest x1 4.97 us: per_device(): slabs = contributions.reshape(targets.shape[0], BLOCK * col_count)]
  transfers between devices with their start and end apart: 3 -> 30, of which waited for: 2 -> 17; matrix products, arithmetic and copies ran while one was open for 2% -> 0% of each run, Pallas kernels for 0% -> 13%
where the time goes in v2:
time: 85.4 us; the launch traced here: 85.1 us
  starting transfers between devices  38.7 us (45%)
  waiting for transfers between devices  28.9 us (34%)
  Pallas kernels  13.4 us (16%)
  local copies, waits for them, and re-layouts  2.79 us (3%)
  other arithmetic  1.14 us (1%)
    ppermute x24, starting transfers between devices, row_permute(): return lax.ppermute(value, 'row', [(s, t[0] * 2 + t[1]) for s, t in pairs])  33.3 us
    ppermute x24, waiting for transfers between devices, row_permute(): return lax.ppermute(value, 'row', [(s, t[0] * 2 + t[1]) for s, t in pairs])  21.5 us
    pallas_call x1, Pallas kernels, multiply(): pl.pallas_call(functools.partial(multiply_body, names), out_shape=[jax.Sh...  7.11 us
    ppermute x5, waiting for transfers between devices, group_swap(): return lax.ppermute(value, 'grp', [(g, g ^ step) for g in range(4)])  4.58 us
    all_to_all x1, starting transfers between devices, staged(): got = lax.all_to_all(slots, 'row', 0, 0, tiled=True)  3.41 us
    all_to_all x1, waiting for transfers between devices, staged(): got = lax.all_to_all(slots, 'row', 0, 0, tiled=True)  2.81 us
    pallas_call x1, Pallas kernels, contribute(): pl.pallas_call(contribute_body, out_shape=[jax.ShapeDtypeStruct(slot, F32...  2.1 us
    ppermute x5, starting transfers between devices, group_swap(): return lax.ppermute(value, 'grp', [(g, g ^ step) for g in range(4)])  1.96 us
  transfers between devices with their start and end apart: 30, of which 17 were waited for; matrix products, arithmetic and copies ran while one was open for 0% of the time, Pallas kernels for 13%

profile of v2, /device:TPU:0, one launch (start us, length us, event | category | flops | bytes accessed | tf_op | source)
XLA Modules:
  0.0 85.1 jit_solution(8268098333219461513)
XLA Ops:
  1.1 3.0 %collective-permute-start = (bf16[448,256]{1,0:T(8,128)(2,1)S(1)}, bf16[448,256]{1,0:T(8,128)(2,1)S(1)}, u32[]{:S(2)}, u32[]{:S(2)}) collective-permute-start(bf16[448,256]{1,0:T(8,128)(2,1)S(1)} %pad_maximum_fusion.1.refs_0_.refs_2_), channel_id=1, source_target_pairs={{0,1},{1,0},{2,3},{3,2},{4,5},{5,4},{6,7},{7,6},{8,9},{9,8},{10,11... | collective-permute-start | bytes 688136 | tf_op jit(solution)/shard_map/ppermute | solution.py:25
  4.2 1.6 %collective-permute-start.1 = (bf16[448,256]{1,0:T(8,128)(2,1)S(1)}, bf16[448,256]{1,0:T(8,128)(2,1)S(1)}, u32[]{:S(2)}, u32[]{:S(2)}) collective-permute-start(bf16[448,256]{1,0:T(8,128)(2,1)S(1)} %pad_maximum_fusion.1.refs_0_.refs_2_), channel_id=1, source_target_pairs={{0,2},{1,3},{2,6},{3,7},{4,0},{5,1},{6,4},{7,5},{8,10},{9,11},{10,... | collective-permute-start | bytes 688136 | tf_op jit(solution)/shard_map/ppermute | solution.py:25
  6.3 2.6 %collective-permute-start.3 = (bf16[384,256]{1,0:T(8,128)(2,1)S(1)}, bf16[384,256]{1,0:T(8,128)(2,1)S(1)}, u32[]{:S(2)}, u32[]{:S(2)}) collective-permute-start(bf16[384,256]{1,0:T(8,128)(2,1)S(1)} %get-tuple-element.67.refs_1_), channel_id=1, source_target_pairs={{0,2},{1,3},{2,6},{3,7},{4,0},{5,1},{6,4},{7,5},{8,10},{9,11},{10,... | collective-permute-start | bytes 589832 | tf_op jit(solution)/shard_map/ppermute | solution.py:25
  11.9 1.7 %collective-permute-done.1.refs_4_ = bf16[448,256]{1,0:T(8,128)(2,1)S(1)} collective-permute-done((bf16[448,256]{1,0:T(8,128)(2,1)S(1)}, bf16[448,256]{1,0:T(8,128)(2,1)S(1)}, u32[]{:S(2)}, u32[]{:S(2)}) %collective-permute-start.1) | collective-permute-done | bytes 229408 | tf_op jit(solution)/shard_map/ppermute | solution.py:25
  14.9 2.3 %collective-permute-done.3.refs_5_ = bf16[384,256]{1,0:T(8,128)(2,1)S(1)} collective-permute-done((bf16[384,256]{1,0:T(8,128)(2,1)S(1)}, bf16[384,256]{1,0:T(8,128)(2,1)S(1)}, u32[]{:S(2)}, u32[]{:S(2)}) %collective-permute-start.3) | collective-permute-done | bytes 196640 | tf_op jit(solution)/shard_map/ppermute | solution.py:25
  17.5 2.3 %collective-permute-start.5 = (bf16[384,256]{1,0:T(8,128)(2,1)S(1)}, bf16[384,256]{1,0:T(8,128)(2,1)S(1)}, u32[]{:S(2)}, u32[]{:S(2)}) collective-permute-start(bf16[384,256]{1,0:T(8,128)(2,1)S(1)} %collective-permute-done.3.refs_5_), channel_id=1, source_target_pairs={{0,2},{1,3},{2,6},{3,7},{4,0},{5,1},{6,4},{7,5},{8,10},{9,11},{10,... | collective-permute-start | bytes 589832 | tf_op jit(solution)/shard_map/ppermute | solution.py:25
  19.8 1.9 %collective-permute-done.8.refs_6_.refs_5_ = bf16[448,256]{1,0:T(8,128)(2,1)S(1)} collective-permute-done((bf16[448,256]{1,0:T(8,128)(2,1)S(1)}, bf16[448,256]{1,0:T(8,128)(2,1)S(1)}, u32[]{:S(2)}, u32[]{:S(2)}) %collective-permute-start.8) | collective-permute-done | bytes 229408 | tf_op jit(solution)/shard_map/ppermute | solution.py:25
  23.2 1.5 %collective-permute-start.10 = (bf16[448,256]{1,0:T(8,128)(2,1)S(1)}, bf16[448,256]{1,0:T(8,128)(2,1)S(1)}, u32[]{:S(2)}, u32[]{:S(2)}) collective-permute-start(bf16[448,256]{1,0:T(8,128)(2,1)S(1)} %collective-permute-done.9.refs_8_.refs_6_), channel_id=1, source_target_pairs={{0,1},{1,0},{2,3},{3,2},{4,5},{5,4},{6,7},{7,6},{8,9},{9,8},{10,11... | collective-permute-start | bytes 688136 | tf_op jit(solution)/shard_map/ppermute | solution.py:25
  25.7 1.7 %collective-permute-done.5.refs_9_ = bf16[384,256]{1,0:T(8,128)(2,1)S(1)} collective-permute-done((bf16[384,256]{1,0:T(8,128)(2,1)S(1)}, bf16[384,256]{1,0:T(8,128)(2,1)S(1)}, u32[]{:S(2)}, u32[]{:S(2)}) %collective-permute-start.5) | collective-permute-done | bytes 196640 | tf_op jit(solution)/shard_map/ppermute | solution.py:25
  33.8 1.7 %collective-permute-done.6.refs_11_ = bf16[384,256]{1,0:T(8,128)(2,1)S(1)} collective-permute-done((bf16[384,256]{1,0:T(8,128)(2,1)S(1)}, bf16[384,256]{1,0:T(8,128)(2,1)S(1)}, u32[]{:S(2)}, u32[]{:S(2)}) %collective-permute-start.6) | collective-permute-done | bytes 196640 | tf_op jit(solution)/shard_map/ppermute | solution.py:25
  36.5 7.1 %shard_map.101 = (f32[768,256]{1,0:T(8,128)S(1)}, bf16[768,768]{1,0:T(8,128)(2,1)S(1)}) custom-call(s32[2]{0:T(128)S(1)} %pad_add_fusion.spot_ref.place_ref, s32[4]{0:T(128)S(1)} %copy-done.7, bf16[768,6144]{1,0:T(8,128)(2,1)} %bitcast.21, bf16[448,256]{1,0:T(8,128)(2,1)S(1)} %pad_maximum_fusion.1.refs_0_.refs_2_, ...), custom_call_target="tpu_custom_call" | custom-call | flops 2415919104 | bytes 9437184 | tf_op jit(solution)/shard_map/pallas_call | solution.py:99
  43.6 2.1 %shard_map.102 = (f32[8,16,256]{2,1,0:T(8,128)S(1)}, f32[8,16,256]{2,1,0:T(8,128)S(1)}, f32[8,16,256]{2,1,0:T(8,128)S(1)}, f32[8,16,256]{2,1,0:T(8,128)S(1)}, bf...) custom-call(s32[2]{0:T(128)S(1)} %pad_add_fusion.spot_ref.place_ref,, ...), custom_call_target="tpu_custom_call" | custom-call | flops 704643072 | bytes 2752512 | tf_op jit(solution)/shard_map/pallas_call | solution.py:150
  50.3 2.3 %collective-permute-start.17 = (bf16[8,16,256]{2,1,0:T(8,128)(2,1)S(1)}, bf16[8,16,256]{2,1,0:T(8,128)(2,1)S(1)}, u32[]{:S(2)}, u32[]{:S(2)}) collective-permute-start(bf16[8,16,256]{2,1,0:T(8,128)(2,1)S(1)} %add_convert_fusion.3), channel_id=1, source_target_pairs={{0,2},{1,3},{2,0},{3,1},{4,6},{5,7},{6,4},{7,5},{8,10},{9,11},{10,... | collective-permute-start | bytes 196616 | tf_op jit(solution)/shard_map/ppermute | solution.py:25
  52.6 2.6 %collective-permute-start.19 = (bf16[8,16,256]{2,1,0:T(8,128)(2,1)S(1)}, bf16[8,16,256]{2,1,0:T(8,128)(2,1)S(1)}, u32[]{:S(2)}, u32[]{:S(2)}) collective-permute-start(bf16[8,16,256]{2,1,0:T(8,128)(2,1)S(1)} %add_convert_fusion.2), channel_id=1, source_target_pairs={{0,4},{1,5},{2,6},{3,7},{4,0},{5,1},{6,2},{7,3},{8,12},{9,13},{10,... | collective-permute-start | bytes 196616 | tf_op jit(solution)/shard_map/ppermute | solution.py:25
  55.2 2.1 %collective-permute-start.21 = (bf16[8,16,256]{2,1,0:T(8,128)(2,1)S(1)}, bf16[8,16,256]{2,1,0:T(8,128)(2,1)S(1)}, u32[]{:S(2)}, u32[]{:S(2)}) collective-permute-start(bf16[8,16,256]{2,1,0:T(8,128)(2,1)S(1)} %add_convert_fusion.1), channel_id=1, source_target_pairs={{0,6},{1,7},{2,4},{3,5},{4,2},{5,3},{6,0},{7,1},{8,14},{9,15},{10,... | collective-permute-start | bytes 196616 | tf_op jit(solution)/shard_map/ppermute | solution.py:25
  59.8 1.6 %collective-permute-done.21 = bf16[8,16,256]{2,1,0:T(8,128)(2,1)S(1)} collective-permute-done((bf16[8,16,256]{2,1,0:T(8,128)(2,1)S(1)}, bf16[8,16,256]{2,1,0:T(8,128)(2,1)S(1)}, u32[]{:S(2)}, u32[]{:S(2)}) %collective-permute-start.21) | collective-permute-done | bytes 65568 | tf_op jit(solution)/shard_map/ppermute | solution.py:25
  61.6 1.6 %collective-permute-start.24 = (bf16[8,16,256]{2,1,0:T(8,128)(2,1)S(1)}, bf16[8,16,256]{2,1,0:T(8,128)(2,1)S(1)}, u32[]{:S(2)}, u32[]{:S(2)}) collective-permute-start(bf16[8,16,256]{2,1,0:T(8,128)(2,1)S(1)} %add_convert_fusion.refs_0_), channel_id=1, source_target_pairs={{0,16},{8,24},{16,0},{24,8},{1,17},{9,25},{17,1},{25,9},{2,18},{10... | collective-permute-start | bytes 196616 | tf_op jit(solution)/shard_map/ppermute | solution.py:41
  64.2 2.0 %collective-permute-done.24.refs_2_ = bf16[8,16,256]{2,1,0:T(8,128)(2,1)S(1)} collective-permute-done((bf16[8,16,256]{2,1,0:T(8,128)(2,1)S(1)}, bf16[8,16,256]{2,1,0:T(8,128)(2,1)S(1)}, u32[]{:S(2)}, u32[]{:S(2)}) %collective-permute-start.24) | collective-permute-done | bytes 65568 | tf_op jit(solution)/shard_map/ppermute | solution.py:41
  67.2 1.6 %shard_map.104 = bf16[32,16,256]{2,1,0:T(8,128)(2,1)} custom-call(s32[4,8]{1,0:T(4,128)S(1)} %copy-done.6, s32[2]{0:T(128)S(1)} %pad_add_fusion.spot_ref.place_ref, bf16[8,16,256]{2,1,0:T(8,128)(2,1)S(1)} %add_convert_fusion.refs_0_, bf16[8,16,256]{2,1,0:T(8,128)(2,1)S(1)} %collective-permute-done.23.refs_1_, ...), custom_call_target="tpu_custom_call" | custom-call | tf_op jit(solution)/shard_map/pallas_call | solution.py:191
  68.9 1.8 %collective-permute-start.27 = (bf16[4,64,256]{2,1,0:T(8,128)(2,1)S(1)}, bf16[4,64,256]{2,1,0:T(8,128)(2,1)S(1)}, u32[]{:S(2)}, u32[]{:S(2)}) collective-permute-start(bf16[4,64,256]{2,1,0:T(8,128)(2,1)S(1)} %pad_maximum_fusion.2), channel_id=1, source_target_pairs={{0,4},{1,5},{2,6},{3,7},{4,0},{5,1},{6,2},{7,3},{8,12},{9,13},{10,... | collective-permute-start | bytes 393224 | tf_op jit(solution)/shard_map/ppermute | solution.py:25
  70.7 3.4 %all-to-all-start = ((bf16[8,4,16,256]{3,2,1,0:T(8,128)(2,1)}), bf16[8,4,16,256]{3,2,1,0:T(8,128)(2,1)S(1)}, u32[]{:S(2)}, u32[]{:S(2)}) async-start(bf16[8,4,16,256]{3,2,1,0:T(8,128)(2,1)} %bitcast.9), calls=%async_computation | async-start | bytes 524288 | tf_op jit(solution)/shard_map/all_to_all | solution.py:349
  74.1 4.6 %collective-permute-done.27 = bf16[4,64,256]{2,1,0:T(8,128)(2,1)S(1)} collective-permute-done((bf16[4,64,256]{2,1,0:T(8,128)(2,1)S(1)}, bf16[4,64,256]{2,1,0:T(8,128)(2,1)S(1)}, u32[]{:S(2)}, u32[]{:S(2)}) %collective-permute-start.27) | collective-permute-done | bytes 131104 | tf_op jit(solution)/shard_map/ppermute | solution.py:25
  78.8 1.5 %collective-permute-done.28.other_ref = bf16[8,64,256]{2,1,0:T(8,128)(2,1)S(1)} collective-permute-done((bf16[8,64,256]{2,1,0:T(8,128)(2,1)S(1)}, bf16[8,64,256]{2,1,0:T(8,128)(2,1)S(1)}, u32[]{:S(2)}, u32[]{:S(2)}) %collective-permute-start.28) | collective-permute-done | bytes 262176 | tf_op jit(solution)/shard_map/ppermute | solution.py:41
  81.3 2.8 %all-to-all-done = bf16[8,4,16,256]{3,2,1,0:T(8,128)(2,1)S(1)} async-done(((bf16[8,4,16,256]{3,2,1,0:T(8,128)(2,1)}), bf16[8,4,16,256]{3,2,1,0:T(8,128)(2,1)S(1)}, u32[]{:S(2)}, u32[]{:S(2)}) %all-to-all-start) | async-done | bytes 262176 | tf_op jit(solution)/shard_map/all_to_all | solution.py:349
  (72 shorter events, 27.3 us)
Async XLA Ops:
  1.1 10.7 %collective-permute-start = (bf16[448,256]{1,0:T(8,128)(2,1)S(1)}, bf16[448,256]{1,0:T(8,128)(2,1)S(1)}, u32[]{:S(2)}, u32[]{:S(2)}) collective-permute-start(bf16[448,256]{1,0:T(8,128)(2,1)S(1)} %pad_maximum_fusion.1.refs_0_.refs_2_), channel_id=1, source_target_pairs={{0,1},{1,0},{2,3},{3,2},{4,5},{5,4},{6,7},{7,6},{8,9},{9,8},{10,11... | collective-permute-start | bytes 688136 | tf_op jit(solution)/shard_map/ppermute | solution.py:25
  4.2 9.4 %collective-permute-start.1 = (bf16[448,256]{1,0:T(8,128)(2,1)S(1)}, bf16[448,256]{1,0:T(8,128)(2,1)S(1)}, u32[]{:S(2)}, u32[]{:S(2)}) collective-permute-start(bf16[448,256]{1,0:T(8,128)(2,1)S(1)} %pad_maximum_fusion.1.refs_0_.refs_2_), channel_id=1, source_target_pairs={{0,2},{1,3},{2,6},{3,7},{4,0},{5,1},{6,4},{7,5},{8,10},{9,11},{10,... | collective-permute-start | bytes 688136 | tf_op jit(solution)/shard_map/ppermute | solution.py:25
  5.8 9.1 %collective-permute-start.2 = (bf16[384,256]{1,0:T(8,128)(2,1)S(1)}, bf16[384,256]{1,0:T(8,128)(2,1)S(1)}, u32[]{:S(2)}, u32[]{:S(2)}) collective-permute-start(bf16[384,256]{1,0:T(8,128)(2,1)S(1)} %get-tuple-element.67.refs_1_), channel_id=1, source_target_pairs={{0,1},{1,0},{2,3},{3,2},{4,5},{5,4},{6,7},{7,6},{8,9},{9,8},{10,11... | collective-permute-start | bytes 589832 | tf_op jit(solution)/shard_map/ppermute | solution.py:25
  6.3 11.0 %collective-permute-start.3 = (bf16[384,256]{1,0:T(8,128)(2,1)S(1)}, bf16[384,256]{1,0:T(8,128)(2,1)S(1)}, u32[]{:S(2)}, u32[]{:S(2)}) collective-permute-start(bf16[384,256]{1,0:T(8,128)(2,1)S(1)} %get-tuple-element.67.refs_1_), channel_id=1, source_target_pairs={{0,2},{1,3},{2,6},{3,7},{4,0},{5,1},{6,4},{7,5},{8,10},{9,11},{10,... | collective-permute-start | bytes 589832 | tf_op jit(solution)/shard_map/ppermute | solution.py:25
  13.6 8.1 %collective-permute-start.8 = (bf16[448,256]{1,0:T(8,128)(2,1)S(1)}, bf16[448,256]{1,0:T(8,128)(2,1)S(1)}, u32[]{:S(2)}, u32[]{:S(2)}) collective-permute-start(bf16[448,256]{1,0:T(8,128)(2,1)S(1)} %collective-permute-done.1.refs_4_), channel_id=1, source_target_pairs={{0,1},{1,0},{2,3},{3,2},{4,5},{5,4},{6,7},{7,6},{8,9},{9,8},{10,11... | collective-permute-start | bytes 688136 | tf_op jit(solution)/shard_map/ppermute | solution.py:25
  13.7 9.4 %collective-permute-start.9 = (bf16[448,256]{1,0:T(8,128)(2,1)S(1)}, bf16[448,256]{1,0:T(8,128)(2,1)S(1)}, u32[]{:S(2)}, u32[]{:S(2)}) collective-permute-start(bf16[448,256]{1,0:T(8,128)(2,1)S(1)} %collective-permute-done.1.refs_4_), channel_id=1, source_target_pairs={{0,2},{1,3},{2,6},{3,7},{4,0},{5,1},{6,4},{7,5},{8,10},{9,11},{10,... | collective-permute-start | bytes 688136 | tf_op jit(solution)/shard_map/ppermute | solution.py:25
  17.2 8.4 %collective-permute-start.4 = (bf16[384,256]{1,0:T(8,128)(2,1)S(1)}, bf16[384,256]{1,0:T(8,128)(2,1)S(1)}, u32[]{:S(2)}, u32[]{:S(2)}) collective-permute-start(bf16[384,256]{1,0:T(8,128)(2,1)S(1)} %collective-permute-done.3.refs_5_), channel_id=1, source_target_pairs={{0,1},{1,0},{2,3},{3,2},{4,5},{5,4},{6,7},{7,6},{8,9},{9,8},{10,11... | collective-permute-start | bytes 589832 | tf_op jit(solution)/shard_map/ppermute | solution.py:25
  17.5 9.9 %collective-permute-start.5 = (bf16[384,256]{1,0:T(8,128)(2,1)S(1)}, bf16[384,256]{1,0:T(8,128)(2,1)S(1)}, u32[]{:S(2)}, u32[]{:S(2)}) collective-permute-start(bf16[384,256]{1,0:T(8,128)(2,1)S(1)} %collective-permute-done.3.refs_5_), channel_id=1, source_target_pairs={{0,2},{1,3},{2,6},{3,7},{4,0},{5,1},{6,4},{7,5},{8,10},{9,11},{10,... | collective-permute-start | bytes 589832 | tf_op jit(solution)/shard_map/ppermute | solution.py:25
  23.2 8.1 %collective-permute-start.10 = (bf16[448,256]{1,0:T(8,128)(2,1)S(1)}, bf16[448,256]{1,0:T(8,128)(2,1)S(1)}, u32[]{:S(2)}, u32[]{:S(2)}) collective-permute-start(bf16[448,256]{1,0:T(8,128)(2,1)S(1)} %collective-permute-done.9.refs_8_.refs_6_), channel_id=1, source_target_pairs={{0,1},{1,0},{2,3},{3,2},{4,5},{5,4},{6,7},{7,6},{8,9},{9,8},{10,11... | collective-permute-start | bytes 688136 | tf_op jit(solution)/shard_map/ppermute | solution.py:25
  24.7 7.8 %collective-permute-start.11 = (bf16[448,256]{1,0:T(8,128)(2,1)S(1)}, bf16[448,256]{1,0:T(8,128)(2,1)S(1)}, u32[]{:S(2)}, u32[]{:S(2)}) collective-permute-start(bf16[448,256]{1,0:T(8,128)(2,1)S(1)} %collective-permute-done.9.refs_8_.refs_6_), channel_id=1, source_target_pairs={{0,2},{1,3},{2,6},{3,7},{4,0},{5,1},{6,4},{7,5},{8,10},{9,11},{10,... | collective-permute-start | bytes 688136 | tf_op jit(solution)/shard_map/ppermute | solution.py:25
  27.4 8.1 %collective-permute-start.6 = (bf16[384,256]{1,0:T(8,128)(2,1)S(1)}, bf16[384,256]{1,0:T(8,128)(2,1)S(1)}, u32[]{:S(2)}, u32[]{:S(2)}) collective-permute-start(bf16[384,256]{1,0:T(8,128)(2,1)S(1)} %collective-permute-done.5.refs_9_), channel_id=1, source_target_pairs={{0,1},{1,0},{2,3},{3,2},{4,5},{5,4},{6,7},{7,6},{8,9},{9,8},{10,11... | collective-permute-start | bytes 589832 | tf_op jit(solution)/shard_map/ppermute | solution.py:25
  28.8 6.8 %collective-permute-start.7 = (bf16[384,256]{1,0:T(8,128)(2,1)S(1)}, bf16[384,256]{1,0:T(8,128)(2,1)S(1)}, u32[]{:S(2)}, u32[]{:S(2)}) collective-permute-start(bf16[384,256]{1,0:T(8,128)(2,1)S(1)} %collective-permute-done.5.refs_9_), channel_id=1, source_target_pairs={{0,2},{1,3},{2,6},{3,7},{4,0},{5,1},{6,4},{7,5},{8,10},{9,11},{10,... | collective-permute-start | bytes 589832 | tf_op jit(solution)/shard_map/ppermute | solution.py:25
  32.5 11.1 %collective-permute-start.12 = (bf16[448,256]{1,0:T(8,128)(2,1)S(1)}, bf16[448,256]{1,0:T(8,128)(2,1)S(1)}, u32[]{:S(2)}, u32[]{:S(2)}) collective-permute-start(bf16[448,256]{1,0:T(8,128)(2,1)S(1)} %collective-permute-done.11.refs_12_.refs_8_), channel_id=1, source_target_pairs={{0,1},{1,0},{2,3},{3,2},{4,5},{5,4},{6,7},{7,6},{8,9},{9,8},{10,11... | collective-permute-start | bytes 688136 | tf_op jit(solution)/shard_map/ppermute | solution.py:25
  35.5 8.1 %collective-permute-start.13 = (bf16[384,256]{1,0:T(8,128)(2,1)S(1)}, bf16[384,256]{1,0:T(8,128)(2,1)S(1)}, u32[]{:S(2)}, u32[]{:S(2)}) collective-permute-start(bf16[384,256]{1,0:T(8,128)(2,1)S(1)} %collective-permute-done.7.refs_13_), channel_id=1, source_target_pairs={{0,1},{1,0},{2,3},{3,2},{4,5},{5,4},{6,7},{7,6},{8,9},{9,8},{10,11... | collective-permute-start | bytes 589832 | tf_op jit(solution)/shard_map/ppermute | solution.py:25
  46.9 10.5 %collective-permute-start.14 = (bf16[8,64,256]{2,1,0:T(8,128)(2,1)S(1)}, bf16[8,64,256]{2,1,0:T(8,128)(2,1)S(1)}, u32[]{:S(2)}, u32[]{:S(2)}) collective-permute-start(bf16[8,64,256]{2,1,0:T(8,128)(2,1)S(1)} %get-tuple-element.54.top_ref), channel_id=1, source_target_pairs={{0,8},{8,0},{16,24},{24,16},{1,9},{9,1},{17,25},{25,17},{2,10},{10... | collective-permute-start | bytes 786440 | tf_op jit(solution)/shard_map/ppermute | solution.py:41
  46.9 5.7 %collective-permute-start.18 = (bf16[8,16,256]{2,1,0:T(8,128)(2,1)S(1)}, bf16[8,16,256]{2,1,0:T(8,128)(2,1)S(1)}, u32[]{:S(2)}, u32[]{:S(2)}) collective-permute-start(bf16[8,16,256]{2,1,0:T(8,128)(2,1)S(1)} %get-tuple-element.60), channel_id=1, source_target_pairs={{0,1},{1,0},{2,3},{3,2},{4,5},{5,4},{6,7},{7,6},{8,9},{9,8},{10,11... | collective-permute-start | bytes 196616 | tf_op jit(solution)/shard_map/ppermute | solution.py:25
  47.9 7.3 %collective-permute-start.20 = (bf16[8,16,256]{2,1,0:T(8,128)(2,1)S(1)}, bf16[8,16,256]{2,1,0:T(8,128)(2,1)S(1)}, u32[]{:S(2)}, u32[]{:S(2)}) collective-permute-start(bf16[8,16,256]{2,1,0:T(8,128)(2,1)S(1)} %get-tuple-element.62), channel_id=1, source_target_pairs={{0,1},{1,0},{2,3},{3,2},{4,5},{5,4},{6,7},{7,6},{8,9},{9,8},{10,11... | collective-permute-start | bytes 196616 | tf_op jit(solution)/shard_map/ppermute | solution.py:25
  48.9 9.6 %collective-permute-start.15 = (bf16[8,16,256]{2,1,0:T(8,128)(2,1)S(1)}, bf16[8,16,256]{2,1,0:T(8,128)(2,1)S(1)}, u32[]{:S(2)}, u32[]{:S(2)}) collective-permute-start(bf16[8,16,256]{2,1,0:T(8,128)(2,1)S(1)} %get-tuple-element.56), channel_id=1, source_target_pairs={{0,1},{1,0},{2,3},{3,2},{4,5},{5,4},{6,7},{7,6},{8,9},{9,8},{10,11... | collective-permute-start | bytes 196616 | tf_op jit(solution)/shard_map/ppermute | solution.py:25
  50.3 8.2 %collective-permute-start.17 = (bf16[8,16,256]{2,1,0:T(8,128)(2,1)S(1)}, bf16[8,16,256]{2,1,0:T(8,128)(2,1)S(1)}, u32[]{:S(2)}, u32[]{:S(2)}) collective-permute-start(bf16[8,16,256]{2,1,0:T(8,128)(2,1)S(1)} %add_convert_fusion.3), channel_id=1, source_target_pairs={{0,2},{1,3},{2,0},{3,1},{4,6},{5,7},{6,4},{7,5},{8,10},{9,11},{10,... | collective-permute-start | bytes 196616 | tf_op jit(solution)/shard_map/ppermute | solution.py:25
  52.6 7.2 %collective-permute-start.19 = (bf16[8,16,256]{2,1,0:T(8,128)(2,1)S(1)}, bf16[8,16,256]{2,1,0:T(8,128)(2,1)S(1)}, u32[]{:S(2)}, u32[]{:S(2)}) collective-permute-start(bf16[8,16,256]{2,1,0:T(8,128)(2,1)S(1)} %add_convert_fusion.2), channel_id=1, source_target_pairs={{0,4},{1,5},{2,6},{3,7},{4,0},{5,1},{6,2},{7,3},{8,12},{9,13},{10,... | collective-permute-start | bytes 196616 | tf_op jit(solution)/shard_map/ppermute | solution.py:25
  55.2 6.2 %collective-permute-start.21 = (bf16[8,16,256]{2,1,0:T(8,128)(2,1)S(1)}, bf16[8,16,256]{2,1,0:T(8,128)(2,1)S(1)}, u32[]{:S(2)}, u32[]{:S(2)}) collective-permute-start(bf16[8,16,256]{2,1,0:T(8,128)(2,1)S(1)} %add_convert_fusion.1), channel_id=1, source_target_pairs={{0,6},{1,7},{2,4},{3,5},{4,2},{5,3},{6,0},{7,1},{8,14},{9,15},{10,... | collective-permute-start | bytes 196616 | tf_op jit(solution)/shard_map/ppermute | solution.py:25
  63.5 5.4 %collective-permute-start.26 = (bf16[2,64,256]{2,1,0:T(8,128)(2,1)S(1)}, bf16[2,64,256]{2,1,0:T(8,128)(2,1)S(1)}, u32[]{:S(2)}, u32[]{:S(2)}) collective-permute-start(bf16[2,64,256]{2,1,0:T(8,128)(2,1)S(1)} %pad_maximum_fusion.3), channel_id=1, source_target_pairs={{0,2},{1,3},{2,0},{3,1},{4,6},{5,7},{6,4},{7,5},{8,10},{9,11},{10,... | collective-permute-start | bytes 196616 | tf_op jit(solution)/shard_map/ppermute | solution.py:25
  68.9 9.8 %collective-permute-start.27 = (bf16[4,64,256]{2,1,0:T(8,128)(2,1)S(1)}, bf16[4,64,256]{2,1,0:T(8,128)(2,1)S(1)}, u32[]{:S(2)}, u32[]{:S(2)}) collective-permute-start(bf16[4,64,256]{2,1,0:T(8,128)(2,1)S(1)} %pad_maximum_fusion.2), channel_id=1, source_target_pairs={{0,4},{1,5},{2,6},{3,7},{4,0},{5,1},{6,2},{7,3},{8,12},{9,13},{10,... | collective-permute-start | bytes 393224 | tf_op jit(solution)/shard_map/ppermute | solution.py:25
  70.7 13.4 %all-to-all-start = ((bf16[8,4,16,256]{3,2,1,0:T(8,128)(2,1)}), bf16[8,4,16,256]{3,2,1,0:T(8,128)(2,1)S(1)}, u32[]{:S(2)}, u32[]{:S(2)}) async-start(bf16[8,4,16,256]{3,2,1,0:T(8,128)(2,1)} %bitcast.9), calls=%async_computation | async-start | bytes 524288 | tf_op jit(solution)/shard_map/all_to_all | solution.py:349
  (14 other events, 139.2 us)

commit v3 on v2

--- a/solution.py
+++ b/solution.py
@@ -9,7 +9,7 @@
 
 BLOCK = 128
 PARTS = 2
-NEXT = (1, 3, 0, 2)
+ORDER = (0, -1, 1, -2, 2, -3, 3, 4)
 LIMIT = 20 << 20
 F32 = jnp.float32
 BF16 = jnp.bfloat16
@@ -25,8 +25,19 @@
     return lax.ppermute(value, "row", [(s, t[0] * 2 + t[1]) for s, t in pairs])
 
 
-def cycle(value):
-    return row_permute(value, lambda z, y: (NEXT[z], y))
+def ring_place(row):
+    z, y = row // 2, row & 1
+    return z + y * (7 - 2 * z)
+
+
+def ring_row(place):
+    y = place >> 2
+    return (place + y * (7 - 2 * place)) * 2 + y
+
+
+def ring_send(value, step):
+    pairs = [(r, ring_row((ring_place(r) + step) & 7)) for r in range(8)]
+    return lax.ppermute(value, "row", pairs)
 
 
 def across(value):
@@ -39,10 +50,6 @@
 
 def group_swap(value, step):
     return lax.ppermute(value, "grp", [(g, g ^ step) for g in range(4)])
-
-
-def before(place):
-    return (place >> 1) | ((1 - (place & 1)) << 1)
 
 
 SMEM = pl.BlockSpec(memory_space=pltpu.SMEM)
@@ -50,12 +57,8 @@
 HBM = pl.BlockSpec(memory_space=pltpu.HBM)
 
 
-def source_rows(spot_ref, steps, crossed):
-    row = spot_ref[0]
-    spot = row // 2
-    for _ in range(steps):
-        spot = before(spot)
-    return spot * 2 + ((row & 1) ^ crossed)
+def source_row(spot_ref, offset):
+    return ring_row((ring_place(spot_ref[0]) + offset) & 7)
 
 
 def live_rows(piece, first, live):
@@ -63,57 +66,65 @@
     return jnp.where(ids < live - first, piece.astype(F32), 0.0).astype(BF16)
 
 
-def multiply_body(names, spot_ref, sizes_ref, inverse_ref, *refs):
-    pieces = refs[: len(names)]
-    total_ref, later_ref, left, right, sem = refs[len(names) :]
-    chunks, height, _ = left.shape
-    copies = [
-        pltpu.make_async_copy(inverse_ref.at[pl.ds(c * height, height)], left.at[c], sem.at[c])
-        for c in range(chunks)
-    ]
-    for copy in copies:
-        copy.start()
+def multiply_body(parts_in, depth, has_total, late, spot_ref, sizes_ref, inverse_ref, *refs):
+    refs = list(refs)
+    pieces = [refs.pop(0) for _ in parts_in]
+    before_ref = refs.pop(0) if has_total else None
+    total_ref = refs.pop(0)
+    later_ref = refs.pop(0) if late else None
+    left, right, sem = refs
+    share = depth * PARTS
+    offsets = [offset for offset, part in parts_in if part == 0]
+    copies, firsts = [], []
+    for i, offset in enumerate(offsets + [4] * late):
+        firsts.append(pl.multiple_of(source_row(spot_ref, offset) * share, share))
+        columns = inverse_ref.at[:, pl.ds(firsts[i], share)]
+        out = later_ref if i == len(offsets) else left.at[:, i * share : (i + 1) * share]
+        copies.append(pltpu.make_async_copy(columns, out, sem.at[i]))
+        copies[i].start()
     live = sizes_ref[spot_ref[1]]
-    width, cols = right.shape
-    share = later_ref.shape[1]
-    depth = share // PARTS
-    for (steps, crossed, part), piece in zip(names, pieces):
-        source = source_rows(spot_ref, steps, crossed)
-        first = pl.multiple_of((source * PARTS + part) * depth, depth)
-        right[pl.ds(first, depth)] = live_rows(piece[:depth], first, live)
-    late = pl.multiple_of(source_rows(spot_ref, 3, 1) * share, share)
-    right[pl.ds(late, share)] = jnp.zeros((share, cols), BF16)
-    for c in range(chunks):
-        copies[c].wait()
-        rows = pl.ds(c * height, height)
-        total_ref[rows] = jnp.dot(left[c], right[...], preferred_element_type=F32)
-        later_ref[rows] = left[c, :, pl.ds(late, share)]
-
-
-def multiply(spot, sizes, inverse, depth, named):
-    names = tuple(n[:3] for n in named)
-    pieces = [n[3] for n in named]
-    rows, width = inverse.shape
-    cols = pieces[0].shape[1]
-    chunks = 3
+    for (offset, part), piece in zip(parts_in, pieces):
+        i = offsets.index(offset)
+        start = i * share + part * depth
+        rows = live_rows(piece[:depth], firsts[i] + part * depth, live)
+        right[start : start + depth] = rows
+    total = before_ref[...] if has_total else None
+    for i in range(len(offsets)):
+        copies[i].wait()
+        place = slice(i * share, (i + 1) * share)
+        part = jnp.dot(left[:, place], right[place], preferred_element_type=F32)
+        total = part if total is None else total + part
+    total_ref[...] = total
+    if late:
+        copies[-1].wait()
+
+
+def multiply(spot, sizes, inverse, depth, named, total=None, late=False):
+    parts_in = tuple(n[:2] for n in named)
+    pieces = [n[2] for n in named]
+    extra = [] if total is None else [total]
+    rows, cols = inverse.shape[0], pieces[0].shape[1]
+    share = depth * PARTS
+    width = depth * len(named)
+    out_shape = [jax.ShapeDtypeStruct((rows, cols), F32)]
+    if late:
+        out_shape.append(jax.ShapeDtypeStruct((rows, share), BF16))
+    inverse = pltpu.with_memory_space_constraint(inverse, pltpu.HBM)
     return pl.pallas_call(
-        functools.partial(multiply_body, names),
-        out_shape=[
-            jax.ShapeDtypeStruct((rows, cols), F32),
-            jax.ShapeDtypeStruct((rows, depth * PARTS), BF16),
-        ],
-        in_specs=[SMEM, SMEM, HBM] + [VMEM] * len(pieces),
-        out_specs=[VMEM, VMEM],
+        functools.partial(multiply_body, parts_in, depth, bool(extra), late),
+        out_shape=out_shape,
+        in_specs=[SMEM, SMEM, HBM] + [VMEM] * (len(pieces) + len(extra)),
+        out_specs=[VMEM] * len(out_shape),
         scratch_shapes=[
-            pltpu.VMEM((chunks, rows // chunks, width), BF16),
+            pltpu.VMEM((rows, width), BF16),
             pltpu.VMEM((width, cols), BF16),
-            pltpu.SemaphoreType.DMA((chunks,)),
+            pltpu.SemaphoreType.DMA((width // share + late,)),
         ],
         compiler_params=params(),
         cost_estimate=pl.CostEstimate(
             flops=2 * rows * width * cols, bytes_accessed=2 * rows * width, transcendentals=0
         ),
-    )(spot, sizes, inverse, *pieces)
+    )(spot, sizes, inverse, *pieces, *extra)
 
 
 def contribute_body(spot_ref, sizes_ref, total_ref, later_ref, lower_ref, *refs):
@@ -123,7 +134,7 @@
     depth = later_ref.shape[1] // PARTS
     for k, carrier in enumerate((*carriers, pieces[0])):
         top_ref[k] = carrier[depth:]
-    first = source_rows(spot_ref, 3, 1) * PARTS * depth
+    first = source_row(spot_ref, 4) * PARTS * depth
     for part, piece in enumerate(pieces):
         place = part * depth
         right[place : place + depth] = live_rows(piece[:depth], first + place, live)
@@ -171,7 +182,7 @@
 def place_body(targets_ref, spot_ref, *refs):
     pieces, slots_ref, total_ref = refs[:4], refs[4], refs[5]
     total_ref[...] = jnp.zeros_like(total_ref)
-    blocks = total_ref.shape[0]
+    blocks = slots_ref.shape[0]
     slabs = pieces[0].shape[0]
     group = spot_ref[1]
     first = group * blocks
@@ -179,11 +190,10 @@
         for j in range(slabs):
             place = targets_ref[group ^ k, j] - first
 
-            @pl.when((place >= 0) & (place < blocks))
-            def _():
-                total_ref[place] += piece[j].astype(F32)
-
-    slots_ref[...] = total_ref[...].astype(BF16)
+            place = jnp.where((place >= 0) & (place < blocks), place, blocks)
+            total_ref[place] += piece[j].astype(F32)
+
+    slots_ref[...] = total_ref[:blocks].astype(BF16)
 
 
 def place(targets, spot, pieces, blocks):
@@ -194,12 +204,9 @@
         in_specs=[pl.BlockSpec(memory_space=pltpu.SMEM)] * 2
         + [pl.BlockSpec(memory_space=pltpu.VMEM)] * 4,
         out_specs=pl.BlockSpec(memory_space=pltpu.VMEM),
-        scratch_shapes=[pltpu.VMEM(shape, F32)],
+        scratch_shapes=[pltpu.VMEM((blocks + 1,) + shape[1:], F32)],
         compiler_params=params(),
     )(targets, spot, *pieces)
-
-
-ORDER = ((0, 0), (0, 1), (1, 0), (1, 1), (2, 0), (2, 1), (3, 0), (3, 1))
 
 
 def reorder_body(spot_ref, order_ref, inverse_ref, *out_refs):
@@ -211,8 +218,8 @@
     lower = jnp.where(cols < rows, mine, jnp.where(cols == rows, 1.0, 0.0)).astype(BF16)
     for side, out_ref in ((core, out_refs[0]), (1 - core, out_refs[1])):
         picks = []
-        for steps, crossed in ORDER:
-            first = (source_rows(spot_ref, steps, crossed) * 2 + side) * half
+        for offset in ORDER:
+            first = (source_row(spot_ref, offset) * 2 + side) * half
             ids = first + lax.broadcasted_iota(jnp.int32, (half, width), 0)
             picks.append((ids == order_ref[...]).astype(F32).astype(BF16))
         pick = jnp.concatenate(picks)
@@ -257,8 +264,8 @@
     row, core = place_ref[0], place_ref[1] & 1
     half = mine_ref.shape[1]
     for ref, side in ((mine_ref, core), (other_ref, 1 - core)):
-        for k in range(mine_ref.shape[0]):
-            first = pl.multiple_of(((row ^ k) * 2 + side) * half, half)
+        for k, apart in enumerate((0, 1, 4, 5, 2, 3, 6, 7)):
+            first = pl.multiple_of(((row ^ apart) * 2 + side) * half, half)
             factor_ref[pl.ds(first, half)] = ref[k]
     product = jnp.dot(lower_ref[...], factor_ref[...], preferred_element_type=F32)
     out_ref[...] = surface_ref[...] - product
@@ -301,28 +308,30 @@
     top = lax.dynamic_slice_in_dim(top_rows, core * half, half, 0)
     a, b = jnp.concatenate([upper[:depth], top]), upper[depth:]
 
-    ay, az, by, bz = across(a), cycle(a), across(b), cycle(b)
+    fold = functools.partial(multiply, spot, front_sizes, inverse, depth)
+    a_up, a_down, b_up, b_down = ring_send(a, 1), ring_send(a, -1), ring_send(b, 1), ring_send(b, -1)
     lower_mine, lower_other = reorder(spot, panel_order, panel_inverse)
-    ay, az, lower_mine = together((ay, az, lower_mine))
-    ay1, az1 = across(az), cycle(az)
-    by, bz = together((by, bz))
-    by1, bz1 = across(bz), cycle(bz)
-    ay1, az1 = together((ay1, az1))
-    ay2, az2 = across(az1), cycle(az1)
-    by1, bz1 = together((by1, bz1))
-    by2, bz2 = across(bz1), cycle(bz1)
-    ay2, az2 = together((ay2, az2))
-    ay3 = across(az2)
-    by2, bz2, ay = together((by2, bz2, ay))
-    by3 = across(bz2)
-    named = [(0, 0, 0, a), (0, 0, 1, b), (0, 1, 0, ay), (0, 1, 1, by)]
-    named += [(1, 0, 0, az), (1, 0, 1, bz), (1, 1, 0, ay1), (1, 1, 1, by1)]
-    named += [(2, 0, 0, az1), (2, 0, 1, bz1), (2, 1, 0, ay2), (2, 1, 1, by2)]
-    named += [(3, 0, 0, az2), (3, 0, 1, bz2)]
-    total, later = multiply(spot, front_sizes, inverse, depth, named)
-    carriers = (a, ay, az, ay1, az1, ay2, az2)
+    a_up, a_down, lower_mine = together((a_up, a_down, lower_mine))
+    a_up2, a_down2 = ring_send(a_up, 1), ring_send(a_down, -1)
+    b_up, b_down = together((b_up, b_down))
+    b_up2, b_down2 = ring_send(b_up, 1), ring_send(b_down, -1)
+    named = [(0, 0, a), (0, 1, b), (-1, 0, a_up), (-1, 1, b_up), (1, 0, a_down), (1, 1, b_down)]
+    (total,) = fold(named)
+    a_up2, a_down2, total = together((a_up2, a_down2, total))
+    a_up3, a_down3 = ring_send(a_up2, 1), ring_send(a_down2, -1)
+    b_up2, b_down2 = together((b_up2, b_down2))
+    b_up3, b_down3 = ring_send(b_up2, 1), ring_send(b_down2, -1)
+    named = [(-2, 0, a_up2), (-2, 1, b_up2), (2, 0, a_down2), (2, 1, b_down2)]
+    (total,) = fold(named, total)
+    a_up3, a_down3, total = together((a_up3, a_down3, total))
+    a4 = ring_send(a_up3, 1)
+    b_up3, b_down3 = together((b_up3, b_down3))
+    b4 = ring_send(b_down3, -1)
+    named = [(-3, 0, a_up3), (-3, 1, b_up3), (3, 0, a_down3), (3, 1, b_down3)]
+    total, later = fold(named, total, late=True)
+    carriers = (a, a_up, a_down, a_up2, a_down2, a_up3, a_down3)
     keep, send, top_mine = contribute(
-        spot, front_sizes, total, later, lower, (ay3, by3), carriers
+        spot, front_sizes, total, later, lower, (a4, b4), carriers
     )
 
     top_other = group_swap(top_mine, 1)
@@ -335,14 +344,14 @@
     mine = (sums[0] + sums[1] + sums[2] + sums[3]).astype(BF16)
     mine, factor_y = together((mine, factor_y))
     factor2 = jnp.stack([factor, factor_y])
-    factor2_in = along(factor2, 1)
+    factor2_in = along(factor2, 2)
     pieces = [mine] + [group_swap(mine, k) for k in (1, 2, 3)]
     local_blocks = surface.shape[0] // BLOCK
     blocks = local_blocks * row_count
     slots = place(border_blocks, spot, pieces, blocks)
     slots, factor2_in = together((slots, factor2_in))
     factor4 = jnp.concatenate([factor2, factor2_in])
-    factor_mine = jnp.concatenate([factor4, along(factor4, 2)])
+    factor_mine = jnp.concatenate([factor4, along(factor4, 1)])
     factor_other = group_swap(factor_mine, 1)
     base = panel_update(spot, surface, panel_lower, factor_mine, factor_other)
     slots = slots.reshape((row_count, local_blocks) + slots.shape[1:])

time: 85.4 us -> 81.4 us (0.953)
  waiting for transfers between devices: 28.9 us -> 22.5 us
  Pallas kernels: 13.4 us -> 16.9 us
  starting transfers between devices: 38.7 us -> 37.5 us
    ppermute x24 -> x10, starting transfers between devices: 33.3 us -> 14.7 us  [row_permute(): return lax.ppermute(value, 'row', [(s, t[0] * 2 + t[1]) for s, t in pairs])]
    ppermute x24 -> x10, waiting for transfers between devices: 21.5 us -> 4.74 us  [row_permute(): return lax.ppermute(value, 'row', [(s, t[0] * 2 + t[1]) for s, t in pairs])]
    ppermute x0 -> x14, starting transfers between devices: none -> 16 us  [ring_send(): return lax.ppermute(value, 'row', pairs)]
    ppermute x0 -> x14, waiting for transfers between devices: none -> 9.29 us  [ring_send(): return lax.ppermute(value, 'row', pairs)]
    pallas_call x1 -> x3, Pallas kernels: 7.11 us -> 10.8 us  [multiply(): pl.pallas_call(functools.partial(multiply_body, parts_in, depth, bool(ext...]
    all_to_all x1, waiting for transfers between devices: 2.81 us -> 5.22 us  [staged(): got = lax.all_to_all(slots, 'row', 0, 0, tiled=True)]
    all_to_all x1, starting transfers between devices: 3.41 us -> 4.79 us  [staged(): got = lax.all_to_all(slots, 'row', 0, 0, tiled=True)]
    ppermute x5, waiting for transfers between devices: 4.58 us -> 3.26 us  [group_swap(): return lax.ppermute(value, 'grp', [(g, g ^ step) for g in range(4)])]
  transfers between devices with their start and end apart: 30 -> 30, of which waited for: 17 -> 17; matrix products, arithmetic and copies ran while one was open for 0% -> 0% of each run, Pallas kernels for 13% -> 18%
where the time goes in v3:
time: 81.4 us; the launch traced here: 81.1 us
  starting transfers between devices  37.5 us (46%)
  waiting for transfers between devices  22.5 us (28%)
  Pallas kernels  16.9 us (21%)
  local copies, waits for them, and re-layouts  2.8 us (3%)
  other arithmetic  1.14 us (1%)
    ppermute x14, starting transfers between devices, ring_send(): return lax.ppermute(value, 'row', pairs)  16 us
    ppermute x10, starting transfers between devices, row_permute(): return lax.ppermute(value, 'row', [(s, t[0] * 2 + t[1]) for s, t in pairs])  14.7 us
    pallas_call x3, Pallas kernels, multiply(): pl.pallas_call(functools.partial(multiply_body, parts_in, depth, bool(ext...  10.8 us
    ppermute x14, waiting for transfers between devices, ring_send(): return lax.ppermute(value, 'row', pairs)  9.29 us
    all_to_all x1, waiting for transfers between devices, staged(): got = lax.all_to_all(slots, 'row', 0, 0, tiled=True)  5.22 us
    all_to_all x1, starting transfers between devices, staged(): got = lax.all_to_all(slots, 'row', 0, 0, tiled=True)  4.79 us
    ppermute x10, waiting for transfers between devices, row_permute(): return lax.ppermute(value, 'row', [(s, t[0] * 2 + t[1]) for s, t in pairs])  4.74 us
    ppermute x5, waiting for transfers between devices, group_swap(): return lax.ppermute(value, 'grp', [(g, g ^ step) for g in range(4)])  3.26 us
  transfers between devices with their start and end apart: 30, of which 17 were waited for; matrix products, arithmetic and copies ran while one was open for 0% of the time, Pallas kernels for 18%

profile of v3, /device:TPU:0, one launch (start us, length us, event | category | flops | bytes accessed | tf_op | source)
XLA Modules:
  0.0 81.1 jit_solution(3299977546487069978)
XLA Ops:
  1.1 3.1 %collective-permute-start = (bf16[448,256]{1,0:T(8,128)(2,1)S(1)}, bf16[448,256]{1,0:T(8,128)(2,1)S(1)}, u32[]{:S(2)}, u32[]{:S(2)}) collective-permute-start(bf16[448,256]{1,0:T(8,128)(2,1)S(1)} %pad_maximum_fusion.1.refs_0_.refs_2_), channel_id=1, source_target_pairs={{0,2},{1,0},{2,4},{3,1},{4,6},{5,3},{6,7},{7,5},{8,10},{9,8},{10,1... | collective-permute-start | bytes 688136 | tf_op jit(solution)/shard_map/ppermute | solution.py:40
  4.2 2.0 %collective-permute-start.4 = (bf16[384,256]{1,0:T(8,128)(2,1)S(1)}, bf16[384,256]{1,0:T(8,128)(2,1)S(1)}, u32[]{:S(2)}, u32[]{:S(2)}) collective-permute-start(bf16[384,256]{1,0:T(8,128)(2,1)S(1)} %get-tuple-element.69.refs_1_), channel_id=1, source_target_pairs={{0,2},{1,0},{2,4},{3,1},{4,6},{5,3},{6,7},{7,5},{8,10},{9,8},{10,1... | collective-permute-start | bytes 589832 | tf_op jit(solution)/shard_map/ppermute | solution.py:40
  8.0 1.3 %shard_map.100 = (bf16[64,512]{1,0:T(8,128)(2,1)S(1)}, bf16[64,512]{1,0:T(8,128)(2,1)S(1)}) custom-call(s32[2]{0:T(128)S(1)} %pad_add_fusion.spot_ref.place_ref, s32[1,1024]{1,0:T(1,128)S(1)} %bitcast.20, bf16[128,1024]{1,0:T(8,128)(2,1)S(1)} %copy-done.4), custom_call_target="tpu_custom_call" | custom-call | tf_op jit(solution)/shard_map/pallas_call | solution.py:234
  10.6 2.2 %collective-permute-done.1.refs_4_ = bf16[448,256]{1,0:T(8,128)(2,1)S(1)} collective-permute-done((bf16[448,256]{1,0:T(8,128)(2,1)S(1)}, bf16[448,256]{1,0:T(8,128)(2,1)S(1)}, u32[]{:S(2)}, u32[]{:S(2)}) %collective-permute-start.1) | collective-permute-done | bytes 229408 | tf_op jit(solution)/shard_map/ppermute | solution.py:40
  12.8 1.6 %collective-permute-start.2 = (bf16[448,256]{1,0:T(8,128)(2,1)S(1)}, bf16[448,256]{1,0:T(8,128)(2,1)S(1)}, u32[]{:S(2)}, u32[]{:S(2)}) collective-permute-start(bf16[448,256]{1,0:T(8,128)(2,1)S(1)} %collective-permute-done.refs_2_.refs_3_), channel_id=1, source_target_pairs={{0,2},{1,0},{2,4},{3,1},{4,6},{5,3},{6,7},{7,5},{8,10},{9,8},{10,1... | collective-permute-start | bytes 688136 | tf_op jit(solution)/shard_map/ppermute | solution.py:40
  14.8 2.2 %collective-permute-done.5.refs_5_ = bf16[384,256]{1,0:T(8,128)(2,1)S(1)} collective-permute-done((bf16[384,256]{1,0:T(8,128)(2,1)S(1)}, bf16[384,256]{1,0:T(8,128)(2,1)S(1)}, u32[]{:S(2)}, u32[]{:S(2)}) %collective-permute-start.5) | collective-permute-done | bytes 196640 | tf_op jit(solution)/shard_map/ppermute | solution.py:40
  17.0 1.6 %collective-permute-start.8 = (bf16[384,256]{1,0:T(8,128)(2,1)S(1)}, bf16[384,256]{1,0:T(8,128)(2,1)S(1)}, u32[]{:S(2)}, u32[]{:S(2)}) collective-permute-start(bf16[384,256]{1,0:T(8,128)(2,1)S(1)} %collective-permute-done.4.refs_3_), channel_id=1, source_target_pairs={{0,2},{1,0},{2,4},{3,1},{4,6},{5,3},{6,7},{7,5},{8,10},{9,8},{10,1... | collective-permute-start | bytes 589832 | tf_op jit(solution)/shard_map/ppermute | solution.py:40
  19.0 4.0 %shard_map.101.refs_4_ = f32[768,256]{1,0:T(8,128)S(1)} custom-call(s32[2]{0:T(128)S(1)} %pad_add_fusion.spot_ref.place_ref, s32[4]{0:T(128)S(1)} %copy-done.5, bf16[768,6144]{1,0:T(8,128)(2,1)} %bitcast.21, bf16[448,256]{1,0:T(8,128)(2,1)S(1)} %pad_maximum_fusion.1.refs_0_.refs_2_, bf16[384,256]{1,0:T(8,128)(2,1)S(1)} %get-tuple-element.69.refs_1_, ...), custom_call_target="tpu_custom_call" | custom-call | flops 905969664 | bytes 3538944 | tf_op jit(solution)/shard_map/pallas_call | solution.py:113
  23.1 1.6 %collective-permute-start.6 = (bf16[448,256]{1,0:T(8,128)(2,1)S(1)}, bf16[448,256]{1,0:T(8,128)(2,1)S(1)}, u32[]{:S(2)}, u32[]{:S(2)}) collective-permute-start(bf16[448,256]{1,0:T(8,128)(2,1)S(1)} %collective-permute-done.2.refs_0_.refs_5_), channel_id=1, source_target_pairs={{0,2},{1,0},{2,4},{3,1},{4,6},{5,3},{6,7},{7,5},{8,10},{9,8},{10,1... | collective-permute-start | bytes 688136 | tf_op jit(solution)/shard_map/ppermute | solution.py:40
  25.6 1.6 %collective-permute-start.10 = (bf16[384,256]{1,0:T(8,128)(2,1)S(1)}, bf16[384,256]{1,0:T(8,128)(2,1)S(1)}, u32[]{:S(2)}, u32[]{:S(2)}) collective-permute-start(bf16[384,256]{1,0:T(8,128)(2,1)S(1)} %collective-permute-done.8.refs_1_), channel_id=1, source_target_pairs={{0,2},{1,0},{2,4},{3,1},{4,6},{5,3},{6,7},{7,5},{8,10},{9,8},{10,1... | collective-permute-start | bytes 589832 | tf_op jit(solution)/shard_map/ppermute | solution.py:40
  27.6 3.4 %shard_map.102.refs_4_ = f32[768,256]{1,0:T(8,128)S(1)} custom-call(s32[2]{0:T(128)S(1)} %pad_add_fusion.spot_ref.place_ref, s32[4]{0:T(128)S(1)} %copy-done.5, bf16[768,6144]{1,0:T(8,128)(2,1)} %bitcast.22, bf16[448,256]{1,0:T(8,128)(2,1)S(1)} %collective-permute-done.2.refs_0_.refs_5_, bf16[384,256]{1,0:T(8,128)(2,1)S(1)} %collective-permute-done.8.refs_1_, ...), custom_call_target="tpu_custom_call" | custom-call | flops 603979776 | bytes 2359296 | tf_op jit(solution)/shard_map/pallas_call | solution.py:113
  31.7 1.6 %collective-permute-start.12 = (bf16[448,256]{1,0:T(8,128)(2,1)S(1)}, bf16[448,256]{1,0:T(8,128)(2,1)S(1)}, u32[]{:S(2)}, u32[]{:S(2)}) collective-permute-start(bf16[448,256]{1,0:T(8,128)(2,1)S(1)} %collective-permute-done.6.refs_0_.refs_7_), channel_id=1, source_target_pairs={{0,2},{1,0},{2,4},{3,1},{4,6},{5,3},{6,7},{7,5},{8,10},{9,8},{10,1... | collective-permute-start | bytes 688136 | tf_op jit(solution)/shard_map/ppermute | solution.py:40
  35.9 3.4 %shard_map.103 = (f32[768,256]{1,0:T(8,128)S(1)}, bf16[768,768]{1,0:T(8,128)(2,1)S(1)}) custom-call(s32[2]{0:T(128)S(1)} %pad_add_fusion.spot_ref.place_ref, s32[4]{0:T(128)S(1)} %copy-done.5, bf16[768,6144]{1,0:T(8,128)(2,1)} %bitcast.23, bf16[448,256]{1,0:T(8,128)(2,1)S(1)} %collective-permute-done.6.refs_0_.refs_7_, ...), custom_call_target="tpu_custom_call" | custom-call | flops 603979776 | bytes 2359296 | tf_op jit(solution)/shard_map/pallas_call | solution.py:113
  40.3 2.1 %shard_map.104 = (f32[8,16,256]{2,1,0:T(8,128)S(1)}, f32[8,16,256]{2,1,0:T(8,128)S(1)}, f32[8,16,256]{2,1,0:T(8,128)S(1)}, f32[8,16,256]{2,1,0:T(8,128)S(1)}, bf...) custom-call(s32[2]{0:T(128)S(1)} %pad_add_fusion.spot_ref.place_ref,, ...), custom_call_target="tpu_custom_call" | custom-call | flops 704643072 | bytes 2752512 | tf_op jit(solution)/shard_map/pallas_call | solution.py:161
  46.8 1.9 %collective-permute-start.17 = (bf16[8,16,256]{2,1,0:T(8,128)(2,1)S(1)}, bf16[8,16,256]{2,1,0:T(8,128)(2,1)S(1)}, u32[]{:S(2)}, u32[]{:S(2)}) collective-permute-start(bf16[8,16,256]{2,1,0:T(8,128)(2,1)S(1)} %add_convert_fusion.3), channel_id=1, source_target_pairs={{0,2},{1,3},{2,0},{3,1},{4,6},{5,7},{6,4},{7,5},{8,10},{9,11},{10,... | collective-permute-start | bytes 196616 | tf_op jit(solution)/shard_map/ppermute | solution.py:25
  48.7 3.0 %collective-permute-start.19 = (bf16[8,16,256]{2,1,0:T(8,128)(2,1)S(1)}, bf16[8,16,256]{2,1,0:T(8,128)(2,1)S(1)}, u32[]{:S(2)}, u32[]{:S(2)}) collective-permute-start(bf16[8,16,256]{2,1,0:T(8,128)(2,1)S(1)} %add_convert_fusion.2), channel_id=1, source_target_pairs={{0,4},{1,5},{2,6},{3,7},{4,0},{5,1},{6,2},{7,3},{8,12},{9,13},{10,... | collective-permute-start | bytes 196616 | tf_op jit(solution)/shard_map/ppermute | solution.py:25
  51.7 2.4 %collective-permute-start.21 = (bf16[8,16,256]{2,1,0:T(8,128)(2,1)S(1)}, bf16[8,16,256]{2,1,0:T(8,128)(2,1)S(1)}, u32[]{:S(2)}, u32[]{:S(2)}) collective-permute-start(bf16[8,16,256]{2,1,0:T(8,128)(2,1)S(1)} %add_convert_fusion.1), channel_id=1, source_target_pairs={{0,6},{1,7},{2,4},{3,5},{4,2},{5,3},{6,0},{7,1},{8,14},{9,15},{10,... | collective-permute-start | bytes 196616 | tf_op jit(solution)/shard_map/ppermute | solution.py:25
  55.6 2.3 %collective-permute-done.21 = bf16[8,16,256]{2,1,0:T(8,128)(2,1)S(1)} collective-permute-done((bf16[8,16,256]{2,1,0:T(8,128)(2,1)S(1)}, bf16[8,16,256]{2,1,0:T(8,128)(2,1)S(1)}, u32[]{:S(2)}, u32[]{:S(2)}) %collective-permute-start.21) | collective-permute-done | bytes 65568 | tf_op jit(solution)/shard_map/ppermute | solution.py:25
  58.3 1.5 %collective-permute-start.24 = (bf16[8,16,256]{2,1,0:T(8,128)(2,1)S(1)}, bf16[8,16,256]{2,1,0:T(8,128)(2,1)S(1)}, u32[]{:S(2)}, u32[]{:S(2)}) collective-permute-start(bf16[8,16,256]{2,1,0:T(8,128)(2,1)S(1)} %add_convert_fusion.refs_0_), channel_id=1, source_target_pairs={{0,16},{8,24},{16,0},{24,8},{1,17},{9,25},{17,1},{25,9},{2,18},{10... | collective-permute-start | bytes 196616 | tf_op jit(solution)/shard_map/ppermute | solution.py:52
  60.2 2.0 %collective-permute-start.26 = (bf16[2,64,256]{2,1,0:T(8,128)(2,1)S(1)}, bf16[2,64,256]{2,1,0:T(8,128)(2,1)S(1)}, u32[]{:S(2)}, u32[]{:S(2)}) collective-permute-start(bf16[2,64,256]{2,1,0:T(8,128)(2,1)S(1)} %pad_maximum_fusion.3), channel_id=1, source_target_pairs={{0,4},{1,5},{2,6},{3,7},{4,0},{5,1},{6,2},{7,3},{8,12},{9,13},{10,... | collective-permute-start | bytes 196616 | tf_op jit(solution)/shard_map/ppermute | solution.py:25
  63.9 1.5 %shard_map.106 = bf16[32,16,256]{2,1,0:T(8,128)(2,1)} custom-call(s32[4,8]{1,0:T(4,128)S(1)} %copy-done.7, s32[2]{0:T(128)S(1)} %pad_add_fusion.spot_ref.place_ref, bf16[8,16,256]{2,1,0:T(8,128)(2,1)S(1)} %add_convert_fusion.refs_0_, bf16[8,16,256]{2,1,0:T(8,128)(2,1)S(1)} %collective-permute-done.23.refs_1_, ...), custom_call_target="tpu_custom_call" | custom-call | tf_op jit(solution)/shard_map/pallas_call | solution.py:201
  66.8 4.8 %all-to-all-start = ((bf16[8,4,16,256]{3,2,1,0:T(8,128)(2,1)}), bf16[8,4,16,256]{3,2,1,0:T(8,128)(2,1)S(1)}, u32[]{:S(2)}, u32[]{:S(2)}) async-start(bf16[8,4,16,256]{3,2,1,0:T(8,128)(2,1)} %bitcast.9), calls=%async_computation | async-start | bytes 524288 | tf_op jit(solution)/shard_map/all_to_all | solution.py:358
  72.3 1.5 %collective-permute-done.28.other_ref = bf16[8,64,256]{2,1,0:T(8,128)(2,1)S(1)} collective-permute-done((bf16[8,64,256]{2,1,0:T(8,128)(2,1)S(1)}, bf16[8,64,256]{2,1,0:T(8,128)(2,1)S(1)}, u32[]{:S(2)}, u32[]{:S(2)}) %collective-permute-start.28) | collective-permute-done | bytes 262176 | tf_op jit(solution)/shard_map/ppermute | solution.py:52
  74.9 5.2 %all-to-all-done = bf16[8,4,16,256]{3,2,1,0:T(8,128)(2,1)S(1)} async-done(((bf16[8,4,16,256]{3,2,1,0:T(8,128)(2,1)}), bf16[8,4,16,256]{3,2,1,0:T(8,128)(2,1)S(1)}, u32[]{:S(2)}, u32[]{:S(2)}) %all-to-all-start) | async-done | bytes 262176 | tf_op jit(solution)/shard_map/all_to_all | solution.py:358
  (74 shorter events, 23.2 us)
Async XLA Ops:
  1.1 9.5 %collective-permute-start = (bf16[448,256]{1,0:T(8,128)(2,1)S(1)}, bf16[448,256]{1,0:T(8,128)(2,1)S(1)}, u32[]{:S(2)}, u32[]{:S(2)}) collective-permute-start(bf16[448,256]{1,0:T(8,128)(2,1)S(1)} %pad_maximum_fusion.1.refs_0_.refs_2_), channel_id=1, source_target_pairs={{0,2},{1,0},{2,4},{3,1},{4,6},{5,3},{6,7},{7,5},{8,10},{9,8},{10,1... | collective-permute-start | bytes 688136 | tf_op jit(solution)/shard_map/ppermute | solution.py:40
  4.2 8.5 %collective-permute-start.1 = (bf16[448,256]{1,0:T(8,128)(2,1)S(1)}, bf16[448,256]{1,0:T(8,128)(2,1)S(1)}, u32[]{:S(2)}, u32[]{:S(2)}) collective-permute-start(bf16[448,256]{1,0:T(8,128)(2,1)S(1)} %pad_maximum_fusion.1.refs_0_.refs_2_), channel_id=1, source_target_pairs={{0,1},{1,3},{2,0},{3,5},{4,2},{5,7},{6,4},{7,6},{8,9},{9,11},{10,8... | collective-permute-start | bytes 688136 | tf_op jit(solution)/shard_map/ppermute | solution.py:40
  4.2 10.6 %collective-permute-start.4 = (bf16[384,256]{1,0:T(8,128)(2,1)S(1)}, bf16[384,256]{1,0:T(8,128)(2,1)S(1)}, u32[]{:S(2)}, u32[]{:S(2)}) collective-permute-start(bf16[384,256]{1,0:T(8,128)(2,1)S(1)} %get-tuple-element.69.refs_1_), channel_id=1, source_target_pairs={{0,2},{1,0},{2,4},{3,1},{4,6},{5,3},{6,7},{7,5},{8,10},{9,8},{10,1... | collective-permute-start | bytes 589832 | tf_op jit(solution)/shard_map/ppermute | solution.py:40
  6.2 10.7 %collective-permute-start.5 = (bf16[384,256]{1,0:T(8,128)(2,1)S(1)}, bf16[384,256]{1,0:T(8,128)(2,1)S(1)}, u32[]{:S(2)}, u32[]{:S(2)}) collective-permute-start(bf16[384,256]{1,0:T(8,128)(2,1)S(1)} %get-tuple-element.69.refs_1_), channel_id=1, source_target_pairs={{0,1},{1,3},{2,0},{3,5},{4,2},{5,7},{6,4},{7,6},{8,9},{9,11},{10,8... | collective-permute-start | bytes 589832 | tf_op jit(solution)/shard_map/ppermute | solution.py:40
  12.8 10.3 %collective-permute-start.2 = (bf16[448,256]{1,0:T(8,128)(2,1)S(1)}, bf16[448,256]{1,0:T(8,128)(2,1)S(1)}, u32[]{:S(2)}, u32[]{:S(2)}) collective-permute-start(bf16[448,256]{1,0:T(8,128)(2,1)S(1)} %collective-permute-done.refs_2_.refs_3_), channel_id=1, source_target_pairs={{0,2},{1,0},{2,4},{3,1},{4,6},{5,3},{6,7},{7,5},{8,10},{9,8},{10,1... | collective-permute-start | bytes 688136 | tf_op jit(solution)/shard_map/ppermute | solution.py:40
  14.3 8.7 %collective-permute-start.3 = (bf16[448,256]{1,0:T(8,128)(2,1)S(1)}, bf16[448,256]{1,0:T(8,128)(2,1)S(1)}, u32[]{:S(2)}, u32[]{:S(2)}) collective-permute-start(bf16[448,256]{1,0:T(8,128)(2,1)S(1)} %collective-permute-done.1.refs_4_), channel_id=1, source_target_pairs={{0,1},{1,3},{2,0},{3,5},{4,2},{5,7},{6,4},{7,6},{8,9},{9,11},{10,8... | collective-permute-start | bytes 688136 | tf_op jit(solution)/shard_map/ppermute | solution.py:40
  17.0 8.2 %collective-permute-start.8 = (bf16[384,256]{1,0:T(8,128)(2,1)S(1)}, bf16[384,256]{1,0:T(8,128)(2,1)S(1)}, u32[]{:S(2)}, u32[]{:S(2)}) collective-permute-start(bf16[384,256]{1,0:T(8,128)(2,1)S(1)} %collective-permute-done.4.refs_3_), channel_id=1, source_target_pairs={{0,2},{1,0},{2,4},{3,1},{4,6},{5,3},{6,7},{7,5},{8,10},{9,8},{10,1... | collective-permute-start | bytes 589832 | tf_op jit(solution)/shard_map/ppermute | solution.py:40
  18.5 7.0 %collective-permute-start.9 = (bf16[384,256]{1,0:T(8,128)(2,1)S(1)}, bf16[384,256]{1,0:T(8,128)(2,1)S(1)}, u32[]{:S(2)}, u32[]{:S(2)}) collective-permute-start(bf16[384,256]{1,0:T(8,128)(2,1)S(1)} %collective-permute-done.5.refs_5_), channel_id=1, source_target_pairs={{0,1},{1,3},{2,0},{3,5},{4,2},{5,7},{6,4},{7,6},{8,9},{9,11},{10,8... | collective-permute-start | bytes 589832 | tf_op jit(solution)/shard_map/ppermute | solution.py:40
  23.1 7.9 %collective-permute-start.6 = (bf16[448,256]{1,0:T(8,128)(2,1)S(1)}, bf16[448,256]{1,0:T(8,128)(2,1)S(1)}, u32[]{:S(2)}, u32[]{:S(2)}) collective-permute-start(bf16[448,256]{1,0:T(8,128)(2,1)S(1)} %collective-permute-done.2.refs_0_.refs_5_), channel_id=1, source_target_pairs={{0,2},{1,0},{2,4},{3,1},{4,6},{5,3},{6,7},{7,5},{8,10},{9,8},{10,1... | collective-permute-start | bytes 688136 | tf_op jit(solution)/shard_map/ppermute | solution.py:40
  24.7 7.0 %collective-permute-start.7 = (bf16[448,256]{1,0:T(8,128)(2,1)S(1)}, bf16[448,256]{1,0:T(8,128)(2,1)S(1)}, u32[]{:S(2)}, u32[]{:S(2)}) collective-permute-start(bf16[448,256]{1,0:T(8,128)(2,1)S(1)} %collective-permute-done.3.refs_2_.refs_6_), channel_id=1, source_target_pairs={{0,1},{1,3},{2,0},{3,5},{4,2},{5,7},{6,4},{7,6},{8,9},{9,11},{10,8... | collective-permute-start | bytes 688136 | tf_op jit(solution)/shard_map/ppermute | solution.py:40
  25.6 9.0 %collective-permute-start.10 = (bf16[384,256]{1,0:T(8,128)(2,1)S(1)}, bf16[384,256]{1,0:T(8,128)(2,1)S(1)}, u32[]{:S(2)}, u32[]{:S(2)}) collective-permute-start(bf16[384,256]{1,0:T(8,128)(2,1)S(1)} %collective-permute-done.8.refs_1_), channel_id=1, source_target_pairs={{0,2},{1,0},{2,4},{3,1},{4,6},{5,3},{6,7},{7,5},{8,10},{9,8},{10,1... | collective-permute-start | bytes 589832 | tf_op jit(solution)/shard_map/ppermute | solution.py:40
  27.1 7.5 %collective-permute-start.11 = (bf16[384,256]{1,0:T(8,128)(2,1)S(1)}, bf16[384,256]{1,0:T(8,128)(2,1)S(1)}, u32[]{:S(2)}, u32[]{:S(2)}) collective-permute-start(bf16[384,256]{1,0:T(8,128)(2,1)S(1)} %collective-permute-done.9.refs_3_), channel_id=1, source_target_pairs={{0,1},{1,3},{2,0},{3,5},{4,2},{5,7},{6,4},{7,6},{8,9},{9,11},{10,8... | collective-permute-start | bytes 589832 | tf_op jit(solution)/shard_map/ppermute | solution.py:40
  31.7 8.7 %collective-permute-start.12 = (bf16[448,256]{1,0:T(8,128)(2,1)S(1)}, bf16[448,256]{1,0:T(8,128)(2,1)S(1)}, u32[]{:S(2)}, u32[]{:S(2)}) collective-permute-start(bf16[448,256]{1,0:T(8,128)(2,1)S(1)} %collective-permute-done.6.refs_0_.refs_7_), channel_id=1, source_target_pairs={{0,2},{1,0},{2,4},{3,1},{4,6},{5,3},{6,7},{7,5},{8,10},{9,8},{10,1... | collective-permute-start | bytes 688136 | tf_op jit(solution)/shard_map/ppermute | solution.py:40
  34.7 5.7 %collective-permute-start.13 = (bf16[384,256]{1,0:T(8,128)(2,1)S(1)}, bf16[384,256]{1,0:T(8,128)(2,1)S(1)}, u32[]{:S(2)}, u32[]{:S(2)}) collective-permute-start(bf16[384,256]{1,0:T(8,128)(2,1)S(1)} %collective-permute-done.11.refs_3_), channel_id=1, source_target_pairs={{0,1},{1,3},{2,0},{3,5},{4,2},{5,7},{6,4},{7,6},{8,9},{9,11},{10,8... | collective-permute-start | bytes 589832 | tf_op jit(solution)/shard_map/ppermute | solution.py:40
  43.7 10.4 %collective-permute-start.14 = (bf16[8,64,256]{2,1,0:T(8,128)(2,1)S(1)}, bf16[8,64,256]{2,1,0:T(8,128)(2,1)S(1)}, u32[]{:S(2)}, u32[]{:S(2)}) collective-permute-start(bf16[8,64,256]{2,1,0:T(8,128)(2,1)S(1)} %get-tuple-element.56.top_ref), channel_id=1, source_target_pairs={{0,8},{8,0},{16,24},{24,16},{1,9},{9,1},{17,25},{25,17},{2,10},{10... | collective-permute-start | bytes 786440 | tf_op jit(solution)/shard_map/ppermute | solution.py:52
  43.7 5.0 %collective-permute-start.18 = (bf16[8,16,256]{2,1,0:T(8,128)(2,1)S(1)}, bf16[8,16,256]{2,1,0:T(8,128)(2,1)S(1)}, u32[]{:S(2)}, u32[]{:S(2)}) collective-permute-start(bf16[8,16,256]{2,1,0:T(8,128)(2,1)S(1)} %get-tuple-element.62), channel_id=1, source_target_pairs={{0,1},{1,0},{2,3},{3,2},{4,5},{5,4},{6,7},{7,6},{8,9},{9,8},{10,11... | collective-permute-start | bytes 196616 | tf_op jit(solution)/shard_map/ppermute | solution.py:25
  44.5 7.1 %collective-permute-start.20 = (bf16[8,16,256]{2,1,0:T(8,128)(2,1)S(1)}, bf16[8,16,256]{2,1,0:T(8,128)(2,1)S(1)}, u32[]{:S(2)}, u32[]{:S(2)}) collective-permute-start(bf16[8,16,256]{2,1,0:T(8,128)(2,1)S(1)} %get-tuple-element.64), channel_id=1, source_target_pairs={{0,1},{1,0},{2,3},{3,2},{4,5},{5,4},{6,7},{7,6},{8,9},{9,8},{10,11... | collective-permute-start | bytes 196616 | tf_op jit(solution)/shard_map/ppermute | solution.py:25
  45.7 9.9 %collective-permute-start.15 = (bf16[8,16,256]{2,1,0:T(8,128)(2,1)S(1)}, bf16[8,16,256]{2,1,0:T(8,128)(2,1)S(1)}, u32[]{:S(2)}, u32[]{:S(2)}) collective-permute-start(bf16[8,16,256]{2,1,0:T(8,128)(2,1)S(1)} %get-tuple-element.58), channel_id=1, source_target_pairs={{0,1},{1,0},{2,3},{3,2},{4,5},{5,4},{6,7},{7,6},{8,9},{9,8},{10,11... | collective-permute-start | bytes 196616 | tf_op jit(solution)/shard_map/ppermute | solution.py:25
  46.8 8.8 %collective-permute-start.17 = (bf16[8,16,256]{2,1,0:T(8,128)(2,1)S(1)}, bf16[8,16,256]{2,1,0:T(8,128)(2,1)S(1)}, u32[]{:S(2)}, u32[]{:S(2)}) collective-permute-start(bf16[8,16,256]{2,1,0:T(8,128)(2,1)S(1)} %add_convert_fusion.3), channel_id=1, source_target_pairs={{0,2},{1,3},{2,0},{3,1},{4,6},{5,7},{6,4},{7,5},{8,10},{9,11},{10,... | collective-permute-start | bytes 196616 | tf_op jit(solution)/shard_map/ppermute | solution.py:25
  48.7 6.9 %collective-permute-start.19 = (bf16[8,16,256]{2,1,0:T(8,128)(2,1)S(1)}, bf16[8,16,256]{2,1,0:T(8,128)(2,1)S(1)}, u32[]{:S(2)}, u32[]{:S(2)}) collective-permute-start(bf16[8,16,256]{2,1,0:T(8,128)(2,1)S(1)} %add_convert_fusion.2), channel_id=1, source_target_pairs={{0,4},{1,5},{2,6},{3,7},{4,0},{5,1},{6,2},{7,3},{8,12},{9,13},{10,... | collective-permute-start | bytes 196616 | tf_op jit(solution)/shard_map/ppermute | solution.py:25
  51.7 6.2 %collective-permute-start.21 = (bf16[8,16,256]{2,1,0:T(8,128)(2,1)S(1)}, bf16[8,16,256]{2,1,0:T(8,128)(2,1)S(1)}, u32[]{:S(2)}, u32[]{:S(2)}) collective-permute-start(bf16[8,16,256]{2,1,0:T(8,128)(2,1)S(1)} %add_convert_fusion.1), channel_id=1, source_target_pairs={{0,6},{1,7},{2,4},{3,5},{4,2},{5,3},{6,0},{7,1},{8,14},{9,15},{10,... | collective-permute-start | bytes 196616 | tf_op jit(solution)/shard_map/ppermute | solution.py:25
  60.2 6.5 %collective-permute-start.26 = (bf16[2,64,256]{2,1,0:T(8,128)(2,1)S(1)}, bf16[2,64,256]{2,1,0:T(8,128)(2,1)S(1)}, u32[]{:S(2)}, u32[]{:S(2)}) collective-permute-start(bf16[2,64,256]{2,1,0:T(8,128)(2,1)S(1)} %pad_maximum_fusion.3), channel_id=1, source_target_pairs={{0,4},{1,5},{2,6},{3,7},{4,0},{5,1},{6,2},{7,3},{8,12},{9,13},{10,... | collective-permute-start | bytes 196616 | tf_op jit(solution)/shard_map/ppermute | solution.py:25
  66.7 5.5 %collective-permute-start.27 = (bf16[4,64,256]{2,1,0:T(8,128)(2,1)S(1)}, bf16[4,64,256]{2,1,0:T(8,128)(2,1)S(1)}, u32[]{:S(2)}, u32[]{:S(2)}) collective-permute-start(bf16[4,64,256]{2,1,0:T(8,128)(2,1)S(1)} %pad_maximum_fusion.2), channel_id=1, source_target_pairs={{0,2},{1,3},{2,0},{3,1},{4,6},{5,7},{6,4},{7,5},{8,10},{9,11},{10,... | collective-permute-start | bytes 393224 | tf_op jit(solution)/shard_map/ppermute | solution.py:25
  66.8 13.3 %all-to-all-start = ((bf16[8,4,16,256]{3,2,1,0:T(8,128)(2,1)}), bf16[8,4,16,256]{3,2,1,0:T(8,128)(2,1)S(1)}, u32[]{:S(2)}, u32[]{:S(2)}) async-start(bf16[8,4,16,256]{3,2,1,0:T(8,128)(2,1)} %bitcast.9), calls=%async_computation | async-start | bytes 524288 | tf_op jit(solution)/shard_map/all_to_all | solution.py:358
  (14 other events, 119.4 us)

commit v4 on v3

--- a/solution.py
+++ b/solution.py
@@ -128,7 +128,7 @@
 
 
 def contribute_body(spot_ref, sizes_ref, total_ref, later_ref, lower_ref, *refs):
-    pieces, carriers, outs = refs[:PARTS], refs[PARTS:-11], refs[-11:-3]
+    pieces, carriers, outs = refs[:PARTS], refs[PARTS:-10], refs[-10:-3]
     top_ref, right, product_ref = refs[-3:]
     live, row = sizes_ref[spot_ref[1]], spot_ref[0]
     depth = later_ref.shape[1] // PARTS
@@ -149,7 +149,11 @@
             mine = pl.multiple_of(base + y * height, height)
             other = pl.multiple_of(base + (1 - y) * height, height)
             outs[k][j] = product_ref[pl.ds(mine, height)]
-            outs[4 + k][j] = product_ref[pl.ds(other, height)].astype(BF16)
+            sent = product_ref[pl.ds(other, height)].astype(BF16)
+            if k > 1:
+                outs[3 + k][j] = sent
+            else:
+                outs[4][k * slabs + j] = sent
 
 
 def contribute(spot, sizes, total, later, lower, pieces, carriers):
@@ -161,10 +165,11 @@
     out = pl.pallas_call(
         contribute_body,
         out_shape=[jax.ShapeDtypeStruct(slot, F32)] * 4
-        + [jax.ShapeDtypeStruct(slot, BF16)] * 4
+        + [jax.ShapeDtypeStruct((2 * slot[0],) + slot[1:], BF16)]
+        + [jax.ShapeDtypeStruct(slot, BF16)] * 2
         + [jax.ShapeDtypeStruct(tops, BF16)],
         in_specs=[SMEM, SMEM] + [VMEM] * (3 + len(pieces) + len(carriers)),
-        out_specs=[VMEM] * 9,
+        out_specs=[VMEM] * 8,
         scratch_shapes=[
             pltpu.VMEM((later.shape[1], cols), BF16),
             pltpu.VMEM((border, cols), F32),
@@ -176,7 +181,7 @@
             transcendentals=0,
         ),
     )(spot, sizes, total, later, lower, *pieces, *carriers)
-    return out[:4], out[4:8], out[8]
+    return out[:4], out[4:7], out[7]
 
 
 def place_body(targets_ref, spot_ref, *refs):
@@ -240,24 +245,27 @@
     )(spot, order[None], inverse)
 
 
-def factor_body(mine_ref, other_ref, top_ref, came_ref, out_ref):
+def factor_body(mine_ref, other_ref, top_ref, came_ref, slots_ref, out_ref):
     count, half, cols = top_ref.shape
+    slots = slots_ref.shape[0]
     total = jnp.dot(
         mine_ref[...], top_ref[...].reshape(count * half, cols), preferred_element_type=F32
     ) + jnp.dot(
         other_ref[...], came_ref[...].reshape(count * half, cols), preferred_element_type=F32
     )
-    out_ref[...] = total.astype(BF16)
-
-
-def panel_factor(mine, other, top, came):
+    out_ref[:slots] = slots_ref[...]
+    out_ref[slots:] = total.astype(BF16).reshape(out_ref.shape[0] - slots, -1, cols)
+
+
+def panel_factor(mine, other, top, came, slots):
+    count, height, cols = slots.shape
     return pl.pallas_call(
         factor_body,
-        out_shape=jax.ShapeDtypeStruct((mine.shape[0], top.shape[-1]), BF16),
-        in_specs=[VMEM] * 4,
+        out_shape=jax.ShapeDtypeStruct((count + mine.shape[0] // height, height, cols), BF16),
+        in_specs=[VMEM] * 5,
         out_specs=VMEM,
         compiler_params=params(),
-    )(mine, other, top, came)
+    )(mine, other, top, came, slots)
 
 
 def base_body(place_ref, surface_ref, lower_ref, mine_ref, other_ref, out_ref, factor_ref):
@@ -335,25 +343,29 @@
     )
 
     top_other = group_swap(top_mine, 1)
-    come = {k: across(send[k]) for k in (3, 2, 1, 0)}
+    come3, come2 = across(send[2]), across(send[1])
+    last = panel_factor(lower_mine, lower_other, top_mine, top_other, send[0])
+    come10 = across(last)
+    come3, come2, last = together((come3, come2, last))
+    slabs = keep[0].shape[0]
+    come = [come10[:slabs], come10[slabs : 2 * slabs], come2, come3]
     sums = [keep[k] + come[k].astype(F32) for k in range(4)]
-    for k in (3, 2, 1):
-        sums[k] = along(sums[k].astype(BF16), k).astype(F32)
-    factor = panel_factor(lower_mine, lower_other, top_mine, top_other)
-    factor_y = across(factor)
-    mine = (sums[0] + sums[1] + sums[2] + sums[3]).astype(BF16)
-    mine, factor_y = together((mine, factor_y))
-    factor2 = jnp.stack([factor, factor_y])
-    factor2_in = along(factor2, 2)
+    swapped = {k: along(sums[k].astype(BF16), k) for k in (3, 2, 1)}
+    factor = jnp.stack([last[2 * slabs :], come10[2 * slabs :]])
+    swapped[2], factor = together((swapped[2], factor))
+    factor_in = along(factor, 2)
+    mine = sums[0] + swapped[1].astype(F32) + swapped[2].astype(F32) + swapped[3].astype(F32)
+    mine = mine.astype(BF16)
     pieces = [mine] + [group_swap(mine, k) for k in (1, 2, 3)]
+    pieces[1], factor_in = together((pieces[1], factor_in))
+    factor4 = jnp.concatenate([factor, factor_in])
+    factor_mine = jnp.concatenate([factor4, along(factor4, 1)])
+    factor_mine = factor_mine.reshape((row_count, half) + top.shape[1:])
+    factor_other = group_swap(factor_mine, 1)
+    base = panel_update(spot, surface, panel_lower, factor_mine, factor_other)
     local_blocks = surface.shape[0] // BLOCK
     blocks = local_blocks * row_count
     slots = place(border_blocks, spot, pieces, blocks)
-    slots, factor2_in = together((slots, factor2_in))
-    factor4 = jnp.concatenate([factor2, factor2_in])
-    factor_mine = jnp.concatenate([factor4, along(factor4, 1)])
-    factor_other = group_swap(factor_mine, 1)
-    base = panel_update(spot, surface, panel_lower, factor_mine, factor_other)
     slots = slots.reshape((row_count, local_blocks) + slots.shape[1:])
     got = lax.all_to_all(slots, "row", 0, 0, tiled=True)
     collected = got.transpose(1, 0, 2, 3).reshape(surface.shape).astype(F32)

time: 81.4 us -> 80.9 us (level)
  starting transfers between devices: 37.5 us -> 31.8 us
  waiting for transfers between devices: 22.5 us -> 27.7 us
    ppermute x10 -> x8, starting transfers between devices: 14.7 us -> 9.14 us  [row_permute(): return lax.ppermute(value, 'row', [(s, t[0] * 2 + t[1]) for s, t in pairs])]
    ppermute x10 -> x8, waiting for transfers between devices: 4.74 us -> 8.51 us  [row_permute(): return lax.ppermute(value, 'row', [(s, t[0] * 2 + t[1]) for s, t in pairs])]
    all_to_all x1, waiting for transfers between devices: 5.22 us -> 6.59 us  [staged(): got = lax.all_to_all(slots, 'row', 0, 0, tiled=True)]
  transfers between devices with their start and end apart: 30 -> 28, of which waited for: 17 -> 17; matrix products, arithmetic and copies ran while one was open for 0% -> 0% of each run, Pallas kernels for 18% -> 18%
where the time goes in v4:
time: 80.9 us; the launch traced here: 80.6 us
  starting transfers between devices  31.8 us (39%)
  waiting for transfers between devices  27.7 us (34%)
  Pallas kernels  16.9 us (21%)
  local copies, waits for them, and re-layouts  2.8 us (3%)
  other arithmetic  1.15 us (1%)
    ppermute x14, starting transfers between devices, ring_send(): return lax.ppermute(value, 'row', pairs)  16 us
    pallas_call x3, Pallas kernels, multiply(): pl.pallas_call(functools.partial(multiply_body, parts_in, depth, bool(ext...  10.8 us
    ppermute x14, waiting for transfers between devices, ring_send(): return lax.ppermute(value, 'row', pairs)  9.29 us
    ppermute x8, starting transfers between devices, row_permute(): return lax.ppermute(value, 'row', [(s, t[0] * 2 + t[1]) for s, t in pairs])  9.14 us
    ppermute x8, waiting for transfers between devices, row_permute(): return lax.ppermute(value, 'row', [(s, t[0] * 2 + t[1]) for s, t in pairs])  8.51 us
    all_to_all x1, waiting for transfers between devices, staged(): got = lax.all_to_all(slots, 'row', 0, 0, tiled=True)  6.59 us
    all_to_all x1, starting transfers between devices, staged(): got = lax.all_to_all(slots, 'row', 0, 0, tiled=True)  4.58 us
    ppermute x5, waiting for transfers between devices, group_swap(): return lax.ppermute(value, 'grp', [(g, g ^ step) for g in range(4)])  3.27 us
  transfers between devices with their start and end apart: 28, of which 17 were waited for; matrix products, arithmetic and copies ran while one was open for 0% of the time, Pallas kernels for 18%

profile of v4, /device:TPU:0, one launch (start us, length us, event | category | flops | bytes accessed | tf_op | source)
XLA Modules:
  0.0 80.6 jit_solution(9886503844580941353)
XLA Ops:
  1.1 3.1 %collective-permute-start = (bf16[448,256]{1,0:T(8,128)(2,1)S(1)}, bf16[448,256]{1,0:T(8,128)(2,1)S(1)}, u32[]{:S(2)}, u32[]{:S(2)}) collective-permute-start(bf16[448,256]{1,0:T(8,128)(2,1)S(1)} %pad_maximum_fusion.1.refs_0_.refs_2_), channel_id=1, source_target_pairs={{0,2},{1,0},{2,4},{3,1},{4,6},{5,3},{6,7},{7,5},{8,10},{9,8},{10,1... | collective-permute-start | bytes 688136 | tf_op jit(solution)/shard_map/ppermute | solution.py:40
  4.2 2.0 %collective-permute-start.4 = (bf16[384,256]{1,0:T(8,128)(2,1)S(1)}, bf16[384,256]{1,0:T(8,128)(2,1)S(1)}, u32[]{:S(2)}, u32[]{:S(2)}) collective-permute-start(bf16[384,256]{1,0:T(8,128)(2,1)S(1)} %get-tuple-element.73.refs_1_), channel_id=1, source_target_pairs={{0,2},{1,0},{2,4},{3,1},{4,6},{5,3},{6,7},{7,5},{8,10},{9,8},{10,1... | collective-permute-start | bytes 589832 | tf_op jit(solution)/shard_map/ppermute | solution.py:40
  10.6 2.2 %collective-permute-done.1.refs_4_ = bf16[448,256]{1,0:T(8,128)(2,1)S(1)} collective-permute-done((bf16[448,256]{1,0:T(8,128)(2,1)S(1)}, bf16[448,256]{1,0:T(8,128)(2,1)S(1)}, u32[]{:S(2)}, u32[]{:S(2)}) %collective-permute-start.1) | collective-permute-done | bytes 229408 | tf_op jit(solution)/shard_map/ppermute | solution.py:40
  12.8 1.6 %collective-permute-start.2 = (bf16[448,256]{1,0:T(8,128)(2,1)S(1)}, bf16[448,256]{1,0:T(8,128)(2,1)S(1)}, u32[]{:S(2)}, u32[]{:S(2)}) collective-permute-start(bf16[448,256]{1,0:T(8,128)(2,1)S(1)} %collective-permute-done.refs_2_.refs_3_), channel_id=1, source_target_pairs={{0,2},{1,0},{2,4},{3,1},{4,6},{5,3},{6,7},{7,5},{8,10},{9,8},{10,1... | collective-permute-start | bytes 688136 | tf_op jit(solution)/shard_map/ppermute | solution.py:40
  14.8 2.2 %collective-permute-done.5.refs_5_ = bf16[384,256]{1,0:T(8,128)(2,1)S(1)} collective-permute-done((bf16[384,256]{1,0:T(8,128)(2,1)S(1)}, bf16[384,256]{1,0:T(8,128)(2,1)S(1)}, u32[]{:S(2)}, u32[]{:S(2)}) %collective-permute-start.5) | collective-permute-done | bytes 196640 | tf_op jit(solution)/shard_map/ppermute | solution.py:40
  17.0 1.6 %collective-permute-start.8 = (bf16[384,256]{1,0:T(8,128)(2,1)S(1)}, bf16[384,256]{1,0:T(8,128)(2,1)S(1)}, u32[]{:S(2)}, u32[]{:S(2)}) collective-permute-start(bf16[384,256]{1,0:T(8,128)(2,1)S(1)} %collective-permute-done.4.refs_3_), channel_id=1, source_target_pairs={{0,2},{1,0},{2,4},{3,1},{4,6},{5,3},{6,7},{7,5},{8,10},{9,8},{10,1... | collective-permute-start | bytes 589832 | tf_op jit(solution)/shard_map/ppermute | solution.py:40
  19.0 4.0 %shard_map.101.refs_4_ = f32[768,256]{1,0:T(8,128)S(1)} custom-call(s32[2]{0:T(128)S(1)} %pad_add_fusion.spot_ref.place_ref, s32[4]{0:T(128)S(1)} %copy-done.5, bf16[768,6144]{1,0:T(8,128)(2,1)} %bitcast.23, bf16[448,256]{1,0:T(8,128)(2,1)S(1)} %pad_maximum_fusion.1.refs_0_.refs_2_, bf16[384,256]{1,0:T(8,128)(2,1)S(1)} %get-tuple-element.73.refs_1_, ...), custom_call_target="tpu_custom_call" | custom-call | flops 905969664 | bytes 3538944 | tf_op jit(solution)/shard_map/pallas_call | solution.py:113
  23.1 1.6 %collective-permute-start.6 = (bf16[448,256]{1,0:T(8,128)(2,1)S(1)}, bf16[448,256]{1,0:T(8,128)(2,1)S(1)}, u32[]{:S(2)}, u32[]{:S(2)}) collective-permute-start(bf16[448,256]{1,0:T(8,128)(2,1)S(1)} %collective-permute-done.2.refs_0_.refs_5_), channel_id=1, source_target_pairs={{0,2},{1,0},{2,4},{3,1},{4,6},{5,3},{6,7},{7,5},{8,10},{9,8},{10,1... | collective-permute-start | bytes 688136 | tf_op jit(solution)/shard_map/ppermute | solution.py:40
  25.6 1.6 %collective-permute-start.10 = (bf16[384,256]{1,0:T(8,128)(2,1)S(1)}, bf16[384,256]{1,0:T(8,128)(2,1)S(1)}, u32[]{:S(2)}, u32[]{:S(2)}) collective-permute-start(bf16[384,256]{1,0:T(8,128)(2,1)S(1)} %collective-permute-done.8.refs_1_), channel_id=1, source_target_pairs={{0,2},{1,0},{2,4},{3,1},{4,6},{5,3},{6,7},{7,5},{8,10},{9,8},{10,1... | collective-permute-start | bytes 589832 | tf_op jit(solution)/shard_map/ppermute | solution.py:40
  27.6 3.4 %shard_map.102.refs_4_ = f32[768,256]{1,0:T(8,128)S(1)} custom-call(s32[2]{0:T(128)S(1)} %pad_add_fusion.spot_ref.place_ref, s32[4]{0:T(128)S(1)} %copy-done.5, bf16[768,6144]{1,0:T(8,128)(2,1)} %bitcast.24, bf16[448,256]{1,0:T(8,128)(2,1)S(1)} %collective-permute-done.2.refs_0_.refs_5_, bf16[384,256]{1,0:T(8,128)(2,1)S(1)} %collective-permute-done.8.refs_1_, ...), custom_call_target="tpu_custom_call" | custom-call | flops 603979776 | bytes 2359296 | tf_op jit(solution)/shard_map/pallas_call | solution.py:113
  31.7 1.6 %collective-permute-start.12 = (bf16[448,256]{1,0:T(8,128)(2,1)S(1)}, bf16[448,256]{1,0:T(8,128)(2,1)S(1)}, u32[]{:S(2)}, u32[]{:S(2)}) collective-permute-start(bf16[448,256]{1,0:T(8,128)(2,1)S(1)} %collective-permute-done.6.refs_0_.refs_7_), channel_id=1, source_target_pairs={{0,2},{1,0},{2,4},{3,1},{4,6},{5,3},{6,7},{7,5},{8,10},{9,8},{10,1... | collective-permute-start | bytes 688136 | tf_op jit(solution)/shard_map/ppermute | solution.py:40
  35.9 3.4 %shard_map.103 = (f32[768,256]{1,0:T(8,128)S(1)}, bf16[768,768]{1,0:T(8,128)(2,1)S(1)}) custom-call(s32[2]{0:T(128)S(1)} %pad_add_fusion.spot_ref.place_ref, s32[4]{0:T(128)S(1)} %copy-done.5, bf16[768,6144]{1,0:T(8,128)(2,1)} %bitcast.25, bf16[448,256]{1,0:T(8,128)(2,1)S(1)} %collective-permute-done.6.refs_0_.refs_7_, ...), custom_call_target="tpu_custom_call" | custom-call | flops 603979776 | bytes 2359296 | tf_op jit(solution)/shard_map/pallas_call | solution.py:113
  40.3 2.1 %shard_map.104 = (f32[8,16,256]{2,1,0:T(8,128)S(1)}, f32[8,16,256]{2,1,0:T(8,128)S(1)}, f32[8,16,256]{2,1,0:T(8,128)S(1)}, f32[8,16,256]{2,1,0:T(8,128)S(1)}, bf...) custom-call(s32[2]{0:T(128)S(1)} %pad_add_fusion.spot_ref.place_ref,, ...), custom_call_target="tpu_custom_call" | custom-call | flops 704643072 | bytes 2752512 | tf_op jit(solution)/shard_map/pallas_call | solution.py:165
  46.1 1.4 %collective-permute-done.14 = bf16[8,16,256]{2,1,0:T(8,128)(2,1)S(1)} collective-permute-done((bf16[8,16,256]{2,1,0:T(8,128)(2,1)S(1)}, bf16[8,16,256]{2,1,0:T(8,128)(2,1)S(1)}, u32[]{:S(2)}, u32[]{:S(2)}) %collective-permute-start.14) | collective-permute-done | bytes 65568 | tf_op jit(solution)/shard_map/ppermute | solution.py:25
  47.5 1.4 %collective-permute-done.15 = bf16[8,16,256]{2,1,0:T(8,128)(2,1)S(1)} collective-permute-done((bf16[8,16,256]{2,1,0:T(8,128)(2,1)S(1)}, bf16[8,16,256]{2,1,0:T(8,128)(2,1)S(1)}, u32[]{:S(2)}, u32[]{:S(2)}) %collective-permute-start.15) | collective-permute-done | bytes 65568 | tf_op jit(solution)/shard_map/ppermute | solution.py:25
  48.9 2.9 %collective-permute-start.17 = (bf16[8,16,256]{2,1,0:T(8,128)(2,1)S(1)}, bf16[8,16,256]{2,1,0:T(8,128)(2,1)S(1)}, u32[]{:S(2)}, u32[]{:S(2)}) collective-permute-start(bf16[8,16,256]{2,1,0:T(8,128)(2,1)S(1)} %add_convert_fusion.3), channel_id=1, source_target_pairs={{0,4},{1,5},{2,6},{3,7},{4,0},{5,1},{6,2},{7,3},{8,12},{9,13},{10,... | collective-permute-start | bytes 196616 | tf_op jit(solution)/shard_map/ppermute | solution.py:25
  51.8 1.4 %collective-permute-start.20 = (bf16[8,16,256]{2,1,0:T(8,128)(2,1)S(1)}, bf16[8,16,256]{2,1,0:T(8,128)(2,1)S(1)}, u32[]{:S(2)}, u32[]{:S(2)}) collective-permute-start(bf16[8,16,256]{2,1,0:T(8,128)(2,1)S(1)} %add_convert_fusion.1), channel_id=1, source_target_pairs={{0,6},{1,7},{2,4},{3,5},{4,2},{5,3},{6,0},{7,1},{8,14},{9,15},{10,... | collective-permute-start | bytes 196616 | tf_op jit(solution)/shard_map/ppermute | solution.py:25
  53.9 2.6 %collective-permute-done.17 = bf16[8,16,256]{2,1,0:T(8,128)(2,1)S(1)} collective-permute-done((bf16[8,16,256]{2,1,0:T(8,128)(2,1)S(1)}, bf16[8,16,256]{2,1,0:T(8,128)(2,1)S(1)}, u32[]{:S(2)}, u32[]{:S(2)}) %collective-permute-start.17) | collective-permute-done | bytes 65568 | tf_op jit(solution)/shard_map/ppermute | solution.py:25
  58.7 1.6 %collective-permute-start.25 = (bf16[8,16,256]{2,1,0:T(8,128)(2,1)S(1)}, bf16[8,16,256]{2,1,0:T(8,128)(2,1)S(1)}, u32[]{:S(2)}, u32[]{:S(2)}) collective-permute-start(bf16[8,16,256]{2,1,0:T(8,128)(2,1)S(1)} %add_convert_fusion.refs_0_), channel_id=1, source_target_pairs={{0,16},{8,24},{16,0},{24,8},{1,17},{9,25},{17,1},{25,9},{2,18},{10... | collective-permute-start | bytes 196616 | tf_op jit(solution)/shard_map/ppermute | solution.py:52
  60.5 1.8 %collective-permute-done.22 = bf16[2,4,16,256]{3,2,1,0:T(8,128)(2,1)S(1)} collective-permute-done((bf16[2,4,16,256]{3,2,1,0:T(8,128)(2,1)S(1)}, bf16[2,4,16,256]{3,2,1,0:T(8,128)(2,1)S(1)}, u32[]{:S(2)}, u32[]{:S(2)}) %collective-permute-start.22) | collective-permute-done | bytes 65568 | tf_op jit(solution)/shard_map/ppermute | solution.py:25
  64.3 1.5 %shard_map.107 = bf16[32,16,256]{2,1,0:T(8,128)(2,1)} custom-call(s32[4,8]{1,0:T(4,128)S(1)} %copy-done.7, s32[2]{0:T(128)S(1)} %pad_add_fusion.spot_ref.place_ref, bf16[8,16,256]{2,1,0:T(8,128)(2,1)S(1)} %add_convert_fusion.refs_0_, bf16[8,16,256]{2,1,0:T(8,128)(2,1)S(1)} %collective-permute-done.21.refs_1_, ...), custom_call_target="tpu_custom_call" | custom-call | tf_op jit(solution)/shard_map/pallas_call | solution.py:206
  65.8 4.6 %all-to-all-start = ((bf16[8,4,16,256]{3,2,1,0:T(8,128)(2,1)}), bf16[8,4,16,256]{3,2,1,0:T(8,128)(2,1)S(1)}, u32[]{:S(2)}, u32[]{:S(2)}) async-start(bf16[8,4,16,256]{3,2,1,0:T(8,128)(2,1)} %bitcast.10), calls=%async_computation | async-start | bytes 524288 | tf_op jit(solution)/shard_map/all_to_all | solution.py:370
  70.5 1.5 %collective-permute-done.24.other_ref = bf16[8,64,256]{2,1,0:T(8,128)(2,1)S(1)} collective-permute-done((bf16[8,64,256]{2,1,0:T(8,128)(2,1)S(1)}, bf16[8,64,256]{2,1,0:T(8,128)(2,1)S(1)}, u32[]{:S(2)}, u32[]{:S(2)}) %collective-permute-start.24) | collective-permute-done | bytes 262176 | tf_op jit(solution)/shard_map/ppermute | solution.py:52
  73.0 6.6 %all-to-all-done = bf16[8,4,16,256]{3,2,1,0:T(8,128)(2,1)S(1)} async-done(((bf16[8,4,16,256]{3,2,1,0:T(8,128)(2,1)}), bf16[8,4,16,256]{3,2,1,0:T(8,128)(2,1)S(1)}, u32[]{:S(2)}, u32[]{:S(2)}) %all-to-all-start) | async-done | bytes 262176 | tf_op jit(solution)/shard_map/all_to_all | solution.py:370
  (72 shorter events, 22.9 us)
Async XLA Ops:
  1.1 9.5 %collective-permute-start = (bf16[448,256]{1,0:T(8,128)(2,1)S(1)}, bf16[448,256]{1,0:T(8,128)(2,1)S(1)}, u32[]{:S(2)}, u32[]{:S(2)}) collective-permute-start(bf16[448,256]{1,0:T(8,128)(2,1)S(1)} %pad_maximum_fusion.1.refs_0_.refs_2_), channel_id=1, source_target_pairs={{0,2},{1,0},{2,4},{3,1},{4,6},{5,3},{6,7},{7,5},{8,10},{9,8},{10,1... | collective-permute-start | bytes 688136 | tf_op jit(solution)/shard_map/ppermute | solution.py:40
  4.2 8.5 %collective-permute-start.1 = (bf16[448,256]{1,0:T(8,128)(2,1)S(1)}, bf16[448,256]{1,0:T(8,128)(2,1)S(1)}, u32[]{:S(2)}, u32[]{:S(2)}) collective-permute-start(bf16[448,256]{1,0:T(8,128)(2,1)S(1)} %pad_maximum_fusion.1.refs_0_.refs_2_), channel_id=1, source_target_pairs={{0,1},{1,3},{2,0},{3,5},{4,2},{5,7},{6,4},{7,6},{8,9},{9,11},{10,8... | collective-permute-start | bytes 688136 | tf_op jit(solution)/shard_map/ppermute | solution.py:40
  4.2 10.6 %collective-permute-start.4 = (bf16[384,256]{1,0:T(8,128)(2,1)S(1)}, bf16[384,256]{1,0:T(8,128)(2,1)S(1)}, u32[]{:S(2)}, u32[]{:S(2)}) collective-permute-start(bf16[384,256]{1,0:T(8,128)(2,1)S(1)} %get-tuple-element.73.refs_1_), channel_id=1, source_target_pairs={{0,2},{1,0},{2,4},{3,1},{4,6},{5,3},{6,7},{7,5},{8,10},{9,8},{10,1... | collective-permute-start | bytes 589832 | tf_op jit(solution)/shard_map/ppermute | solution.py:40
  6.2 10.7 %collective-permute-start.5 = (bf16[384,256]{1,0:T(8,128)(2,1)S(1)}, bf16[384,256]{1,0:T(8,128)(2,1)S(1)}, u32[]{:S(2)}, u32[]{:S(2)}) collective-permute-start(bf16[384,256]{1,0:T(8,128)(2,1)S(1)} %get-tuple-element.73.refs_1_), channel_id=1, source_target_pairs={{0,1},{1,3},{2,0},{3,5},{4,2},{5,7},{6,4},{7,6},{8,9},{9,11},{10,8... | collective-permute-start | bytes 589832 | tf_op jit(solution)/shard_map/ppermute | solution.py:40
  12.8 10.3 %collective-permute-start.2 = (bf16[448,256]{1,0:T(8,128)(2,1)S(1)}, bf16[448,256]{1,0:T(8,128)(2,1)S(1)}, u32[]{:S(2)}, u32[]{:S(2)}) collective-permute-start(bf16[448,256]{1,0:T(8,128)(2,1)S(1)} %collective-permute-done.refs_2_.refs_3_), channel_id=1, source_target_pairs={{0,2},{1,0},{2,4},{3,1},{4,6},{5,3},{6,7},{7,5},{8,10},{9,8},{10,1... | collective-permute-start | bytes 688136 | tf_op jit(solution)/shard_map/ppermute | solution.py:40
  14.3 8.7 %collective-permute-start.3 = (bf16[448,256]{1,0:T(8,128)(2,1)S(1)}, bf16[448,256]{1,0:T(8,128)(2,1)S(1)}, u32[]{:S(2)}, u32[]{:S(2)}) collective-permute-start(bf16[448,256]{1,0:T(8,128)(2,1)S(1)} %collective-permute-done.1.refs_4_), channel_id=1, source_target_pairs={{0,1},{1,3},{2,0},{3,5},{4,2},{5,7},{6,4},{7,6},{8,9},{9,11},{10,8... | collective-permute-start | bytes 688136 | tf_op jit(solution)/shard_map/ppermute | solution.py:40
  17.0 8.2 %collective-permute-start.8 = (bf16[384,256]{1,0:T(8,128)(2,1)S(1)}, bf16[384,256]{1,0:T(8,128)(2,1)S(1)}, u32[]{:S(2)}, u32[]{:S(2)}) collective-permute-start(bf16[384,256]{1,0:T(8,128)(2,1)S(1)} %collective-permute-done.4.refs_3_), channel_id=1, source_target_pairs={{0,2},{1,0},{2,4},{3,1},{4,6},{5,3},{6,7},{7,5},{8,10},{9,8},{10,1... | collective-permute-start | bytes 589832 | tf_op jit(solution)/shard_map/ppermute | solution.py:40
  18.5 7.0 %collective-permute-start.9 = (bf16[384,256]{1,0:T(8,128)(2,1)S(1)}, bf16[384,256]{1,0:T(8,128)(2,1)S(1)}, u32[]{:S(2)}, u32[]{:S(2)}) collective-permute-start(bf16[384,256]{1,0:T(8,128)(2,1)S(1)} %collective-permute-done.5.refs_5_), channel_id=1, source_target_pairs={{0,1},{1,3},{2,0},{3,5},{4,2},{5,7},{6,4},{7,6},{8,9},{9,11},{10,8... | collective-permute-start | bytes 589832 | tf_op jit(solution)/shard_map/ppermute | solution.py:40
  23.1 7.9 %collective-permute-start.6 = (bf16[448,256]{1,0:T(8,128)(2,1)S(1)}, bf16[448,256]{1,0:T(8,128)(2,1)S(1)}, u32[]{:S(2)}, u32[]{:S(2)}) collective-permute-start(bf16[448,256]{1,0:T(8,128)(2,1)S(1)} %collective-permute-done.2.refs_0_.refs_5_), channel_id=1, source_target_pairs={{0,2},{1,0},{2,4},{3,1},{4,6},{5,3},{6,7},{7,5},{8,10},{9,8},{10,1... | collective-permute-start | bytes 688136 | tf_op jit(solution)/shard_map/ppermute | solution.py:40
  24.7 7.0 %collective-permute-start.7 = (bf16[448,256]{1,0:T(8,128)(2,1)S(1)}, bf16[448,256]{1,0:T(8,128)(2,1)S(1)}, u32[]{:S(2)}, u32[]{:S(2)}) collective-permute-start(bf16[448,256]{1,0:T(8,128)(2,1)S(1)} %collective-permute-done.3.refs_2_.refs_6_), channel_id=1, source_target_pairs={{0,1},{1,3},{2,0},{3,5},{4,2},{5,7},{6,4},{7,6},{8,9},{9,11},{10,8... | collective-permute-start | bytes 688136 | tf_op jit(solution)/shard_map/ppermute | solution.py:40
  25.6 9.0 %collective-permute-start.10 = (bf16[384,256]{1,0:T(8,128)(2,1)S(1)}, bf16[384,256]{1,0:T(8,128)(2,1)S(1)}, u32[]{:S(2)}, u32[]{:S(2)}) collective-permute-start(bf16[384,256]{1,0:T(8,128)(2,1)S(1)} %collective-permute-done.8.refs_1_), channel_id=1, source_target_pairs={{0,2},{1,0},{2,4},{3,1},{4,6},{5,3},{6,7},{7,5},{8,10},{9,8},{10,1... | collective-permute-start | bytes 589832 | tf_op jit(solution)/shard_map/ppermute | solution.py:40
  27.1 7.5 %collective-permute-start.11 = (bf16[384,256]{1,0:T(8,128)(2,1)S(1)}, bf16[384,256]{1,0:T(8,128)(2,1)S(1)}, u32[]{:S(2)}, u32[]{:S(2)}) collective-permute-start(bf16[384,256]{1,0:T(8,128)(2,1)S(1)} %collective-permute-done.9.refs_3_), channel_id=1, source_target_pairs={{0,1},{1,3},{2,0},{3,5},{4,2},{5,7},{6,4},{7,6},{8,9},{9,11},{10,8... | collective-permute-start | bytes 589832 | tf_op jit(solution)/shard_map/ppermute | solution.py:40
  31.7 8.7 %collective-permute-start.12 = (bf16[448,256]{1,0:T(8,128)(2,1)S(1)}, bf16[448,256]{1,0:T(8,128)(2,1)S(1)}, u32[]{:S(2)}, u32[]{:S(2)}) collective-permute-start(bf16[448,256]{1,0:T(8,128)(2,1)S(1)} %collective-permute-done.6.refs_0_.refs_7_), channel_id=1, source_target_pairs={{0,2},{1,0},{2,4},{3,1},{4,6},{5,3},{6,7},{7,5},{8,10},{9,8},{10,1... | collective-permute-start | bytes 688136 | tf_op jit(solution)/shard_map/ppermute | solution.py:40
  34.7 5.7 %collective-permute-start.13 = (bf16[384,256]{1,0:T(8,128)(2,1)S(1)}, bf16[384,256]{1,0:T(8,128)(2,1)S(1)}, u32[]{:S(2)}, u32[]{:S(2)}) collective-permute-start(bf16[384,256]{1,0:T(8,128)(2,1)S(1)} %collective-permute-done.11.refs_3_), channel_id=1, source_target_pairs={{0,1},{1,3},{2,0},{3,5},{4,2},{5,7},{6,4},{7,6},{8,9},{9,11},{10,8... | collective-permute-start | bytes 589832 | tf_op jit(solution)/shard_map/ppermute | solution.py:40
  42.5 5.0 %collective-permute-start.14 = (bf16[8,16,256]{2,1,0:T(8,128)(2,1)S(1)}, bf16[8,16,256]{2,1,0:T(8,128)(2,1)S(1)}, u32[]{:S(2)}, u32[]{:S(2)}) collective-permute-start(bf16[8,16,256]{2,1,0:T(8,128)(2,1)S(1)} %get-tuple-element.57), channel_id=1, source_target_pairs={{0,1},{1,0},{2,3},{3,2},{4,5},{5,4},{6,7},{7,6},{8,9},{9,8},{10,11... | collective-permute-start | bytes 196616 | tf_op jit(solution)/shard_map/ppermute | solution.py:25
  43.8 5.1 %collective-permute-start.15 = (bf16[8,16,256]{2,1,0:T(8,128)(2,1)S(1)}, bf16[8,16,256]{2,1,0:T(8,128)(2,1)S(1)}, u32[]{:S(2)}, u32[]{:S(2)}) collective-permute-start(bf16[8,16,256]{2,1,0:T(8,128)(2,1)S(1)} %get-tuple-element.58), channel_id=1, source_target_pairs={{0,1},{1,0},{2,3},{3,2},{4,5},{5,4},{6,7},{7,6},{8,9},{9,8},{10,11... | collective-permute-start | bytes 196616 | tf_op jit(solution)/shard_map/ppermute | solution.py:25
  44.8 8.4 %collective-permute-start.18 = (bf16[20,16,256]{2,1,0:T(8,128)(2,1)S(1)}, bf16[20,16,256]{2,1,0:T(8,128)(2,1)S(1)}, u32[]{:S(2)}, u32[]{:S(2)}) collective-permute-start(bf16[20,16,256]{2,1,0:T(8,128)(2,1)S(1)} %shard_map.105), channel_id=1, source_target_pairs={{0,1},{1,0},{2,3},{3,2},{4,5},{5,4},{6,7},{7,6},{8,9},{9,8},{10,11... | collective-permute-start | bytes 491528 | tf_op jit(solution)/shard_map/ppermute | solution.py:25
  48.9 7.6 %collective-permute-start.17 = (bf16[8,16,256]{2,1,0:T(8,128)(2,1)S(1)}, bf16[8,16,256]{2,1,0:T(8,128)(2,1)S(1)}, u32[]{:S(2)}, u32[]{:S(2)}) collective-permute-start(bf16[8,16,256]{2,1,0:T(8,128)(2,1)S(1)} %add_convert_fusion.3), channel_id=1, source_target_pairs={{0,4},{1,5},{2,6},{3,7},{4,0},{5,1},{6,2},{7,3},{8,12},{9,13},{10,... | collective-permute-start | bytes 196616 | tf_op jit(solution)/shard_map/ppermute | solution.py:25
  51.8 6.7 %collective-permute-start.20 = (bf16[8,16,256]{2,1,0:T(8,128)(2,1)S(1)}, bf16[8,16,256]{2,1,0:T(8,128)(2,1)S(1)}, u32[]{:S(2)}, u32[]{:S(2)}) collective-permute-start(bf16[8,16,256]{2,1,0:T(8,128)(2,1)S(1)} %add_convert_fusion.1), channel_id=1, source_target_pairs={{0,6},{1,7},{2,4},{3,5},{4,2},{5,3},{6,0},{7,1},{8,14},{9,15},{10,... | collective-permute-start | bytes 196616 | tf_op jit(solution)/shard_map/ppermute | solution.py:25
  53.3 5.3 %collective-permute-start.19 = (bf16[8,16,256]{2,1,0:T(8,128)(2,1)S(1)}, bf16[8,16,256]{2,1,0:T(8,128)(2,1)S(1)}, u32[]{:S(2)}, u32[]{:S(2)}) collective-permute-start(bf16[8,16,256]{2,1,0:T(8,128)(2,1)S(1)} %add_convert_fusion.2), channel_id=1, source_target_pairs={{0,2},{1,3},{2,0},{3,1},{4,6},{5,7},{6,4},{7,5},{8,10},{9,11},{10,... | collective-permute-start | bytes 196616 | tf_op jit(solution)/shard_map/ppermute | solution.py:25
  56.5 5.9 %collective-permute-start.22 = (bf16[2,4,16,256]{3,2,1,0:T(8,128)(2,1)S(1)}, bf16[2,4,16,256]{3,2,1,0:T(8,128)(2,1)S(1)}, u32[]{:S(2)}, u32[]{:S(2)}) collective-permute-start(bf16[2,4,16,256]{3,2,1,0:T(8,128)(2,1)S(1)} %pad_maximum_fusion.3), channel_id=1, source_target_pairs={{0,4},{1,5},{2,6},{3,7},{4,0},{5,1},{6,2},{7,3},{8,12},{9,13},{10,... | collective-permute-start | bytes 196616 | tf_op jit(solution)/shard_map/ppermute | solution.py:25
  58.7 4.5 %collective-permute-start.25 = (bf16[8,16,256]{2,1,0:T(8,128)(2,1)S(1)}, bf16[8,16,256]{2,1,0:T(8,128)(2,1)S(1)}, u32[]{:S(2)}, u32[]{:S(2)}) collective-permute-start(bf16[8,16,256]{2,1,0:T(8,128)(2,1)S(1)} %add_convert_fusion.refs_0_), channel_id=1, source_target_pairs={{0,16},{8,24},{16,0},{24,8},{1,17},{9,25},{17,1},{25,9},{2,18},{10... | collective-permute-start | bytes 196616 | tf_op jit(solution)/shard_map/ppermute | solution.py:52
  62.4 8.0 %collective-permute-start.23 = (bf16[4,4,16,256]{3,2,1,0:T(8,128)(2,1)S(1)}, bf16[4,4,16,256]{3,2,1,0:T(8,128)(2,1)S(1)}, u32[]{:S(2)}, u32[]{:S(2)}) collective-permute-start(bf16[4,4,16,256]{3,2,1,0:T(8,128)(2,1)S(1)} %pad_maximum_fusion.2), channel_id=1, source_target_pairs={{0,2},{1,3},{2,0},{3,1},{4,6},{5,7},{6,4},{7,5},{8,10},{9,11},{10,... | collective-permute-start | bytes 393224 | tf_op jit(solution)/shard_map/ppermute | solution.py:25
  65.8 13.8 %all-to-all-start = ((bf16[8,4,16,256]{3,2,1,0:T(8,128)(2,1)}), bf16[8,4,16,256]{3,2,1,0:T(8,128)(2,1)S(1)}, u32[]{:S(2)}, u32[]{:S(2)}) async-start(bf16[8,4,16,256]{3,2,1,0:T(8,128)(2,1)} %bitcast.10), calls=%async_computation | async-start | bytes 524288 | tf_op jit(solution)/shard_map/all_to_all | solution.py:370
  (12 other events, 110.7 us)

commit v5 on v4

--- a/solution.py
+++ b/solution.py
@@ -128,7 +128,7 @@
 
 
 def contribute_body(spot_ref, sizes_ref, total_ref, later_ref, lower_ref, *refs):
-    pieces, carriers, outs = refs[:PARTS], refs[PARTS:-10], refs[-10:-3]
+    pieces, carriers, outs = refs[:PARTS], refs[PARTS:-9], refs[-9:-3]
     top_ref, right, product_ref = refs[-3:]
     live, row = sizes_ref[spot_ref[1]], spot_ref[0]
     depth = later_ref.shape[1] // PARTS
@@ -150,10 +150,7 @@
             other = pl.multiple_of(base + (1 - y) * height, height)
             outs[k][j] = product_ref[pl.ds(mine, height)]
             sent = product_ref[pl.ds(other, height)].astype(BF16)
-            if k > 1:
-                outs[3 + k][j] = sent
-            else:
-                outs[4][k * slabs + j] = sent
+            outs[4 + k // 2][k % 2 * slabs + j] = sent
 
 
 def contribute(spot, sizes, total, later, lower, pieces, carriers):
@@ -165,11 +162,10 @@
     out = pl.pallas_call(
         contribute_body,
         out_shape=[jax.ShapeDtypeStruct(slot, F32)] * 4
-        + [jax.ShapeDtypeStruct((2 * slot[0],) + slot[1:], BF16)]
-        + [jax.ShapeDtypeStruct(slot, BF16)] * 2
+        + [jax.ShapeDtypeStruct((2 * slot[0],) + slot[1:], BF16)] * 2
         + [jax.ShapeDtypeStruct(tops, BF16)],
         in_specs=[SMEM, SMEM] + [VMEM] * (3 + len(pieces) + len(carriers)),
-        out_specs=[VMEM] * 8,
+        out_specs=[VMEM] * 7,
         scratch_shapes=[
             pltpu.VMEM((later.shape[1], cols), BF16),
             pltpu.VMEM((border, cols), F32),
@@ -181,7 +177,7 @@
             transcendentals=0,
         ),
     )(spot, sizes, total, later, lower, *pieces, *carriers)
-    return out[:4], out[4:7], out[7]
+    return out[:4], out[4:6], out[6]
 
 
 def place_body(targets_ref, spot_ref, *refs):
@@ -343,12 +339,12 @@
     )
 
     top_other = group_swap(top_mine, 1)
-    come3, come2 = across(send[2]), across(send[1])
+    come32 = across(send[1])
     last = panel_factor(lower_mine, lower_other, top_mine, top_other, send[0])
     come10 = across(last)
-    come3, come2, last = together((come3, come2, last))
+    come32, last = together((come32, last))
     slabs = keep[0].shape[0]
-    come = [come10[:slabs], come10[slabs : 2 * slabs], come2, come3]
+    come = [come10[:slabs], come10[slabs : 2 * slabs], come32[:slabs], come32[slabs:]]
     sums = [keep[k] + come[k].astype(F32) for k in range(4)]
     swapped = {k: along(sums[k].astype(BF16), k) for k in (3, 2, 1)}
     factor = jnp.stack([last[2 * slabs :], come10[2 * slabs :]])

time: 80.9 us -> 80.9 us (level)
  starting transfers between devices: 31.8 us -> 35.6 us
  waiting for transfers between devices: 27.7 us -> 23.9 us
    ppermute x8 -> x7, starting transfers between devices: 9.14 us -> 12.6 us  [row_permute(): return lax.ppermute(value, 'row', [(s, t[0] * 2 + t[1]) for s, t in pairs])]
    ppermute x8 -> x7, waiting for transfers between devices: 8.51 us -> 5.35 us  [row_permute(): return lax.ppermute(value, 'row', [(s, t[0] * 2 + t[1]) for s, t in pairs])]
  transfers between devices with their start and end apart: 28 -> 27, of which waited for: 17 -> 16; matrix products, arithmetic and copies ran while one was open for 0% -> 0% of each run, Pallas kernels for 18% -> 18%
where the time goes in v5:
time: 80.9 us; the launch traced here: 80.6 us
  starting transfers between devices  35.6 us (44%)
  waiting for transfers between devices  23.9 us (30%)
  Pallas kernels  16.9 us (21%)
  local copies, waits for them, and re-layouts  2.8 us (3%)
  other arithmetic  1.16 us (1%)
    ppermute x14, starting transfers between devices, ring_send(): return lax.ppermute(value, 'row', pairs)  16 us
    ppermute x7, starting transfers between devices, row_permute(): return lax.ppermute(value, 'row', [(s, t[0] * 2 + t[1]) for s, t in pairs])  12.6 us
    pallas_call x3, Pallas kernels, multiply(): pl.pallas_call(functools.partial(multiply_body, parts_in, depth, bool(ext...  10.8 us
    ppermute x14, waiting for transfers between devices, ring_send(): return lax.ppermute(value, 'row', pairs)  9.29 us
    all_to_all x1, waiting for transfers between devices, staged(): got = lax.all_to_all(slots, 'row', 0, 0, tiled=True)  6.56 us
    ppermute x7, waiting for transfers between devices, row_permute(): return lax.ppermute(value, 'row', [(s, t[0] * 2 + t[1]) for s, t in pairs])  5.35 us
    all_to_all x1, starting transfers between devices, staged(): got = lax.all_to_all(slots, 'row', 0, 0, tiled=True)  4.8 us
    ppermute x5, waiting for transfers between devices, group_swap(): return lax.ppermute(value, 'grp', [(g, g ^ step) for g in range(4)])  2.74 us
  transfers between devices with their start and end apart: 27, of which 16 were waited for; matrix products, arithmetic and copies ran while one was open for 0% of the time, Pallas kernels for 18%

profile of v5, /device:TPU:0, one launch (start us, length us, event | category | flops | bytes accessed | tf_op | source)
XLA Modules:
  0.0 80.6 jit_solution(634950994545940048)
XLA Ops:
  1.1 3.1 %collective-permute-start = (bf16[448,256]{1,0:T(8,128)(2,1)S(1)}, bf16[448,256]{1,0:T(8,128)(2,1)S(1)}, u32[]{:S(2)}, u32[]{:S(2)}) collective-permute-start(bf16[448,256]{1,0:T(8,128)(2,1)S(1)} %pad_maximum_fusion.1.refs_0_.refs_2_), channel_id=1, source_target_pairs={{0,2},{1,0},{2,4},{3,1},{4,6},{5,3},{6,7},{7,5},{8,10},{9,8},{10,1... | collective-permute-start | bytes 688136 | tf_op jit(solution)/shard_map/ppermute | solution.py:40
  4.2 2.0 %collective-permute-start.4 = (bf16[384,256]{1,0:T(8,128)(2,1)S(1)}, bf16[384,256]{1,0:T(8,128)(2,1)S(1)}, u32[]{:S(2)}, u32[]{:S(2)}) collective-permute-start(bf16[384,256]{1,0:T(8,128)(2,1)S(1)} %get-tuple-element.69.refs_1_), channel_id=1, source_target_pairs={{0,2},{1,0},{2,4},{3,1},{4,6},{5,3},{6,7},{7,5},{8,10},{9,8},{10,1... | collective-permute-start | bytes 589832 | tf_op jit(solution)/shard_map/ppermute | solution.py:40
  8.0 1.3 %shard_map.100 = (bf16[64,512]{1,0:T(8,128)(2,1)S(1)}, bf16[64,512]{1,0:T(8,128)(2,1)S(1)}) custom-call(s32[2]{0:T(128)S(1)} %pad_add_fusion.spot_ref.place_ref, s32[1,1024]{1,0:T(1,128)S(1)} %bitcast.22, bf16[128,1024]{1,0:T(8,128)(2,1)S(1)} %copy-done.4), custom_call_target="tpu_custom_call" | custom-call | tf_op jit(solution)/shard_map/pallas_call | solution.py:235
  10.6 2.2 %collective-permute-done.1.refs_4_ = bf16[448,256]{1,0:T(8,128)(2,1)S(1)} collective-permute-done((bf16[448,256]{1,0:T(8,128)(2,1)S(1)}, bf16[448,256]{1,0:T(8,128)(2,1)S(1)}, u32[]{:S(2)}, u32[]{:S(2)}) %collective-permute-start.1) | collective-permute-done | bytes 229408 | tf_op jit(solution)/shard_map/ppermute | solution.py:40
  12.8 1.6 %collective-permute-start.2 = (bf16[448,256]{1,0:T(8,128)(2,1)S(1)}, bf16[448,256]{1,0:T(8,128)(2,1)S(1)}, u32[]{:S(2)}, u32[]{:S(2)}) collective-permute-start(bf16[448,256]{1,0:T(8,128)(2,1)S(1)} %collective-permute-done.refs_2_.refs_3_), channel_id=1, source_target_pairs={{0,2},{1,0},{2,4},{3,1},{4,6},{5,3},{6,7},{7,5},{8,10},{9,8},{10,1... | collective-permute-start | bytes 688136 | tf_op jit(solution)/shard_map/ppermute | solution.py:40
  14.8 2.2 %collective-permute-done.5.refs_5_ = bf16[384,256]{1,0:T(8,128)(2,1)S(1)} collective-permute-done((bf16[384,256]{1,0:T(8,128)(2,1)S(1)}, bf16[384,256]{1,0:T(8,128)(2,1)S(1)}, u32[]{:S(2)}, u32[]{:S(2)}) %collective-permute-start.5) | collective-permute-done | bytes 196640 | tf_op jit(solution)/shard_map/ppermute | solution.py:40
  17.0 1.6 %collective-permute-start.8 = (bf16[384,256]{1,0:T(8,128)(2,1)S(1)}, bf16[384,256]{1,0:T(8,128)(2,1)S(1)}, u32[]{:S(2)}, u32[]{:S(2)}) collective-permute-start(bf16[384,256]{1,0:T(8,128)(2,1)S(1)} %collective-permute-done.4.refs_3_), channel_id=1, source_target_pairs={{0,2},{1,0},{2,4},{3,1},{4,6},{5,3},{6,7},{7,5},{8,10},{9,8},{10,1... | collective-permute-start | bytes 589832 | tf_op jit(solution)/shard_map/ppermute | solution.py:40
  19.0 4.0 %shard_map.101.refs_4_ = f32[768,256]{1,0:T(8,128)S(1)} custom-call(s32[2]{0:T(128)S(1)} %pad_add_fusion.spot_ref.place_ref, s32[4]{0:T(128)S(1)} %copy-done.5, bf16[768,6144]{1,0:T(8,128)(2,1)} %bitcast.23, bf16[448,256]{1,0:T(8,128)(2,1)S(1)} %pad_maximum_fusion.1.refs_0_.refs_2_, bf16[384,256]{1,0:T(8,128)(2,1)S(1)} %get-tuple-element.69.refs_1_, ...), custom_call_target="tpu_custom_call" | custom-call | flops 905969664 | bytes 3538944 | tf_op jit(solution)/shard_map/pallas_call | solution.py:113
  23.1 1.6 %collective-permute-start.6 = (bf16[448,256]{1,0:T(8,128)(2,1)S(1)}, bf16[448,256]{1,0:T(8,128)(2,1)S(1)}, u32[]{:S(2)}, u32[]{:S(2)}) collective-permute-start(bf16[448,256]{1,0:T(8,128)(2,1)S(1)} %collective-permute-done.2.refs_0_.refs_5_), channel_id=1, source_target_pairs={{0,2},{1,0},{2,4},{3,1},{4,6},{5,3},{6,7},{7,5},{8,10},{9,8},{10,1... | collective-permute-start | bytes 688136 | tf_op jit(solution)/shard_map/ppermute | solution.py:40
  25.6 1.6 %collective-permute-start.10 = (bf16[384,256]{1,0:T(8,128)(2,1)S(1)}, bf16[384,256]{1,0:T(8,128)(2,1)S(1)}, u32[]{:S(2)}, u32[]{:S(2)}) collective-permute-start(bf16[384,256]{1,0:T(8,128)(2,1)S(1)} %collective-permute-done.8.refs_1_), channel_id=1, source_target_pairs={{0,2},{1,0},{2,4},{3,1},{4,6},{5,3},{6,7},{7,5},{8,10},{9,8},{10,1... | collective-permute-start | bytes 589832 | tf_op jit(solution)/shard_map/ppermute | solution.py:40
  27.6 3.4 %shard_map.102.refs_4_ = f32[768,256]{1,0:T(8,128)S(1)} custom-call(s32[2]{0:T(128)S(1)} %pad_add_fusion.spot_ref.place_ref, s32[4]{0:T(128)S(1)} %copy-done.5, bf16[768,6144]{1,0:T(8,128)(2,1)} %bitcast.24, bf16[448,256]{1,0:T(8,128)(2,1)S(1)} %collective-permute-done.2.refs_0_.refs_5_, bf16[384,256]{1,0:T(8,128)(2,1)S(1)} %collective-permute-done.8.refs_1_, ...), custom_call_target="tpu_custom_call" | custom-call | flops 603979776 | bytes 2359296 | tf_op jit(solution)/shard_map/pallas_call | solution.py:113
  31.7 1.6 %collective-permute-start.12 = (bf16[448,256]{1,0:T(8,128)(2,1)S(1)}, bf16[448,256]{1,0:T(8,128)(2,1)S(1)}, u32[]{:S(2)}, u32[]{:S(2)}) collective-permute-start(bf16[448,256]{1,0:T(8,128)(2,1)S(1)} %collective-permute-done.6.refs_0_.refs_7_), channel_id=1, source_target_pairs={{0,2},{1,0},{2,4},{3,1},{4,6},{5,3},{6,7},{7,5},{8,10},{9,8},{10,1... | collective-permute-start | bytes 688136 | tf_op jit(solution)/shard_map/ppermute | solution.py:40
  35.9 3.4 %shard_map.103 = (f32[768,256]{1,0:T(8,128)S(1)}, bf16[768,768]{1,0:T(8,128)(2,1)S(1)}) custom-call(s32[2]{0:T(128)S(1)} %pad_add_fusion.spot_ref.place_ref, s32[4]{0:T(128)S(1)} %copy-done.5, bf16[768,6144]{1,0:T(8,128)(2,1)} %bitcast.25, bf16[448,256]{1,0:T(8,128)(2,1)S(1)} %collective-permute-done.6.refs_0_.refs_7_, ...), custom_call_target="tpu_custom_call" | custom-call | flops 603979776 | bytes 2359296 | tf_op jit(solution)/shard_map/pallas_call | solution.py:113
  40.3 2.1 %shard_map.104 = (f32[8,16,256]{2,1,0:T(8,128)S(1)}, f32[8,16,256]{2,1,0:T(8,128)S(1)}, f32[8,16,256]{2,1,0:T(8,128)S(1)}, f32[8,16,256]{2,1,0:T(8,128)S(1)}, bf...) custom-call(s32[2]{0:T(128)S(1)} %pad_add_fusion.spot_ref.place_ref, ...), custom_call_target="tpu_custom_call" | custom-call | flops 704643072 | bytes 2752512 | tf_op jit(solution)/shard_map/pallas_call | solution.py:162
  45.5 3.4 %collective-permute-done.14 = bf16[16,16,256]{2,1,0:T(8,128)(2,1)S(1)} collective-permute-done((bf16[16,16,256]{2,1,0:T(8,128)(2,1)S(1)}, bf16[16,16,256]{2,1,0:T(8,128)(2,1)S(1)}, u32[]{:S(2)}, u32[]{:S(2)}) %collective-permute-start.14) | collective-permute-done | bytes 131104 | tf_op jit(solution)/shard_map/ppermute | solution.py:25
  48.9 2.4 %collective-permute-start.16 = (bf16[8,16,256]{2,1,0:T(8,128)(2,1)S(1)}, bf16[8,16,256]{2,1,0:T(8,128)(2,1)S(1)}, u32[]{:S(2)}, u32[]{:S(2)}) collective-permute-start(bf16[8,16,256]{2,1,0:T(8,128)(2,1)S(1)} %get-tuple-element.71), channel_id=1, source_target_pairs={{0,4},{1,5},{2,6},{3,7},{4,0},{5,1},{6,2},{7,3},{8,12},{9,13},{10,... | collective-permute-start | bytes 196616 | tf_op jit(solution)/shard_map/ppermute | solution.py:25
  51.3 1.9 %collective-permute-start.19 = (bf16[8,16,256]{2,1,0:T(8,128)(2,1)S(1)}, bf16[8,16,256]{2,1,0:T(8,128)(2,1)S(1)}, u32[]{:S(2)}, u32[]{:S(2)}) collective-permute-start(bf16[8,16,256]{2,1,0:T(8,128)(2,1)S(1)} %get-tuple-element.72), channel_id=1, source_target_pairs={{0,6},{1,7},{2,4},{3,5},{4,2},{5,3},{6,0},{7,1},{8,14},{9,15},{10,... | collective-permute-start | bytes 196616 | tf_op jit(solution)/shard_map/ppermute | solution.py:25
  54.6 2.5 %collective-permute-start.21 = (bf16[2,4,16,256]{3,2,1,0:T(8,128)(2,1)S(1)}, bf16[2,4,16,256]{3,2,1,0:T(8,128)(2,1)S(1)}, u32[]{:S(2)}, u32[]{:S(2)}) collective-permute-start(bf16[2,4,16,256]{3,2,1,0:T(8,128)(2,1)S(1)} %pad_maximum_fusion.3), channel_id=1, source_target_pairs={{0,4},{1,5},{2,6},{3,7},{4,0},{5,1},{6,2},{7,3},{8,12},{9,13},{10,... | collective-permute-start | bytes 196616 | tf_op jit(solution)/shard_map/ppermute | solution.py:25
  58.5 1.5 %collective-permute-start.24 = (bf16[8,16,256]{2,1,0:T(8,128)(2,1)S(1)}, bf16[8,16,256]{2,1,0:T(8,128)(2,1)S(1)}, u32[]{:S(2)}, u32[]{:S(2)}) collective-permute-start(bf16[8,16,256]{2,1,0:T(8,128)(2,1)S(1)} %add_convert_fusion.refs_0_), channel_id=1, source_target_pairs={{0,16},{8,24},{16,0},{24,8},{1,17},{9,25},{17,1},{25,9},{2,18},{10... | collective-permute-start | bytes 196616 | tf_op jit(solution)/shard_map/ppermute | solution.py:52
  60.4 2.7 %collective-permute-start.22 = (bf16[4,4,16,256]{3,2,1,0:T(8,128)(2,1)S(1)}, bf16[4,4,16,256]{3,2,1,0:T(8,128)(2,1)S(1)}, u32[]{:S(2)}, u32[]{:S(2)}) collective-permute-start(bf16[4,4,16,256]{3,2,1,0:T(8,128)(2,1)S(1)} %pad_maximum_fusion.2), channel_id=1, source_target_pairs={{0,2},{1,3},{2,0},{3,1},{4,6},{5,7},{6,4},{7,5},{8,10},{9,11},{10,... | collective-permute-start | bytes 393224 | tf_op jit(solution)/shard_map/ppermute | solution.py:25
  64.0 1.5 %shard_map.107 = bf16[32,16,256]{2,1,0:T(8,128)(2,1)} custom-call(s32[4,8]{1,0:T(4,128)S(1)} %copy-done.7, s32[2]{0:T(128)S(1)} %pad_add_fusion.spot_ref.place_ref, bf16[8,16,256]{2,1,0:T(8,128)(2,1)S(1)} %add_convert_fusion.refs_0_, bf16[8,16,256]{2,1,0:T(8,128)(2,1)S(1)} %collective-permute-done.20.refs_1_, ...), custom_call_target="tpu_custom_call" | custom-call | tf_op jit(solution)/shard_map/pallas_call | solution.py:202
  65.6 4.8 %all-to-all-start = ((bf16[8,4,16,256]{3,2,1,0:T(8,128)(2,1)}), bf16[8,4,16,256]{3,2,1,0:T(8,128)(2,1)S(1)}, u32[]{:S(2)}, u32[]{:S(2)}) async-start(bf16[8,4,16,256]{3,2,1,0:T(8,128)(2,1)} %bitcast.10), calls=%async_computation | async-start | bytes 524288 | tf_op jit(solution)/shard_map/all_to_all | solution.py:366
  70.5 1.5 %collective-permute-done.23.other_ref = bf16[8,64,256]{2,1,0:T(8,128)(2,1)S(1)} collective-permute-done((bf16[8,64,256]{2,1,0:T(8,128)(2,1)S(1)}, bf16[8,64,256]{2,1,0:T(8,128)(2,1)S(1)}, u32[]{:S(2)}, u32[]{:S(2)}) %collective-permute-start.23) | collective-permute-done | bytes 262176 | tf_op jit(solution)/shard_map/ppermute | solution.py:52
  73.1 6.6 %all-to-all-done = bf16[8,4,16,256]{3,2,1,0:T(8,128)(2,1)S(1)} async-done(((bf16[8,4,16,256]{3,2,1,0:T(8,128)(2,1)}), bf16[8,4,16,256]{3,2,1,0:T(8,128)(2,1)S(1)}, u32[]{:S(2)}, u32[]{:S(2)}) %all-to-all-start) | async-done | bytes 262176 | tf_op jit(solution)/shard_map/all_to_all | solution.py:366
  (69 shorter events, 20.1 us)
Async XLA Ops:
  1.1 9.5 %collective-permute-start = (bf16[448,256]{1,0:T(8,128)(2,1)S(1)}, bf16[448,256]{1,0:T(8,128)(2,1)S(1)}, u32[]{:S(2)}, u32[]{:S(2)}) collective-permute-start(bf16[448,256]{1,0:T(8,128)(2,1)S(1)} %pad_maximum_fusion.1.refs_0_.refs_2_), channel_id=1, source_target_pairs={{0,2},{1,0},{2,4},{3,1},{4,6},{5,3},{6,7},{7,5},{8,10},{9,8},{10,1... | collective-permute-start | bytes 688136 | tf_op jit(solution)/shard_map/ppermute | solution.py:40
  4.2 8.5 %collective-permute-start.1 = (bf16[448,256]{1,0:T(8,128)(2,1)S(1)}, bf16[448,256]{1,0:T(8,128)(2,1)S(1)}, u32[]{:S(2)}, u32[]{:S(2)}) collective-permute-start(bf16[448,256]{1,0:T(8,128)(2,1)S(1)} %pad_maximum_fusion.1.refs_0_.refs_2_), channel_id=1, source_target_pairs={{0,1},{1,3},{2,0},{3,5},{4,2},{5,7},{6,4},{7,6},{8,9},{9,11},{10,8... | collective-permute-start | bytes 688136 | tf_op jit(solution)/shard_map/ppermute | solution.py:40
  4.2 10.6 %collective-permute-start.4 = (bf16[384,256]{1,0:T(8,128)(2,1)S(1)}, bf16[384,256]{1,0:T(8,128)(2,1)S(1)}, u32[]{:S(2)}, u32[]{:S(2)}) collective-permute-start(bf16[384,256]{1,0:T(8,128)(2,1)S(1)} %get-tuple-element.69.refs_1_), channel_id=1, source_target_pairs={{0,2},{1,0},{2,4},{3,1},{4,6},{5,3},{6,7},{7,5},{8,10},{9,8},{10,1... | collective-permute-start | bytes 589832 | tf_op jit(solution)/shard_map/ppermute | solution.py:40
  6.2 10.7 %collective-permute-start.5 = (bf16[384,256]{1,0:T(8,128)(2,1)S(1)}, bf16[384,256]{1,0:T(8,128)(2,1)S(1)}, u32[]{:S(2)}, u32[]{:S(2)}) collective-permute-start(bf16[384,256]{1,0:T(8,128)(2,1)S(1)} %get-tuple-element.69.refs_1_), channel_id=1, source_target_pairs={{0,1},{1,3},{2,0},{3,5},{4,2},{5,7},{6,4},{7,6},{8,9},{9,11},{10,8... | collective-permute-start | bytes 589832 | tf_op jit(solution)/shard_map/ppermute | solution.py:40
  12.8 10.3 %collective-permute-start.2 = (bf16[448,256]{1,0:T(8,128)(2,1)S(1)}, bf16[448,256]{1,0:T(8,128)(2,1)S(1)}, u32[]{:S(2)}, u32[]{:S(2)}) collective-permute-start(bf16[448,256]{1,0:T(8,128)(2,1)S(1)} %collective-permute-done.refs_2_.refs_3_), channel_id=1, source_target_pairs={{0,2},{1,0},{2,4},{3,1},{4,6},{5,3},{6,7},{7,5},{8,10},{9,8},{10,1... | collective-permute-start | bytes 688136 | tf_op jit(solution)/shard_map/ppermute | solution.py:40
  14.3 8.7 %collective-permute-start.3 = (bf16[448,256]{1,0:T(8,128)(2,1)S(1)}, bf16[448,256]{1,0:T(8,128)(2,1)S(1)}, u32[]{:S(2)}, u32[]{:S(2)}) collective-permute-start(bf16[448,256]{1,0:T(8,128)(2,1)S(1)} %collective-permute-done.1.refs_4_), channel_id=1, source_target_pairs={{0,1},{1,3},{2,0},{3,5},{4,2},{5,7},{6,4},{7,6},{8,9},{9,11},{10,8... | collective-permute-start | bytes 688136 | tf_op jit(solution)/shard_map/ppermute | solution.py:40
  17.0 8.2 %collective-permute-start.8 = (bf16[384,256]{1,0:T(8,128)(2,1)S(1)}, bf16[384,256]{1,0:T(8,128)(2,1)S(1)}, u32[]{:S(2)}, u32[]{:S(2)}) collective-permute-start(bf16[384,256]{1,0:T(8,128)(2,1)S(1)} %collective-permute-done.4.refs_3_), channel_id=1, source_target_pairs={{0,2},{1,0},{2,4},{3,1},{4,6},{5,3},{6,7},{7,5},{8,10},{9,8},{10,1... | collective-permute-start | bytes 589832 | tf_op jit(solution)/shard_map/ppermute | solution.py:40
  18.5 7.0 %collective-permute-start.9 = (bf16[384,256]{1,0:T(8,128)(2,1)S(1)}, bf16[384,256]{1,0:T(8,128)(2,1)S(1)}, u32[]{:S(2)}, u32[]{:S(2)}) collective-permute-start(bf16[384,256]{1,0:T(8,128)(2,1)S(1)} %collective-permute-done.5.refs_5_), channel_id=1, source_target_pairs={{0,1},{1,3},{2,0},{3,5},{4,2},{5,7},{6,4},{7,6},{8,9},{9,11},{10,8... | collective-permute-start | bytes 589832 | tf_op jit(solution)/shard_map/ppermute | solution.py:40
  23.1 7.9 %collective-permute-start.6 = (bf16[448,256]{1,0:T(8,128)(2,1)S(1)}, bf16[448,256]{1,0:T(8,128)(2,1)S(1)}, u32[]{:S(2)}, u32[]{:S(2)}) collective-permute-start(bf16[448,256]{1,0:T(8,128)(2,1)S(1)} %collective-permute-done.2.refs_0_.refs_5_), channel_id=1, source_target_pairs={{0,2},{1,0},{2,4},{3,1},{4,6},{5,3},{6,7},{7,5},{8,10},{9,8},{10,1... | collective-permute-start | bytes 688136 | tf_op jit(solution)/shard_map/ppermute | solution.py:40
  24.7 7.0 %collective-permute-start.7 = (bf16[448,256]{1,0:T(8,128)(2,1)S(1)}, bf16[448,256]{1,0:T(8,128)(2,1)S(1)}, u32[]{:S(2)}, u32[]{:S(2)}) collective-permute-start(bf16[448,256]{1,0:T(8,128)(2,1)S(1)} %collective-permute-done.3.refs_2_.refs_6_), channel_id=1, source_target_pairs={{0,1},{1,3},{2,0},{3,5},{4,2},{5,7},{6,4},{7,6},{8,9},{9,11},{10,8... | collective-permute-start | bytes 688136 | tf_op jit(solution)/shard_map/ppermute | solution.py:40
  25.6 9.0 %collective-permute-start.10 = (bf16[384,256]{1,0:T(8,128)(2,1)S(1)}, bf16[384,256]{1,0:T(8,128)(2,1)S(1)}, u32[]{:S(2)}, u32[]{:S(2)}) collective-permute-start(bf16[384,256]{1,0:T(8,128)(2,1)S(1)} %collective-permute-done.8.refs_1_), channel_id=1, source_target_pairs={{0,2},{1,0},{2,4},{3,1},{4,6},{5,3},{6,7},{7,5},{8,10},{9,8},{10,1... | collective-permute-start | bytes 589832 | tf_op jit(solution)/shard_map/ppermute | solution.py:40
  27.1 7.5 %collective-permute-start.11 = (bf16[384,256]{1,0:T(8,128)(2,1)S(1)}, bf16[384,256]{1,0:T(8,128)(2,1)S(1)}, u32[]{:S(2)}, u32[]{:S(2)}) collective-permute-start(bf16[384,256]{1,0:T(8,128)(2,1)S(1)} %collective-permute-done.9.refs_3_), channel_id=1, source_target_pairs={{0,1},{1,3},{2,0},{3,5},{4,2},{5,7},{6,4},{7,6},{8,9},{9,11},{10,8... | collective-permute-start | bytes 589832 | tf_op jit(solution)/shard_map/ppermute | solution.py:40
  31.7 8.7 %collective-permute-start.12 = (bf16[448,256]{1,0:T(8,128)(2,1)S(1)}, bf16[448,256]{1,0:T(8,128)(2,1)S(1)}, u32[]{:S(2)}, u32[]{:S(2)}) collective-permute-start(bf16[448,256]{1,0:T(8,128)(2,1)S(1)} %collective-permute-done.6.refs_0_.refs_7_), channel_id=1, source_target_pairs={{0,2},{1,0},{2,4},{3,1},{4,6},{5,3},{6,7},{7,5},{8,10},{9,8},{10,1... | collective-permute-start | bytes 688136 | tf_op jit(solution)/shard_map/ppermute | solution.py:40
  34.7 5.7 %collective-permute-start.13 = (bf16[384,256]{1,0:T(8,128)(2,1)S(1)}, bf16[384,256]{1,0:T(8,128)(2,1)S(1)}, u32[]{:S(2)}, u32[]{:S(2)}) collective-permute-start(bf16[384,256]{1,0:T(8,128)(2,1)S(1)} %collective-permute-done.11.refs_3_), channel_id=1, source_target_pairs={{0,1},{1,3},{2,0},{3,5},{4,2},{5,7},{6,4},{7,6},{8,9},{9,11},{10,8... | collective-permute-start | bytes 589832 | tf_op jit(solution)/shard_map/ppermute | solution.py:40
  42.5 6.4 %collective-permute-start.14 = (bf16[16,16,256]{2,1,0:T(8,128)(2,1)S(1)}, bf16[16,16,256]{2,1,0:T(8,128)(2,1)S(1)}, u32[]{:S(2)}, u32[]{:S(2)}) collective-permute-start(bf16[16,16,256]{2,1,0:T(8,128)(2,1)S(1)} %get-tuple-element.55), channel_id=1, source_target_pairs={{0,1},{1,0},{2,3},{3,2},{4,5},{5,4},{6,7},{7,6},{8,9},{9,8},{10,11... | collective-permute-start | bytes 393224 | tf_op jit(solution)/shard_map/ppermute | solution.py:25
  44.3 8.9 %collective-permute-start.17 = (bf16[20,16,256]{2,1,0:T(8,128)(2,1)S(1)}, bf16[20,16,256]{2,1,0:T(8,128)(2,1)S(1)}, u32[]{:S(2)}, u32[]{:S(2)}) collective-permute-start(bf16[20,16,256]{2,1,0:T(8,128)(2,1)S(1)} %shard_map.105), channel_id=1, source_target_pairs={{0,1},{1,0},{2,3},{3,2},{4,5},{5,4},{6,7},{7,6},{8,9},{9,8},{10,11... | collective-permute-start | bytes 491528 | tf_op jit(solution)/shard_map/ppermute | solution.py:25
  48.9 5.7 %collective-permute-start.16 = (bf16[8,16,256]{2,1,0:T(8,128)(2,1)S(1)}, bf16[8,16,256]{2,1,0:T(8,128)(2,1)S(1)}, u32[]{:S(2)}, u32[]{:S(2)}) collective-permute-start(bf16[8,16,256]{2,1,0:T(8,128)(2,1)S(1)} %get-tuple-element.71), channel_id=1, source_target_pairs={{0,4},{1,5},{2,6},{3,7},{4,0},{5,1},{6,2},{7,3},{8,12},{9,13},{10,... | collective-permute-start | bytes 196616 | tf_op jit(solution)/shard_map/ppermute | solution.py:25
  51.3 6.7 %collective-permute-start.19 = (bf16[8,16,256]{2,1,0:T(8,128)(2,1)S(1)}, bf16[8,16,256]{2,1,0:T(8,128)(2,1)S(1)}, u32[]{:S(2)}, u32[]{:S(2)}) collective-permute-start(bf16[8,16,256]{2,1,0:T(8,128)(2,1)S(1)} %get-tuple-element.72), channel_id=1, source_target_pairs={{0,6},{1,7},{2,4},{3,5},{4,2},{5,3},{6,0},{7,1},{8,14},{9,15},{10,... | collective-permute-start | bytes 196616 | tf_op jit(solution)/shard_map/ppermute | solution.py:25
  53.2 5.1 %collective-permute-start.18 = (bf16[8,16,256]{2,1,0:T(8,128)(2,1)S(1)}, bf16[8,16,256]{2,1,0:T(8,128)(2,1)S(1)}, u32[]{:S(2)}, u32[]{:S(2)}) collective-permute-start(bf16[8,16,256]{2,1,0:T(8,128)(2,1)S(1)} %add_convert_fusion.2), channel_id=1, source_target_pairs={{0,2},{1,3},{2,0},{3,1},{4,6},{5,7},{6,4},{7,5},{8,10},{9,11},{10,... | collective-permute-start | bytes 196616 | tf_op jit(solution)/shard_map/ppermute | solution.py:25
  54.6 5.7 %collective-permute-start.21 = (bf16[2,4,16,256]{3,2,1,0:T(8,128)(2,1)S(1)}, bf16[2,4,16,256]{3,2,1,0:T(8,128)(2,1)S(1)}, u32[]{:S(2)}, u32[]{:S(2)}) collective-permute-start(bf16[2,4,16,256]{3,2,1,0:T(8,128)(2,1)S(1)} %pad_maximum_fusion.3), channel_id=1, source_target_pairs={{0,4},{1,5},{2,6},{3,7},{4,0},{5,1},{6,2},{7,3},{8,12},{9,13},{10,... | collective-permute-start | bytes 196616 | tf_op jit(solution)/shard_map/ppermute | solution.py:25
  58.5 4.6 %collective-permute-start.24 = (bf16[8,16,256]{2,1,0:T(8,128)(2,1)S(1)}, bf16[8,16,256]{2,1,0:T(8,128)(2,1)S(1)}, u32[]{:S(2)}, u32[]{:S(2)}) collective-permute-start(bf16[8,16,256]{2,1,0:T(8,128)(2,1)S(1)} %add_convert_fusion.refs_0_), channel_id=1, source_target_pairs={{0,16},{8,24},{16,0},{24,8},{1,17},{9,25},{17,1},{25,9},{2,18},{10... | collective-permute-start | bytes 196616 | tf_op jit(solution)/shard_map/ppermute | solution.py:52
  60.0 4.0 %collective-permute-start.25 = (bf16[8,16,256]{2,1,0:T(8,128)(2,1)S(1)}, bf16[8,16,256]{2,1,0:T(8,128)(2,1)S(1)}, u32[]{:S(2)}, u32[]{:S(2)}) collective-permute-start(bf16[8,16,256]{2,1,0:T(8,128)(2,1)S(1)} %add_convert_fusion.refs_0_), channel_id=1, source_target_pairs={{0,24},{8,16},{16,8},{24,0},{1,25},{9,17},{17,9},{25,1},{2,26},{10... | collective-permute-start | bytes 196616 | tf_op jit(solution)/shard_map/ppermute | solution.py:52
  60.4 10.0 %collective-permute-start.22 = (bf16[4,4,16,256]{3,2,1,0:T(8,128)(2,1)S(1)}, bf16[4,4,16,256]{3,2,1,0:T(8,128)(2,1)S(1)}, u32[]{:S(2)}, u32[]{:S(2)}) collective-permute-start(bf16[4,4,16,256]{3,2,1,0:T(8,128)(2,1)S(1)} %pad_maximum_fusion.2), channel_id=1, source_target_pairs={{0,2},{1,3},{2,0},{3,1},{4,6},{5,7},{6,4},{7,5},{8,10},{9,11},{10,... | collective-permute-start | bytes 393224 | tf_op jit(solution)/shard_map/ppermute | solution.py:25
  65.6 14.0 %all-to-all-start = ((bf16[8,4,16,256]{3,2,1,0:T(8,128)(2,1)}), bf16[8,4,16,256]{3,2,1,0:T(8,128)(2,1)S(1)}, u32[]{:S(2)}, u32[]{:S(2)}) async-start(bf16[8,4,16,256]{3,2,1,0:T(8,128)(2,1)} %bitcast.10), calls=%async_computation | async-start | bytes 524288 | tf_op jit(solution)/shard_map/all_to_all | solution.py:366
  (11 other events, 104.1 us)

commit v6 on v5

--- a/solution.py
+++ b/solution.py
@@ -180,34 +180,29 @@
     return out[:4], out[4:6], out[6]
 
 
-def place_body(targets_ref, spot_ref, *refs):
+def place_body(targets_ref, *refs):
     pieces, slots_ref, total_ref = refs[:4], refs[4], refs[5]
     total_ref[...] = jnp.zeros_like(total_ref)
     blocks = slots_ref.shape[0]
-    slabs = pieces[0].shape[0]
-    group = spot_ref[1]
-    first = group * blocks
     for k, piece in enumerate(pieces):
-        for j in range(slabs):
-            place = targets_ref[group ^ k, j] - first
-
-            place = jnp.where((place >= 0) & (place < blocks), place, blocks)
-            total_ref[place] += piece[j].astype(F32)
-
+        for j in range(piece.shape[0]):
+            total_ref[targets_ref[k, j]] += piece[j].astype(F32)
     slots_ref[...] = total_ref[:blocks].astype(BF16)
 
 
-def place(targets, spot, pieces, blocks):
+def place(targets, group, pieces, blocks):
     shape = (blocks,) + pieces[0].shape[1:]
+    fronts = group ^ jnp.arange(len(pieces), dtype=jnp.int32)
+    at = jnp.take(targets, fronts, axis=0) - group * blocks
+    at = jnp.where((at >= 0) & (at < blocks), at, blocks)
     return pl.pallas_call(
         place_body,
         out_shape=jax.ShapeDtypeStruct(shape, BF16),
-        in_specs=[pl.BlockSpec(memory_space=pltpu.SMEM)] * 2
-        + [pl.BlockSpec(memory_space=pltpu.VMEM)] * 4,
-        out_specs=pl.BlockSpec(memory_space=pltpu.VMEM),
+        in_specs=[SMEM] + [VMEM] * 4,
+        out_specs=VMEM,
         scratch_shapes=[pltpu.VMEM((blocks + 1,) + shape[1:], F32)],
         compiler_params=params(),
-    )(targets, spot, *pieces)
+    )(at, *pieces)
 
 
 def reorder_body(spot_ref, order_ref, inverse_ref, *out_refs):
@@ -361,7 +356,7 @@
     base = panel_update(spot, surface, panel_lower, factor_mine, factor_other)
     local_blocks = surface.shape[0] // BLOCK
     blocks = local_blocks * row_count
-    slots = place(border_blocks, spot, pieces, blocks)
+    slots = place(border_blocks, group, pieces, blocks)
     slots = slots.reshape((row_count, local_blocks) + slots.shape[1:])
     got = lax.all_to_all(slots, "row", 0, 0, tiled=True)
     collected = got.transpose(1, 0, 2, 3).reshape(surface.shape).astype(F32)

time: 80.9 us -> 80.9 us (level)
  transfers between devices with their start and end apart: 27 -> 27, of which waited for: 16 -> 15; matrix products, arithmetic and copies ran while one was open for 0% -> 1% of each run, Pallas kernels for 18% -> 18%
where the time goes in v6:
time: 80.9 us; the launch traced here: 80.6 us
  starting transfers between devices  35.4 us (44%)
  waiting for transfers between devices  23.4 us (29%)
  Pallas kernels  16.9 us (21%)
  local copies, waits for them, and re-layouts  3.35 us (4%)
  other arithmetic  1.24 us (2%)
    ppermute x14, starting transfers between devices, ring_send(): return lax.ppermute(value, 'row', pairs)  16 us
    ppermute x7, starting transfers between devices, row_permute(): return lax.ppermute(value, 'row', [(s, t[0] * 2 + t[1]) for s, t in pairs])  12.4 us
    pallas_call x3, Pallas kernels, multiply(): pl.pallas_call(functools.partial(multiply_body, parts_in, depth, bool(ext...  10.8 us
    ppermute x14, waiting for transfers between devices, ring_send(): return lax.ppermute(value, 'row', pairs)  9.29 us
    all_to_all x1, waiting for transfers between devices, staged(): got = lax.all_to_all(slots, 'row', 0, 0, tiled=True)  6.57 us
    ppermute x7, waiting for transfers between devices, row_permute(): return lax.ppermute(value, 'row', [(s, t[0] * 2 + t[1]) for s, t in pairs])  5.28 us
    all_to_all x1, starting transfers between devices, staged(): got = lax.all_to_all(slots, 'row', 0, 0, tiled=True)  4.87 us
    ppermute x5, waiting for transfers between devices, group_swap(): return lax.ppermute(value, 'grp', [(g, g ^ step) for g in range(4)])  2.29 us
  transfers between devices with their start and end apart: 27, of which 15 were waited for; matrix products, arithmetic and copies ran while one was open for 1% of the time, Pallas kernels for 18%

profile of v6, /device:TPU:0, one launch (start us, length us, event | category | flops | bytes accessed | tf_op | source)
XLA Modules:
  0.0 80.6 jit_solution(3844339583140621713)
XLA Ops:
  1.1 3.1 %collective-permute-start = (bf16[448,256]{1,0:T(8,128)(2,1)S(1)}, bf16[448,256]{1,0:T(8,128)(2,1)S(1)}, u32[]{:S(2)}, u32[]{:S(2)}) collective-permute-start(bf16[448,256]{1,0:T(8,128)(2,1)S(1)} %pad_maximum_fusion.1.refs_0_.refs_2_), channel_id=1, source_target_pairs={{0,2},{1,0},{2,4},{3,1},{4,6},{5,3},{6,7},{7,5},{8,10},{9,8},{10,1... | collective-permute-start | bytes 688136 | tf_op jit(solution)/shard_map/ppermute | solution.py:40
  4.2 2.0 %collective-permute-start.4 = (bf16[384,256]{1,0:T(8,128)(2,1)S(1)}, bf16[384,256]{1,0:T(8,128)(2,1)S(1)}, u32[]{:S(2)}, u32[]{:S(2)}) collective-permute-start(bf16[384,256]{1,0:T(8,128)(2,1)S(1)} %get-tuple-element.69.refs_1_), channel_id=1, source_target_pairs={{0,2},{1,0},{2,4},{3,1},{4,6},{5,3},{6,7},{7,5},{8,10},{9,8},{10,1... | collective-permute-start | bytes 589832 | tf_op jit(solution)/shard_map/ppermute | solution.py:40
  8.0 1.3 %shard_map.100 = (bf16[64,512]{1,0:T(8,128)(2,1)S(1)}, bf16[64,512]{1,0:T(8,128)(2,1)S(1)}) custom-call(s32[2]{0:T(128)S(1)} %pad_add_fusion.spot_ref.place_ref, s32[1,1024]{1,0:T(1,128)S(1)} %bitcast.24, bf16[128,1024]{1,0:T(8,128)(2,1)S(1)} %copy-done.4), custom_call_target="tpu_custom_call" | custom-call | tf_op jit(solution)/shard_map/pallas_call | solution.py:230
  10.6 2.2 %collective-permute-done.1.refs_4_ = bf16[448,256]{1,0:T(8,128)(2,1)S(1)} collective-permute-done((bf16[448,256]{1,0:T(8,128)(2,1)S(1)}, bf16[448,256]{1,0:T(8,128)(2,1)S(1)}, u32[]{:S(2)}, u32[]{:S(2)}) %collective-permute-start.1) | collective-permute-done | bytes 229408 | tf_op jit(solution)/shard_map/ppermute | solution.py:40
  12.8 1.6 %collective-permute-start.2 = (bf16[448,256]{1,0:T(8,128)(2,1)S(1)}, bf16[448,256]{1,0:T(8,128)(2,1)S(1)}, u32[]{:S(2)}, u32[]{:S(2)}) collective-permute-start(bf16[448,256]{1,0:T(8,128)(2,1)S(1)} %collective-permute-done.refs_2_.refs_3_), channel_id=1, source_target_pairs={{0,2},{1,0},{2,4},{3,1},{4,6},{5,3},{6,7},{7,5},{8,10},{9,8},{10,1... | collective-permute-start | bytes 688136 | tf_op jit(solution)/shard_map/ppermute | solution.py:40
  14.8 2.2 %collective-permute-done.5.refs_5_ = bf16[384,256]{1,0:T(8,128)(2,1)S(1)} collective-permute-done((bf16[384,256]{1,0:T(8,128)(2,1)S(1)}, bf16[384,256]{1,0:T(8,128)(2,1)S(1)}, u32[]{:S(2)}, u32[]{:S(2)}) %collective-permute-start.5) | collective-permute-done | bytes 196640 | tf_op jit(solution)/shard_map/ppermute | solution.py:40
  17.0 1.6 %collective-permute-start.8 = (bf16[384,256]{1,0:T(8,128)(2,1)S(1)}, bf16[384,256]{1,0:T(8,128)(2,1)S(1)}, u32[]{:S(2)}, u32[]{:S(2)}) collective-permute-start(bf16[384,256]{1,0:T(8,128)(2,1)S(1)} %collective-permute-done.4.refs_3_), channel_id=1, source_target_pairs={{0,2},{1,0},{2,4},{3,1},{4,6},{5,3},{6,7},{7,5},{8,10},{9,8},{10,1... | collective-permute-start | bytes 589832 | tf_op jit(solution)/shard_map/ppermute | solution.py:40
  19.0 4.0 %shard_map.101.refs_4_ = f32[768,256]{1,0:T(8,128)S(1)} custom-call(s32[2]{0:T(128)S(1)} %pad_add_fusion.spot_ref.place_ref, s32[4]{0:T(128)S(1)} %copy-done.5, bf16[768,6144]{1,0:T(8,128)(2,1)} %bitcast.25, bf16[448,256]{1,0:T(8,128)(2,1)S(1)} %pad_maximum_fusion.1.refs_0_.refs_2_, bf16[384,256]{1,0:T(8,128)(2,1)S(1)} %get-tuple-element.69.refs_1_, ...), custom_call_target="tpu_custom_call" | custom-call | flops 905969664 | bytes 3538944 | tf_op jit(solution)/shard_map/pallas_call | solution.py:113
  23.1 1.6 %collective-permute-start.6 = (bf16[448,256]{1,0:T(8,128)(2,1)S(1)}, bf16[448,256]{1,0:T(8,128)(2,1)S(1)}, u32[]{:S(2)}, u32[]{:S(2)}) collective-permute-start(bf16[448,256]{1,0:T(8,128)(2,1)S(1)} %collective-permute-done.2.refs_0_.refs_5_), channel_id=1, source_target_pairs={{0,2},{1,0},{2,4},{3,1},{4,6},{5,3},{6,7},{7,5},{8,10},{9,8},{10,1... | collective-permute-start | bytes 688136 | tf_op jit(solution)/shard_map/ppermute | solution.py:40
  25.6 1.6 %collective-permute-start.10 = (bf16[384,256]{1,0:T(8,128)(2,1)S(1)}, bf16[384,256]{1,0:T(8,128)(2,1)S(1)}, u32[]{:S(2)}, u32[]{:S(2)}) collective-permute-start(bf16[384,256]{1,0:T(8,128)(2,1)S(1)} %collective-permute-done.8.refs_1_), channel_id=1, source_target_pairs={{0,2},{1,0},{2,4},{3,1},{4,6},{5,3},{6,7},{7,5},{8,10},{9,8},{10,1... | collective-permute-start | bytes 589832 | tf_op jit(solution)/shard_map/ppermute | solution.py:40
  27.6 3.4 %shard_map.102.refs_4_ = f32[768,256]{1,0:T(8,128)S(1)} custom-call(s32[2]{0:T(128)S(1)} %pad_add_fusion.spot_ref.place_ref, s32[4]{0:T(128)S(1)} %copy-done.5, bf16[768,6144]{1,0:T(8,128)(2,1)} %bitcast.26, bf16[448,256]{1,0:T(8,128)(2,1)S(1)} %collective-permute-done.2.refs_0_.refs_5_, bf16[384,256]{1,0:T(8,128)(2,1)S(1)} %collective-permute-done.8.refs_1_, ...), custom_call_target="tpu_custom_call" | custom-call | flops 603979776 | bytes 2359296 | tf_op jit(solution)/shard_map/pallas_call | solution.py:113
  31.7 1.6 %collective-permute-start.12 = (bf16[448,256]{1,0:T(8,128)(2,1)S(1)}, bf16[448,256]{1,0:T(8,128)(2,1)S(1)}, u32[]{:S(2)}, u32[]{:S(2)}) collective-permute-start(bf16[448,256]{1,0:T(8,128)(2,1)S(1)} %collective-permute-done.6.refs_0_.refs_7_), channel_id=1, source_target_pairs={{0,2},{1,0},{2,4},{3,1},{4,6},{5,3},{6,7},{7,5},{8,10},{9,8},{10,1... | collective-permute-start | bytes 688136 | tf_op jit(solution)/shard_map/ppermute | solution.py:40
  35.9 3.4 %shard_map.103 = (f32[768,256]{1,0:T(8,128)S(1)}, bf16[768,768]{1,0:T(8,128)(2,1)S(1)}) custom-call(s32[2]{0:T(128)S(1)} %pad_add_fusion.spot_ref.place_ref, s32[4]{0:T(128)S(1)} %copy-done.5, bf16[768,6144]{1,0:T(8,128)(2,1)} %bitcast.27, bf16[448,256]{1,0:T(8,128)(2,1)S(1)} %collective-permute-done.6.refs_0_.refs_7_, ...), custom_call_target="tpu_custom_call" | custom-call | flops 603979776 | bytes 2359296 | tf_op jit(solution)/shard_map/pallas_call | solution.py:113
  40.3 2.1 %shard_map.104 = (f32[8,16,256]{2,1,0:T(8,128)S(1)}, f32[8,16,256]{2,1,0:T(8,128)S(1)}, f32[8,16,256]{2,1,0:T(8,128)S(1)}, f32[8,16,256]{2,1,0:T(8,128)S(1)}, bf...) custom-call(s32[2]{0:T(128)S(1)} %pad_add_fusion.spot_ref.place_ref, ...), custom_call_target="tpu_custom_call" | custom-call | flops 704643072 | bytes 2752512 | tf_op jit(solution)/shard_map/pallas_call | solution.py:162
  45.5 3.4 %collective-permute-done.14 = bf16[16,16,256]{2,1,0:T(8,128)(2,1)S(1)} collective-permute-done((bf16[16,16,256]{2,1,0:T(8,128)(2,1)S(1)}, bf16[16,16,256]{2,1,0:T(8,128)(2,1)S(1)}, u32[]{:S(2)}, u32[]{:S(2)}) %collective-permute-start.14) | collective-permute-done | bytes 131104 | tf_op jit(solution)/shard_map/ppermute | solution.py:25
  48.9 2.4 %collective-permute-start.16 = (bf16[8,16,256]{2,1,0:T(8,128)(2,1)S(1)}, bf16[8,16,256]{2,1,0:T(8,128)(2,1)S(1)}, u32[]{:S(2)}, u32[]{:S(2)}) collective-permute-start(bf16[8,16,256]{2,1,0:T(8,128)(2,1)S(1)} %get-tuple-element.71), channel_id=1, source_target_pairs={{0,4},{1,5},{2,6},{3,7},{4,0},{5,1},{6,2},{7,3},{8,12},{9,13},{10,... | collective-permute-start | bytes 196616 | tf_op jit(solution)/shard_map/ppermute | solution.py:25
  51.3 1.9 %collective-permute-start.19 = (bf16[8,16,256]{2,1,0:T(8,128)(2,1)S(1)}, bf16[8,16,256]{2,1,0:T(8,128)(2,1)S(1)}, u32[]{:S(2)}, u32[]{:S(2)}) collective-permute-start(bf16[8,16,256]{2,1,0:T(8,128)(2,1)S(1)} %get-tuple-element.72), channel_id=1, source_target_pairs={{0,6},{1,7},{2,4},{3,5},{4,2},{5,3},{6,0},{7,1},{8,14},{9,15},{10,... | collective-permute-start | bytes 196616 | tf_op jit(solution)/shard_map/ppermute | solution.py:25
  54.6 2.5 %collective-permute-start.21 = (bf16[2,4,16,256]{3,2,1,0:T(8,128)(2,1)S(1)}, bf16[2,4,16,256]{3,2,1,0:T(8,128)(2,1)S(1)}, u32[]{:S(2)}, u32[]{:S(2)}) collective-permute-start(bf16[2,4,16,256]{3,2,1,0:T(8,128)(2,1)S(1)} %pad_maximum_fusion.3), channel_id=1, source_target_pairs={{0,4},{1,5},{2,6},{3,7},{4,0},{5,1},{6,2},{7,3},{8,12},{9,13},{10,... | collective-permute-start | bytes 196616 | tf_op jit(solution)/shard_map/ppermute | solution.py:25
  58.4 1.5 %collective-permute-start.24 = (bf16[8,16,256]{2,1,0:T(8,128)(2,1)S(1)}, bf16[8,16,256]{2,1,0:T(8,128)(2,1)S(1)}, u32[]{:S(2)}, u32[]{:S(2)}) collective-permute-start(bf16[8,16,256]{2,1,0:T(8,128)(2,1)S(1)} %add_convert_fusion.refs_0_), channel_id=1, source_target_pairs={{0,16},{8,24},{16,0},{24,8},{1,17},{9,25},{17,1},{25,9},{2,18},{10... | collective-permute-start | bytes 196616 | tf_op jit(solution)/shard_map/ppermute | solution.py:52
  60.3 2.9 %collective-permute-start.22 = (bf16[4,4,16,256]{3,2,1,0:T(8,128)(2,1)S(1)}, bf16[4,4,16,256]{3,2,1,0:T(8,128)(2,1)S(1)}, u32[]{:S(2)}, u32[]{:S(2)}) collective-permute-start(bf16[4,4,16,256]{3,2,1,0:T(8,128)(2,1)S(1)} %pad_maximum_fusion.2), channel_id=1, source_target_pairs={{0,2},{1,3},{2,0},{3,1},{4,6},{5,7},{6,4},{7,5},{8,10},{9,11},{10,... | collective-permute-start | bytes 393224 | tf_op jit(solution)/shard_map/ppermute | solution.py:25
  64.0 1.5 %shard_map.107 = bf16[32,16,256]{2,1,0:T(8,128)(2,1)} custom-call(s32[4,8]{1,0:T(4,128)S(1)} %and_select_fusion.targets_ref, bf16[8,16,256]{2,1,0:T(8,128)(2,1)S(1)} %add_convert_fusion.refs_0_, bf16[8,16,256]{2,1,0:T(8,128)(2,1)S(1)} %collective-permute-done.20.refs_1_, bf16[8,16,256]{2,1,0:T(8,128)(2,1)S(1)} %collective-permute-done.24.refs_2_, ...), custom_call_target="tpu_custom_call" | custom-call | tf_op jit(solution)/shard_map/pallas_call | solution.py:198
  65.5 4.9 %all-to-all-start = ((bf16[8,4,16,256]{3,2,1,0:T(8,128)(2,1)}), bf16[8,4,16,256]{3,2,1,0:T(8,128)(2,1)S(1)}, u32[]{:S(2)}, u32[]{:S(2)}) async-start(bf16[8,4,16,256]{3,2,1,0:T(8,128)(2,1)} %bitcast.11), calls=%async_computation | async-start | bytes 524288 | tf_op jit(solution)/shard_map/all_to_all | solution.py:361
  70.5 1.5 %collective-permute-done.23.other_ref = bf16[8,64,256]{2,1,0:T(8,128)(2,1)S(1)} collective-permute-done((bf16[8,64,256]{2,1,0:T(8,128)(2,1)S(1)}, bf16[8,64,256]{2,1,0:T(8,128)(2,1)S(1)}, u32[]{:S(2)}, u32[]{:S(2)}) %collective-permute-start.23) | collective-permute-done | bytes 262176 | tf_op jit(solution)/shard_map/ppermute | solution.py:52
  73.1 6.6 %all-to-all-done = bf16[8,4,16,256]{3,2,1,0:T(8,128)(2,1)S(1)} async-done(((bf16[8,4,16,256]{3,2,1,0:T(8,128)(2,1)}), bf16[8,4,16,256]{3,2,1,0:T(8,128)(2,1)S(1)}, u32[]{:S(2)}, u32[]{:S(2)}) %all-to-all-start) | async-done | bytes 262176 | tf_op jit(solution)/shard_map/all_to_all | solution.py:361
  (74 shorter events, 19.9 us)
Async XLA Ops:
  1.1 9.5 %collective-permute-start = (bf16[448,256]{1,0:T(8,128)(2,1)S(1)}, bf16[448,256]{1,0:T(8,128)(2,1)S(1)}, u32[]{:S(2)}, u32[]{:S(2)}) collective-permute-start(bf16[448,256]{1,0:T(8,128)(2,1)S(1)} %pad_maximum_fusion.1.refs_0_.refs_2_), channel_id=1, source_target_pairs={{0,2},{1,0},{2,4},{3,1},{4,6},{5,3},{6,7},{7,5},{8,10},{9,8},{10,1... | collective-permute-start | bytes 688136 | tf_op jit(solution)/shard_map/ppermute | solution.py:40
  4.2 8.5 %collective-permute-start.1 = (bf16[448,256]{1,0:T(8,128)(2,1)S(1)}, bf16[448,256]{1,0:T(8,128)(2,1)S(1)}, u32[]{:S(2)}, u32[]{:S(2)}) collective-permute-start(bf16[448,256]{1,0:T(8,128)(2,1)S(1)} %pad_maximum_fusion.1.refs_0_.refs_2_), channel_id=1, source_target_pairs={{0,1},{1,3},{2,0},{3,5},{4,2},{5,7},{6,4},{7,6},{8,9},{9,11},{10,8... | collective-permute-start | bytes 688136 | tf_op jit(solution)/shard_map/ppermute | solution.py:40
  4.2 10.6 %collective-permute-start.4 = (bf16[384,256]{1,0:T(8,128)(2,1)S(1)}, bf16[384,256]{1,0:T(8,128)(2,1)S(1)}, u32[]{:S(2)}, u32[]{:S(2)}) collective-permute-start(bf16[384,256]{1,0:T(8,128)(2,1)S(1)} %get-tuple-element.69.refs_1_), channel_id=1, source_target_pairs={{0,2},{1,0},{2,4},{3,1},{4,6},{5,3},{6,7},{7,5},{8,10},{9,8},{10,1... | collective-permute-start | bytes 589832 | tf_op jit(solution)/shard_map/ppermute | solution.py:40
  6.2 10.7 %collective-permute-start.5 = (bf16[384,256]{1,0:T(8,128)(2,1)S(1)}, bf16[384,256]{1,0:T(8,128)(2,1)S(1)}, u32[]{:S(2)}, u32[]{:S(2)}) collective-permute-start(bf16[384,256]{1,0:T(8,128)(2,1)S(1)} %get-tuple-element.69.refs_1_), channel_id=1, source_target_pairs={{0,1},{1,3},{2,0},{3,5},{4,2},{5,7},{6,4},{7,6},{8,9},{9,11},{10,8... | collective-permute-start | bytes 589832 | tf_op jit(solution)/shard_map/ppermute | solution.py:40
  12.8 10.3 %collective-permute-start.2 = (bf16[448,256]{1,0:T(8,128)(2,1)S(1)}, bf16[448,256]{1,0:T(8,128)(2,1)S(1)}, u32[]{:S(2)}, u32[]{:S(2)}) collective-permute-start(bf16[448,256]{1,0:T(8,128)(2,1)S(1)} %collective-permute-done.refs_2_.refs_3_), channel_id=1, source_target_pairs={{0,2},{1,0},{2,4},{3,1},{4,6},{5,3},{6,7},{7,5},{8,10},{9,8},{10,1... | collective-permute-start | bytes 688136 | tf_op jit(solution)/shard_map/ppermute | solution.py:40
  14.3 8.7 %collective-permute-start.3 = (bf16[448,256]{1,0:T(8,128)(2,1)S(1)}, bf16[448,256]{1,0:T(8,128)(2,1)S(1)}, u32[]{:S(2)}, u32[]{:S(2)}) collective-permute-start(bf16[448,256]{1,0:T(8,128)(2,1)S(1)} %collective-permute-done.1.refs_4_), channel_id=1, source_target_pairs={{0,1},{1,3},{2,0},{3,5},{4,2},{5,7},{6,4},{7,6},{8,9},{9,11},{10,8... | collective-permute-start | bytes 688136 | tf_op jit(solution)/shard_map/ppermute | solution.py:40
  17.0 8.2 %collective-permute-start.8 = (bf16[384,256]{1,0:T(8,128)(2,1)S(1)}, bf16[384,256]{1,0:T(8,128)(2,1)S(1)}, u32[]{:S(2)}, u32[]{:S(2)}) collective-permute-start(bf16[384,256]{1,0:T(8,128)(2,1)S(1)} %collective-permute-done.4.refs_3_), channel_id=1, source_target_pairs={{0,2},{1,0},{2,4},{3,1},{4,6},{5,3},{6,7},{7,5},{8,10},{9,8},{10,1... | collective-permute-start | bytes 589832 | tf_op jit(solution)/shard_map/ppermute | solution.py:40
  18.5 7.0 %collective-permute-start.9 = (bf16[384,256]{1,0:T(8,128)(2,1)S(1)}, bf16[384,256]{1,0:T(8,128)(2,1)S(1)}, u32[]{:S(2)}, u32[]{:S(2)}) collective-permute-start(bf16[384,256]{1,0:T(8,128)(2,1)S(1)} %collective-permute-done.5.refs_5_), channel_id=1, source_target_pairs={{0,1},{1,3},{2,0},{3,5},{4,2},{5,7},{6,4},{7,6},{8,9},{9,11},{10,8... | collective-permute-start | bytes 589832 | tf_op jit(solution)/shard_map/ppermute | solution.py:40
  23.1 7.9 %collective-permute-start.6 = (bf16[448,256]{1,0:T(8,128)(2,1)S(1)}, bf16[448,256]{1,0:T(8,128)(2,1)S(1)}, u32[]{:S(2)}, u32[]{:S(2)}) collective-permute-start(bf16[448,256]{1,0:T(8,128)(2,1)S(1)} %collective-permute-done.2.refs_0_.refs_5_), channel_id=1, source_target_pairs={{0,2},{1,0},{2,4},{3,1},{4,6},{5,3},{6,7},{7,5},{8,10},{9,8},{10,1... | collective-permute-start | bytes 688136 | tf_op jit(solution)/shard_map/ppermute | solution.py:40
  24.7 7.0 %collective-permute-start.7 = (bf16[448,256]{1,0:T(8,128)(2,1)S(1)}, bf16[448,256]{1,0:T(8,128)(2,1)S(1)}, u32[]{:S(2)}, u32[]{:S(2)}) collective-permute-start(bf16[448,256]{1,0:T(8,128)(2,1)S(1)} %collective-permute-done.3.refs_2_.refs_6_), channel_id=1, source_target_pairs={{0,1},{1,3},{2,0},{3,5},{4,2},{5,7},{6,4},{7,6},{8,9},{9,11},{10,8... | collective-permute-start | bytes 688136 | tf_op jit(solution)/shard_map/ppermute | solution.py:40
  25.6 9.0 %collective-permute-start.10 = (bf16[384,256]{1,0:T(8,128)(2,1)S(1)}, bf16[384,256]{1,0:T(8,128)(2,1)S(1)}, u32[]{:S(2)}, u32[]{:S(2)}) collective-permute-start(bf16[384,256]{1,0:T(8,128)(2,1)S(1)} %collective-permute-done.8.refs_1_), channel_id=1, source_target_pairs={{0,2},{1,0},{2,4},{3,1},{4,6},{5,3},{6,7},{7,5},{8,10},{9,8},{10,1... | collective-permute-start | bytes 589832 | tf_op jit(solution)/shard_map/ppermute | solution.py:40
  27.1 7.5 %collective-permute-start.11 = (bf16[384,256]{1,0:T(8,128)(2,1)S(1)}, bf16[384,256]{1,0:T(8,128)(2,1)S(1)}, u32[]{:S(2)}, u32[]{:S(2)}) collective-permute-start(bf16[384,256]{1,0:T(8,128)(2,1)S(1)} %collective-permute-done.9.refs_3_), channel_id=1, source_target_pairs={{0,1},{1,3},{2,0},{3,5},{4,2},{5,7},{6,4},{7,6},{8,9},{9,11},{10,8... | collective-permute-start | bytes 589832 | tf_op jit(solution)/shard_map/ppermute | solution.py:40
  31.7 8.7 %collective-permute-start.12 = (bf16[448,256]{1,0:T(8,128)(2,1)S(1)}, bf16[448,256]{1,0:T(8,128)(2,1)S(1)}, u32[]{:S(2)}, u32[]{:S(2)}) collective-permute-start(bf16[448,256]{1,0:T(8,128)(2,1)S(1)} %collective-permute-done.6.refs_0_.refs_7_), channel_id=1, source_target_pairs={{0,2},{1,0},{2,4},{3,1},{4,6},{5,3},{6,7},{7,5},{8,10},{9,8},{10,1... | collective-permute-start | bytes 688136 | tf_op jit(solution)/shard_map/ppermute | solution.py:40
  34.7 5.7 %collective-permute-start.13 = (bf16[384,256]{1,0:T(8,128)(2,1)S(1)}, bf16[384,256]{1,0:T(8,128)(2,1)S(1)}, u32[]{:S(2)}, u32[]{:S(2)}) collective-permute-start(bf16[384,256]{1,0:T(8,128)(2,1)S(1)} %collective-permute-done.11.refs_3_), channel_id=1, source_target_pairs={{0,1},{1,3},{2,0},{3,5},{4,2},{5,7},{6,4},{7,6},{8,9},{9,11},{10,8... | collective-permute-start | bytes 589832 | tf_op jit(solution)/shard_map/ppermute | solution.py:40
  42.5 6.4 %collective-permute-start.14 = (bf16[16,16,256]{2,1,0:T(8,128)(2,1)S(1)}, bf16[16,16,256]{2,1,0:T(8,128)(2,1)S(1)}, u32[]{:S(2)}, u32[]{:S(2)}) collective-permute-start(bf16[16,16,256]{2,1,0:T(8,128)(2,1)S(1)} %get-tuple-element.55), channel_id=1, source_target_pairs={{0,1},{1,0},{2,3},{3,2},{4,5},{5,4},{6,7},{7,6},{8,9},{9,8},{10,11... | collective-permute-start | bytes 393224 | tf_op jit(solution)/shard_map/ppermute | solution.py:25
  44.6 8.6 %collective-permute-start.17 = (bf16[20,16,256]{2,1,0:T(8,128)(2,1)S(1)}, bf16[20,16,256]{2,1,0:T(8,128)(2,1)S(1)}, u32[]{:S(2)}, u32[]{:S(2)}) collective-permute-start(bf16[20,16,256]{2,1,0:T(8,128)(2,1)S(1)} %shard_map.105), channel_id=1, source_target_pairs={{0,1},{1,0},{2,3},{3,2},{4,5},{5,4},{6,7},{7,6},{8,9},{9,8},{10,11... | collective-permute-start | bytes 491528 | tf_op jit(solution)/shard_map/ppermute | solution.py:25
  48.9 5.7 %collective-permute-start.16 = (bf16[8,16,256]{2,1,0:T(8,128)(2,1)S(1)}, bf16[8,16,256]{2,1,0:T(8,128)(2,1)S(1)}, u32[]{:S(2)}, u32[]{:S(2)}) collective-permute-start(bf16[8,16,256]{2,1,0:T(8,128)(2,1)S(1)} %get-tuple-element.71), channel_id=1, source_target_pairs={{0,4},{1,5},{2,6},{3,7},{4,0},{5,1},{6,2},{7,3},{8,12},{9,13},{10,... | collective-permute-start | bytes 196616 | tf_op jit(solution)/shard_map/ppermute | solution.py:25
  51.3 6.7 %collective-permute-start.19 = (bf16[8,16,256]{2,1,0:T(8,128)(2,1)S(1)}, bf16[8,16,256]{2,1,0:T(8,128)(2,1)S(1)}, u32[]{:S(2)}, u32[]{:S(2)}) collective-permute-start(bf16[8,16,256]{2,1,0:T(8,128)(2,1)S(1)} %get-tuple-element.72), channel_id=1, source_target_pairs={{0,6},{1,7},{2,4},{3,5},{4,2},{5,3},{6,0},{7,1},{8,14},{9,15},{10,... | collective-permute-start | bytes 196616 | tf_op jit(solution)/shard_map/ppermute | solution.py:25
  53.2 5.1 %collective-permute-start.18 = (bf16[8,16,256]{2,1,0:T(8,128)(2,1)S(1)}, bf16[8,16,256]{2,1,0:T(8,128)(2,1)S(1)}, u32[]{:S(2)}, u32[]{:S(2)}) collective-permute-start(bf16[8,16,256]{2,1,0:T(8,128)(2,1)S(1)} %add_convert_fusion.2), channel_id=1, source_target_pairs={{0,2},{1,3},{2,0},{3,1},{4,6},{5,7},{6,4},{7,5},{8,10},{9,11},{10,... | collective-permute-start | bytes 196616 | tf_op jit(solution)/shard_map/ppermute | solution.py:25
  54.6 5.6 %collective-permute-start.21 = (bf16[2,4,16,256]{3,2,1,0:T(8,128)(2,1)S(1)}, bf16[2,4,16,256]{3,2,1,0:T(8,128)(2,1)S(1)}, u32[]{:S(2)}, u32[]{:S(2)}) collective-permute-start(bf16[2,4,16,256]{3,2,1,0:T(8,128)(2,1)S(1)} %pad_maximum_fusion.3), channel_id=1, source_target_pairs={{0,4},{1,5},{2,6},{3,7},{4,0},{5,1},{6,2},{7,3},{8,12},{9,13},{10,... | collective-permute-start | bytes 196616 | tf_op jit(solution)/shard_map/ppermute | solution.py:25
  58.4 4.8 %collective-permute-start.24 = (bf16[8,16,256]{2,1,0:T(8,128)(2,1)S(1)}, bf16[8,16,256]{2,1,0:T(8,128)(2,1)S(1)}, u32[]{:S(2)}, u32[]{:S(2)}) collective-permute-start(bf16[8,16,256]{2,1,0:T(8,128)(2,1)S(1)} %add_convert_fusion.refs_0_), channel_id=1, source_target_pairs={{0,16},{8,24},{16,0},{24,8},{1,17},{9,25},{17,1},{25,9},{2,18},{10... | collective-permute-start | bytes 196616 | tf_op jit(solution)/shard_map/ppermute | solution.py:52
  59.9 4.1 %collective-permute-start.25 = (bf16[8,16,256]{2,1,0:T(8,128)(2,1)S(1)}, bf16[8,16,256]{2,1,0:T(8,128)(2,1)S(1)}, u32[]{:S(2)}, u32[]{:S(2)}) collective-permute-start(bf16[8,16,256]{2,1,0:T(8,128)(2,1)S(1)} %add_convert_fusion.refs_0_), channel_id=1, source_target_pairs={{0,24},{8,16},{16,8},{24,0},{1,25},{9,17},{17,9},{25,1},{2,26},{10... | collective-permute-start | bytes 196616 | tf_op jit(solution)/shard_map/ppermute | solution.py:52
  60.3 10.1 %collective-permute-start.22 = (bf16[4,4,16,256]{3,2,1,0:T(8,128)(2,1)S(1)}, bf16[4,4,16,256]{3,2,1,0:T(8,128)(2,1)S(1)}, u32[]{:S(2)}, u32[]{:S(2)}) collective-permute-start(bf16[4,4,16,256]{3,2,1,0:T(8,128)(2,1)S(1)} %pad_maximum_fusion.2), channel_id=1, source_target_pairs={{0,2},{1,3},{2,0},{3,1},{4,6},{5,7},{6,4},{7,5},{8,10},{9,11},{10,... | collective-permute-start | bytes 393224 | tf_op jit(solution)/shard_map/ppermute | solution.py:25
  65.5 14.1 %all-to-all-start = ((bf16[8,4,16,256]{3,2,1,0:T(8,128)(2,1)}), bf16[8,4,16,256]{3,2,1,0:T(8,128)(2,1)S(1)}, u32[]{:S(2)}, u32[]{:S(2)}) async-start(bf16[8,4,16,256]{3,2,1,0:T(8,128)(2,1)} %bitcast.11), calls=%async_computation | async-start | bytes 524288 | tf_op jit(solution)/shard_map/all_to_all | solution.py:361
  (11 other events, 86.3 us)
